TPU v7x, 128 devices: a whole 4x4x4 slice. The times are simulated.
128 devices in a mesh: dp: 8 (over x, core), fsdp: 4 (over y), tensor: 4 (over z).
Axes of the slice: x: 4, y: 4, z: 4, core: 2. Of those that a mesh axis runs over, the one named last changes fastest.
Arguments:
- tokens: bfloat16 [5120, 8192], P('dp', 'fsdp'), may hold values from -6 to 6
- cotangent: bfloat16 [5120, 28672], P('dp', 'tensor'), may hold values from -6 to 6
- left_factor: bfloat16 [8192, 512], P('fsdp'), may hold values from -0.0625 to 0.0625
- right_factor: bfloat16 [512, 4, 7168], P(None, 'tensor', 'fsdp'), may hold values from -0.25 to 0.25
- block_values: bfloat16 [512, 128, 128], P(('fsdp', 'tensor')), may hold values from -0.5 to 0.5
- block_rows: int32 [512], P(('fsdp', 'tensor')), may hold values from 0 to 15, as said below
- block_cols: int32 [512], P(('fsdp', 'tensor')), may hold values from 0 to 55
- block_counts: int32 [16], replicated, may hold values from 1 to 32, as said below
Outputs:
- mixed: bfloat16 [5120, 4, 7168], P('dp', 'tensor', 'fsdp')
- grad_left: bfloat16 [8192, 512], P('fsdp')
- grad_right: bfloat16 [512, 4, 7168], P(None, 'tensor', 'fsdp')
- grad_blocks: bfloat16 [512, 128, 128], P(('fsdp', 'tensor'))
Inputs may be any that keep to these rules, and one draw needn't show every extreme that they name: Within one owner's 32 slots, the pairs (block_rows, block_cols) are all different. `block_counts`: some owner has exactly 32 live slots.
All inputs are finite; a program needn't handle non-finite values.
Results may differ from a plain program's by a relative error of at most 0.005.
Values may be sent and summed in bfloat16 or wider, within the bound.
No kernel may reach another device: no remote copies, remote signals or barrier semaphores. Data moves between devices by JAX's collectives and lax.ppermute only.
A program may use at most 192 MiB of HBM per device.

v0:
```python
import jax
import jax.numpy as jnp
from jax import lax
from jax.experimental import pallas as pl
from jax.experimental.pallas import tpu as pltpu
from jax.sharding import PartitionSpec as P

F32 = jnp.float32
BF16 = jnp.bfloat16
SIDE = 128
SMEM = pl.BlockSpec(memory_space=pltpu.SMEM)
VMEM = pl.BlockSpec(memory_space=pltpu.VMEM)
HBM = pl.BlockSpec(memory_space=pl.ANY)
ROWS = (((0,), (0,)), ((), ()))
COLS = (((1,), (1,)), ((), ()))


def lanes(block):
    return pl.ds(pl.multiple_of(block * SIDE, SIDE), SIDE)


def span(block, size):
    return pl.ds(pl.multiple_of(block * size, size), size)


def shape(dims, dtype):
    return jax.ShapeDtypeStruct(dims, dtype)


def call(kernel, outs, smem=(), hbm=(), vmem=(), scratch=(), after=(), mib=8):
    n_in, n_out = len(smem) + len(hbm) + len(vmem), len(outs)

    def body(*refs):
        rest = refs[n_in + len(after) :]
        rest[n_out][0] = 0
        kernel(*refs[:n_in], *rest[:n_out], *rest[n_out + 1 :])

    return pl.pallas_call(
        body,
        out_shape=(*outs, shape((1,), jnp.int32)),
        in_specs=[SMEM] * len(smem) + [HBM] * len(hbm) + [VMEM] * len(vmem) + [SMEM] * len(after),
        out_specs=(VMEM,) * n_out + (SMEM,),
        scratch_shapes=list(scratch),
        cost_estimate=pl.CostEstimate(flops=0, bytes_accessed=0, transcendentals=0),
        compiler_params=pltpu.CompilerParams(vmem_limit_bytes=mib << 20),
    )(*smem, *hbm, *vmem, *after)


class Place:
    def __init__(self, n_f, n_t, n_d):
        self.n_f, self.n_t, self.n_d, self.chips = n_f, n_t, n_d, n_d // 2

    f = property(lambda self: lax.axis_index("fsdp"))
    t = property(lambda self: lax.axis_index("tensor"))
    chip = property(lambda self: lax.axis_index("dp") // 2)
    core = property(lambda self: lax.rem(lax.axis_index("dp"), 2))

    def live(self, counts):
        return counts[self.f * self.n_t + self.t]


def fetch(*pairs_and_sems):
    copies = [pltpu.make_async_copy(src, dst, sem) for src, dst, sem in pairs_and_sems]
    for copy in copies:
        copy.start()
    return copies


def add_blocks(place, q_blocks, step, counts, rows, cols, tok, vals, acc):
    first = lax.rem(place.f + step, place.n_f) * q_blocks

    def body(s, carry):
        col = cols[s] - first

        @pl.when((col >= 0) & (col < q_blocks))
        def _():
            acc[:, lanes(col)] += jnp.dot(tok[:, lanes(rows[s])], vals[s], preferred_element_type=F32)

        return carry

    lax.fori_loop(0, place.live(counts), body, 0)


def front_kernel(
    place, q_blocks, counts, rows, cols, tok, left, cot, right, vals,
    rank, low, back, s1, s2, s3, ahead, behind,
    tokv, leftv, cotv, rightv, valv, full, acc, sems,
):
    quarter = cotv.shape[1]
    here = pl.ds(pl.multiple_of(place.f * quarter, SIDE), quarter)
    c_tok, c_left, c_val, c_cot, c_right = fetch(
        (tok, tokv, sems.at[0]),
        (left.at[:, lanes(place.t)], leftv, sems.at[1]),
        (vals, valv, sems.at[2]),
        (cot.at[:, here], cotv, sems.at[3]),
        (right, rightv, sems.at[4]),
    )
    acc[...] = jnp.zeros_like(acc)
    c_tok.wait()
    c_left.wait()
    rank[...] = jnp.dot(tokv[...], leftv[...], preferred_element_type=F32)
    low[...] = rank[...].astype(BF16)
    c_val.wait()
    add_blocks(place, q_blocks, place.n_f // 2, counts, rows, cols, tokv, valv, acc)
    half = ahead.shape[0]
    ahead[...] = acc[:half].astype(BF16)
    behind[...] = acc[half:].astype(BF16)
    c_cot.wait()
    c_right.wait()
    full[...] = lax.dot_general(cotv[...], rightv[...], COLS, preferred_element_type=F32)
    back[...] = full[:, lanes(place.t)]
    for k, out in ((1, s1), (2, s2), (3, s3)):
        out[...] = full[:, lanes(lax.rem(place.t + k, place.n_t))].astype(BF16)


def total_kernel(own, g1, g2, g3, *outs):
    total = own[...] + g1[...].astype(F32) + g2[...].astype(F32) + g3[...].astype(F32)
    for out in outs:
        out[...] = total.astype(out.dtype)


def residual_kernel(place, q_blocks, steps, counts, rows, cols, tok, vals, *refs):
    outs, acc = refs[:-1], refs[-1]
    for step, out in zip(steps, outs):
        acc[...] = jnp.zeros_like(acc)
        add_blocks(place, q_blocks, step, counts, rows, cols, tok, vals, acc)
        out[...] = acc[...].astype(BF16)


def blocks_kernel(place, counts, rows, cols, tok, cot, mine, theirs):
    live = place.live(counts)
    per = mine.shape[1] // SIDE

    def body(owner, carry):
        grads = []
        for u in range(per):
            s = owner * per + u
            grad = lax.dot_general(
                tok[:, lanes(rows[s])], cot[:, lanes(cols[s])], ROWS, preferred_element_type=F32
            )
            grads.append(jnp.where(s < live, grad, jnp.zeros_like(grad)))
        j = lax.rem(owner // 2 - place.chip + place.chips, place.chips)
        keep = lax.rem(owner, 2) == place.core

        @pl.when(keep)
        def _():
            for u, grad in enumerate(grads):
                mine[j, u * SIDE : (u + 1) * SIDE] = grad

        @pl.when(jnp.logical_not(keep))
        def _():
            for u, grad in enumerate(grads):
                theirs[j, u * SIDE : (u + 1) * SIDE] = grad.astype(BF16)

        return carry

    lax.fori_loop(0, place.n_d, body, 0)


def factors_kernel(
    place, tok, cot, g0, g1, g2, g3, b0, b1, b2, b3, blocks_mine, blocks_theirs,
    mine, out1, out2, out3, theirs0, left, right,
):
    quarter = right.shape[1]
    here = pl.ds(pl.multiple_of(place.f * quarter, SIDE), quarter)
    n_l = left.shape[0] // place.n_d
    n_r = right.shape[0] // place.n_d
    n_lr = n_l + quarter // SIDE * n_r
    outs = (out1, out2, out3)
    theirs = (theirs0, *outs)
    for j in range(place.chips):
        mine[j, n_lr:] = blocks_mine[j]
        theirs[j][n_lr : n_lr + blocks_theirs.shape[1]] = blocks_theirs[j]
    back = b0[...] + b1[...].astype(F32) + b2[...].astype(F32) + b3[...].astype(F32)
    left[...] = lax.dot_general(
        back.astype(BF16), tok[...], ROWS, preferred_element_type=F32
    ).T
    for k, g in enumerate((g0, g1, g2, g3)):
        at = span(lax.rem(place.t - k + place.n_t, place.n_t), SIDE)
        right[at, :] = lax.dot_general(
            g[...], cot[:, here], ROWS, preferred_element_type=F32
        )
    for j in range(place.chips):
        chip = lax.rem(place.chip + j, place.chips)
        for core, out in ((place.core, mine.at[j]), (1 - place.core, theirs[j])):
            at = chip * 2 + core
            out[:n_l] = left[span(at, n_l), :].astype(out.dtype)
            for p in range(quarter // SIDE):
                out[n_l + p * n_r : n_l + (p + 1) * n_r] = right[
                    span(at, n_r), p * SIDE : (p + 1) * SIDE
                ].astype(out.dtype)
    row, n_all = 0, theirs0.shape[0]
    for out in outs:
        extra = out.shape[0] - n_all
        out[n_all:] = theirs0[row : row + extra]
        row += extra


def cores_kernel(n_l, mine, got1, got2, got3, own, near, ahead, behind, far):
    mid = n_l + (own.shape[0] - n_l) // 2
    got = (None, got1, got2, got3)

    def both(k, lo, hi):
        return mine[k, lo:hi] + got[k][lo:hi].astype(F32)

    row = 0
    for g in got[1:]:
        extra = g.shape[0] - own.shape[0]
        own[row : row + extra] = mine[0, row : row + extra] + g[own.shape[0] :].astype(F32)
        row += extra

    end = own.shape[0]
    half = end - mid
    far[...] = both(2, 0, n_l).astype(BF16)
    ahead[:n_l] = both(1, 0, n_l).astype(BF16)
    behind[:n_l] = both(3, 0, n_l).astype(BF16)
    ahead[n_l:mid] = both(2, n_l, mid).astype(BF16)
    behind[n_l:mid] = both(2, mid, end).astype(BF16)
    ahead[mid:] = both(1, mid, end).astype(BF16)
    behind[mid:] = both(3, n_l, mid).astype(BF16)
    near[:half] = both(1, n_l, mid)
    near[half:] = both(3, mid, end)


def relay_kernel(own, near, from_behind, from_ahead, from_far, left, ahead, behind):
    n_l, half = left.shape[0], ahead.shape[0]
    mid = n_l + half
    left[...] = (
        own[:n_l] + from_behind[:n_l].astype(F32) + from_ahead[:n_l].astype(F32)
        + from_far[...].astype(F32)
    ).astype(BF16)
    ahead[...] = (near[:half] + from_behind[n_l:mid].astype(F32)).astype(BF16)
    behind[...] = (near[half:] + from_ahead[n_l:mid].astype(F32)).astype(BF16)


def chunk_kernel(own, from_behind, from_ahead, last_behind, last_ahead, pair, far, out):
    half, n = last_behind.shape[0], pair.shape[0]
    n_l = own.shape[0] - 2 * half
    mid = n_l + half
    out[:n] = pair[...]
    out[n : 2 * n] = far[...]
    out[2 * n : 2 * n + half] = (
        own[n_l:mid] + from_ahead[mid:].astype(F32) + last_behind[...].astype(F32)
    ).astype(BF16)
    out[2 * n + half :] = (
        own[mid:] + from_behind[mid:].astype(F32) + last_ahead[...].astype(F32)
    ).astype(BF16)


def stack_kernel(a, b, out):
    out[: a.shape[0]] = a[...]
    out[a.shape[0] :] = b[...]


def pass_kernel(p1, p3, from_behind, from_ahead, ahead, behind):
    half = from_behind.shape[0]
    ahead[:half] = (p1[:half].astype(F32) + from_behind[...].astype(F32)).astype(BF16)
    ahead[half:] = p1[half:]
    behind[:half] = p3[:half]
    behind[half:] = (p3[half:].astype(F32) + from_ahead[...].astype(F32)).astype(BF16)


def low_kernel(place, q_blocks, counts, rows, cols, tok, vals, g0, g1, g2, g3, right, out):
    acc = jnp.zeros(out.shape, F32)
    for k, g in enumerate((g0, g1, g2, g3)):
        at = span(lax.rem(place.t - k + place.n_t, place.n_t), SIDE)
        acc += jnp.dot(g[...], right[at, :], preferred_element_type=F32)
    out[...] = acc
    add_blocks(place, q_blocks, 0, counts, rows, cols, tok, vals, out)


def finish_kernel(low, from_behind, from_ahead, out):
    out[...] = (low[...] + from_behind[...].astype(F32) + from_ahead[...].astype(F32)).astype(BF16)


def spread_kernel(place, *refs):
    refs, (left, right, blocks) = refs[:-3], refs[-3:]
    n_l = left.shape[0] // place.n_d
    n_r = right.shape[0] // place.n_d
    n_b = blocks.shape[0] // place.n_d
    panels = right.shape[1] // SIDE
    n_left = place.n_t * n_l
    t = place.t
    near_t = t + 1 - 2 * lax.rem(t, 2)
    far_t = place.n_t - 1 - t
    order = (t, near_t, far_t, place.n_t - 1 - near_t)
    n = len(refs) // 2
    for core, mine in ((place.core, refs[:n]), (1 - place.core, refs[n:])):
        own, behind, ahead, last = mine
        half = last.shape[0] // 2
        last_behind, last_ahead = last.at[:half], last.at[half:]
        for j, whole in ((0, own), (-1, behind), (1, ahead), (2, None)):
            at = lax.rem(place.chip + j + place.chips, place.chips) * 2 + core

            def copy(dst, where, lo, hi):
                cuts = [lo, hi] if whole is not None or not lo < half < hi else [lo, half, hi]
                for a, b in zip(cuts, cuts[1:]):
                    if whole is not None:
                        piece = whole[a:b]
                    elif a < half:
                        piece = last_behind[a:b]
                    else:
                        piece = last_ahead[a - half : b - half]
                    start = where[0] * (hi - lo) + (a - lo)
                    rows = pl.ds(pl.multiple_of(start, 16), b - a)
                    if where[1] is None:
                        dst[rows, :] = piece
                    else:
                        dst[rows, where[1]] = piece

            for k in range(place.n_t):
                copy(left, (at, lanes(order[k])), k * n_l, (k + 1) * n_l)
            for p in range(panels):
                lo = n_left + p * n_r
                copy(right, (at, pl.ds(p * SIDE, SIDE)), lo, lo + n_r)
            lo = n_left + panels * n_r
            copy(blocks, (at, None), lo, lo + n_b)


def shift(x, axis, n, k):
    return lax.ppermute(x, axis, [(i, (i + k) % n) for i in range(n)])


def chip_shift(x, n_data, k):
    chips = n_data // 2
    perm = [(2 * a + c, 2 * ((a + k) % chips) + c) for a in range(chips) for c in range(2)]
    return lax.ppermute(x, "dp", perm)


def core_swap(x, n_data):
    return lax.ppermute(x, "dp", [(i, i ^ 1) for i in range(n_data)])


def per_device(
    tokens, cotangent, left_factor, right_factor, block_values, block_rows, block_cols, block_counts
):
    n_f = lax.axis_size("fsdp")
    n_t = lax.axis_size("tensor")
    n_d = lax.axis_size("dp")
    place = Place(n_f, n_t, n_d)
    chips = n_d // 2
    maxb = block_values.shape[0]
    tok_rows, features = tokens.shape
    right = right_factor.reshape(right_factor.shape[0], -1)
    rank_size, quarter = right.shape
    q_blocks = quarter // SIDE
    half = tok_rows // 2
    lists = (block_counts, block_rows, block_cols)
    vm, dma = pltpu.VMEM, pltpu.SemaphoreType.DMA

    def bind(kernel, *args):
        return lambda *refs: kernel(place, *args, *refs)

    def over(n, k_shift):
        return [k_shift(k) for k in range(1, n)]

    wide, narrow = shape((tok_rows, SIDE), F32), shape((tok_rows, SIDE), BF16)
    part, whole = shape((half, quarter), BF16), shape((tok_rows, quarter), BF16)
    rank, rank_low, back, *back_out, ahead, behind, step = call(
        bind(front_kernel, q_blocks),
        (wide, narrow, wide, narrow, narrow, narrow, part, part),
        smem=lists,
        hbm=(tokens, left_factor, cotangent, right, block_values),
        scratch=[
            vm((tok_rows, features), BF16),
            vm((features, SIDE), BF16),
            vm((tok_rows, quarter), BF16),
            vm((rank_size, quarter), BF16),
            vm((maxb, SIDE, SIDE), BF16),
            vm((tok_rows, rank_size), F32),
            vm((tok_rows, quarter), F32),
            dma((5,)),
        ],
        mib=50,
    )
    rank_in = over(n_f, lambda k: shift(rank_low, "fsdp", n_f, k))
    back_in = [shift(x, "tensor", n_t, k + 1) for k, x in enumerate(back_out)]

    rank, step = call(total_kernel, (narrow,), vmem=(rank, *rank_in), after=(step,))
    ranks = [rank] + over(n_t, lambda k: shift(rank, "tensor", n_t, k))
    back, back_low, step = call(
        total_kernel, (wide, narrow), vmem=(back, *back_in), after=(step,)
    )
    backs = [back] + over(n_f, lambda k: shift(back_low, "fsdp", n_f, k))

    def hand_on(*refs):
        refs[-1][0] = 0

    ahead, behind, step = pl.pallas_call(
        hand_on,
        out_shape=(part, part, shape((1,), jnp.int32)),
        in_specs=[HBM] * 2 + [VMEM] * 6 + [SMEM],
        out_specs=(HBM, HBM, SMEM),
        input_output_aliases={0: 0, 1: 1},
        compiler_params=pltpu.CompilerParams(vmem_limit_bytes=8 << 20),
    )(ahead, behind, *ranks[1:], *backs[1:], step)
    from_behind = shift(ahead, "fsdp", n_f, 1)
    from_ahead = shift(behind, "fsdp", n_f, -1)

    n_b = maxb // n_d * SIDE
    blocks_mine, blocks_theirs, step = call(
        bind(blocks_kernel),
        (shape((chips, n_b, SIDE), F32), shape((chips, n_b, SIDE), BF16)),
        smem=lists,
        vmem=(tokens, cotangent),
        after=(step,),
        mib=20,
    )

    n_l = features // n_d
    n_r = rank_size // n_d
    n_rest = q_blocks * n_r + n_b
    n_all = n_l + n_rest
    chunk = shape((n_all, SIDE), BF16)
    extra = -(-n_all // 3 // 16) * 16
    mine, *theirs, step = call(
        bind(factors_kernel),
        (shape((chips, n_all, SIDE), F32),)
        + tuple(shape((n_all + n, SIDE), BF16) for n in (extra, extra, n_all - 2 * extra)),
        vmem=(tokens, cotangent, *ranks, *backs, blocks_mine, blocks_theirs),
        scratch=[
            vm((n_all, SIDE), BF16),
            vm((features, SIDE), F32),
            vm((rank_size, quarter), F32),
        ],
        after=(step,),
        mib=36,
    )
    got = [core_swap(x, n_d) for x in theirs]
    p1, p3, step = call(
        bind(residual_kernel, q_blocks, (1, 3)),
        (whole, whole),
        smem=lists,
        vmem=(tokens, block_values),
        scratch=[vm((tok_rows, quarter), F32)],
        after=(step,),
        mib=20,
    )
    own, c_near, c_ahead, c_behind, c_far, step = call(
        lambda *refs: cores_kernel(n_l, *refs),
        (
            shape((n_all, SIDE), F32),
            shape((n_rest, SIDE), F32),
            chunk,
            chunk,
            shape((n_l, SIDE), BF16),
        ),
        vmem=(mine, *got),
        after=(step,),
        mib=16,
    )
    c_from_behind = chip_shift(c_ahead, n_d, 1)
    c_from_ahead = chip_shift(c_behind, n_d, -1)
    c_from_far = chip_shift(c_far, n_d, 2)

    ahead, behind, step = call(
        pass_kernel, (whole, whole), vmem=(p1, p3, from_behind, from_ahead), after=(step,), mib=16
    )
    last_behind = shift(ahead, "fsdp", n_f, 1)
    last_ahead = shift(behind, "fsdp", n_f, -1)
    low, step = call(
        bind(low_kernel, q_blocks),
        (shape((tok_rows, quarter), F32),),
        smem=lists,
        vmem=(tokens, block_values, *ranks, right),
        after=(step,),
        mib=20,
    )

    left, c_ahead, c_behind, step = call(
        relay_kernel,
        (shape((n_l, SIDE), BF16),) + (shape((n_rest // 2, SIDE), BF16),) * 2,
        vmem=(own, c_near, c_from_behind, c_from_ahead, c_from_far),
        after=(step,),
    )
    left_near = lax.ppermute(left, "tensor", [(i, i ^ 1) for i in range(n_t)])
    c_last_behind = chip_shift(c_ahead, n_d, 1)
    c_last_ahead = chip_shift(c_behind, n_d, -1)
    left_pair, step = call(
        stack_kernel, (shape((2 * n_l, SIDE), BF16),), vmem=(left, left_near), after=(step,)
    )
    left_far = lax.ppermute(left_pair, "tensor", [(i, n_t - 1 - i) for i in range(n_t)])
    n_msg = n_t * n_l + n_rest
    message, step = call(
        chunk_kernel,
        (shape((n_msg, SIDE), BF16),),
        vmem=(own, c_from_behind, c_from_ahead, c_last_behind, c_last_ahead, left_pair, left_far),
        after=(step,),
    )

    m_behind = chip_shift(message, n_d, 1)
    m_ahead = chip_shift(message, n_d, -1)
    m_last_behind = chip_shift(m_behind[: n_msg // 2], n_d, 1)
    m_last_ahead = chip_shift(m_ahead[n_msg // 2 :], n_d, -1)
    ours = (message, m_behind, m_ahead, jnp.concatenate([m_last_behind, m_last_ahead], axis=0))
    partner = [core_swap(x, n_d) for x in ours]

    out_left, out_right, out_blocks, step = call(
        bind(spread_kernel),
        (
            shape((features, rank_size), BF16),
            shape((rank_size, quarter), BF16),
            shape((maxb * SIDE, SIDE), BF16),
        ),
        vmem=(*ours, *partner),
        mib=14,
    )
    mixed, _ = call(
        finish_kernel, (whole,), vmem=(low, last_behind, last_ahead), mib=12
    )
    return (
        mixed.reshape(tok_rows, 1, quarter),
        out_left,
        out_right.reshape(right_factor.shape),
        out_blocks.reshape(maxb, SIDE, SIDE),
    )


def solution(mesh):
    return jax.shard_map(
        per_device,
        mesh=mesh,
        in_specs=(
            P("dp", "fsdp"),
            P("dp", "tensor"),
            P("fsdp", None),
            P(None, "tensor", "fsdp"),
            P(("fsdp", "tensor"), None, None),
            P(("fsdp", "tensor")),
            P(("fsdp", "tensor")),
            P(),
        ),
        out_specs=(
            P("dp", "tensor", "fsdp"),
            P("fsdp", None),
            P(None, "tensor", "fsdp"),
            P(("fsdp", "tensor"), None, None),
        ),
        check_vma=False,
    )
```

profile of v0, /device:TPU:1, one launch (start us, length us, event | category | flops | bytes accessed | tf_op | source)
XLA Modules:
  0.0 132.5 jit_solution(1981239311175802833)
XLA Ops:
  4.2 6.1 %shard_map.111 = (f32[640,128]{1,0:T(8,128)S(1)}, bf16[640,128]{1,0:T(8,128)(2,1)S(1)}, f32[640,128]{1,0:T(8,128)S(1)}, bf16[640,128]{1,0:T(8,128)(2,1)S(1)}, bf...) custom-call(s32[16]{0:T(128)S(1)} %copy-done.4, ...), custom_call_target="tpu_custom_call" | custom-call | tf_op jit(solution)/shard_map/pallas_call | solution.py:38
  10.3 2.4 %collective-permute-start = (bf16[640,128]{1,0:T(8,128)(2,1)S(1)}, bf16[640,128]{1,0:T(8,128)(2,1)S(1)}, u32[]{:S(2)}, u32[]{:S(2)}) collective-permute-start(bf16[640,128]{1,0:T(8,128)(2,1)S(1)} %get-tuple-element.55), channel_id=1, source_target_pairs={{0,4},{4,8},{8,12},{12,0},{1,5},{5,9},{9,13},{13,1},{2,6},{6,10},{... | collective-permute-start | bytes 491528 | tf_op jit(solution)/shard_map/ppermute | solution.py:321
  12.7 2.7 %collective-permute-start.1 = (bf16[640,128]{1,0:T(8,128)(2,1)S(1)}, bf16[640,128]{1,0:T(8,128)(2,1)S(1)}, u32[]{:S(2)}, u32[]{:S(2)}) collective-permute-start(bf16[640,128]{1,0:T(8,128)(2,1)S(1)} %get-tuple-element.55), channel_id=1, source_target_pairs={{0,8},{4,12},{8,0},{12,4},{1,9},{5,13},{9,1},{13,5},{2,10},{6,14},... | collective-permute-start | bytes 491528 | tf_op jit(solution)/shard_map/ppermute | solution.py:321
  17.4 4.1 %collective-permute-start.7 = (bf16[640,128]{1,0:T(8,128)(2,1)S(1)}, bf16[640,128]{1,0:T(8,128)(2,1)S(1)}, u32[]{:S(2)}, u32[]{:S(2)}) collective-permute-start(bf16[640,128]{1,0:T(8,128)(2,1)S(1)} %get-tuple-element.60), channel_id=1, source_target_pairs={{0,2},{1,3},{2,0},{3,1},{4,6},{5,7},{6,4},{7,5},{8,10},{9,11},{10,... | collective-permute-start | bytes 491528 | tf_op jit(solution)/shard_map/ppermute | solution.py:321
  24.9 4.2 %collective-permute-start.4 = (bf16[640,128]{1,0:T(8,128)(2,1)S(1)}, bf16[640,128]{1,0:T(8,128)(2,1)S(1)}, u32[]{:S(2)}, u32[]{:S(2)}) collective-permute-start(bf16[640,128]{1,0:T(8,128)(2,1)S(1)} %get-tuple-element.57.refs_2_.refs_5_), channel_id=1, source_target_pairs={{0,2},{1,3},{2,0},{3,1},{4,6},{5,7},{6,4},{7,5},{8,10},{9,11},{10,... | collective-permute-start | bytes 491528 | tf_op jit(solution)/shard_map/ppermute | solution.py:321
  33.2 3.1 %collective-permute-start.10 = (bf16[640,128]{1,0:T(8,128)(2,1)S(1)}, bf16[640,128]{1,0:T(8,128)(2,1)S(1)}, u32[]{:S(2)}, u32[]{:S(2)}) collective-permute-start(bf16[640,128]{1,0:T(8,128)(2,1)S(1)} %get-tuple-element.64), channel_id=1, source_target_pairs={{0,8},{4,12},{8,0},{12,4},{1,9},{5,13},{9,1},{13,5},{2,10},{6,14},... | collective-permute-start | bytes 491528 | tf_op jit(solution)/shard_map/ppermute | solution.py:321
  37.8 4.6 %collective-permute-done.10.refs_6_.refs_8_ = bf16[640,128]{1,0:T(8,128)(2,1)S(1)} collective-permute-done((bf16[640,128]{1,0:T(8,128)(2,1)S(1)}, bf16[640,128]{1,0:T(8,128)(2,1)S(1)}, u32[]{:S(2)}, u32[]{:S(2)}) %collective-permute-start.10) | collective-permute-done | bytes 163872 | tf_op jit(solution)/shard_map/ppermute | solution.py:321
  44.5 2.4 %collective-permute-start.13 = (bf16[320,1792]{1,0:T(8,128)(2,1)S(1)}, bf16[320,1792]{1,0:T(8,128)(2,1)S(1)}, u32[]{:S(2)}, u32[]{:S(2)}) collective-permute-start(bf16[320,1792]{1,0:T(8,128)(2,1)S(1)} %get-tuple-element.76), channel_id=1, source_target_pairs={{0,12},{4,0},{8,4},{12,8},{1,13},{5,1},{9,5},{13,9},{2,14},{6,2},{... | collective-permute-start | bytes 3440648 | tf_op jit(solution)/shard_map/ppermute | solution.py:321
  46.9 5.8 %shard_map.115 = (f32[4,512,128]{2,1,0:T(8,128)S(1)}, bf16[4,512,128]{2,1,0:T(8,128)(2,1)S(1)}, s32[1]{0:T(128)}) custom-call(s32[16]{0:T(128)S(1)} %copy-done.4, s32[32]{0:T(128)S(1)} %copy-done.6, s32[32]{0:T(128)S(1)} %copy-done.8, bf16[640,2048]{1,0:T(8,128)(2,1)S(1)} %copy-done, bf16[640,7168]{1,0:T(8,128)(2,1)S(1)} %bitcast.5, s32[1]{0:T(128)} %get-tuple-element.68.refs_5_), custom_call_target="tpu_custom_call" | custom-call | tf_op jit(solution)/shard_map/pallas_call | solution.py:38
  52.7 7.1 %shard_map.116 = (f32[4,1664,128]{2,1,0:T(8,128)S(1)}, bf16[2224,128]{1,0:T(8,128)(2,1)S(1)}, bf16[2224,128]{1,0:T(8,128)(2,1)S(1)}, bf16[2208,128]{1,0:T(8,128)(2,1)S(1)}, s32[1]{0:T(128)}) custom-call(bf16[640,2048]{1,0:T(8,128)(2,1)S(1)} %copy-done, bf16[640,7168]{1,0:T(8,128)(2,1)} %refs_1_.7, bf16[640,128]{1,0:T(8,128)(2,1)S(1)} %get-tuple-element.57.refs_2_.refs_5_, ...), custom_call_target="tpu_custom_call" | custom-call | tf_op jit(solution)/shard_map/pallas_call | solution.py:38
  59.8 2.7 %collective-permute-start.14 = (bf16[2224,128]{1,0:T(8,128)(2,1)S(1)}, bf16[2224,128]{1,0:T(8,128)(2,1)S(1)}, u32[]{:S(2)}, u32[]{:S(2)}) collective-permute-start(bf16[2224,128]{1,0:T(8,128)(2,1)S(1)} %get-tuple-element.78), channel_id=1, source_target_pairs={{0,16},{16,0},{32,48},{48,32},{64,80},{80,64},{96,112},{112,96},{1... | collective-permute-start | bytes 1708040 | tf_op jit(solution)/shard_map/ppermute | solution.py:331
  62.9 3.7 %shard_map.117 = (bf16[640,1792]{1,0:T(8,128)(2,1)S(1)}, bf16[640,1792]{1,0:T(8,128)(2,1)S(1)}, s32[1]{0:T(128)}) custom-call(s32[16]{0:T(128)S(1)} %copy-done.4, s32[32]{0:T(128)S(1)} %copy-done.6, s32[32]{0:T(128)S(1)} %copy-done.8, bf16[640,2048]{1,0:T(8,128)(2,1)S(1)} %copy-done, bf16[32,128,128]{2,1,0:T(8,128)(2,1)S(1)} %copy-done.1, ...), custom_call_target="tpu_custom_call" | custom-call | tf_op jit(solution)/shard_map/pallas_call | solution.py:38
  74.0 2.7 %collective-permute-start.18 = (bf16[640,1792]{1,0:T(8,128)(2,1)S(1)}, bf16[640,1792]{1,0:T(8,128)(2,1)S(1)}, u32[]{:S(2)}, u32[]{:S(2)}) collective-permute-start(bf16[640,1792]{1,0:T(8,128)(2,1)S(1)} %get-tuple-element.86), channel_id=1, source_target_pairs={{0,12},{4,0},{8,4},{12,8},{1,13},{5,1},{9,5},{13,9},{2,14},{6,2},{... | collective-permute-start | bytes 6881288 | tf_op jit(solution)/shard_map/ppermute | solution.py:321
  76.7 5.3 %shard_map.120 = (f32[640,1792]{1,0:T(8,128)S(1)}, s32[1]{0:T(128)}) custom-call(s32[16]{0:T(128)S(1)} %copy-done.5, s32[32]{0:T(128)S(1)} %copy-done.7, s32[32]{0:T(128)S(1)} %copy-done.8, bf16[640,2048]{1,0:T(8,128)(2,1)S(1)} %copy-done, bf16[32,128,128]{2,1,0:T(8,128)(2,1)S(1)} %copy-done.1, bf16[640,128]{1,0:T(8,128)(2,1)S(1)} %get-tuple-element.57.refs_2_.refs_5_, ...), custom_call_target="tpu_custom_call" | custom-call | tf_op jit(solution)/shard_map/pallas_call | solution.py:38
  85.1 2.1 %collective-permute-start.23 = (bf16[704,128]{1,0:T(8,128)(2,1)S(1)}, bf16[704,128]{1,0:T(8,128)(2,1)S(1)}, u32[]{:S(2)}, u32[]{:S(2)}) collective-permute-start(bf16[704,128]{1,0:T(8,128)(2,1)S(1)} %get-tuple-element.95), channel_id=1, source_target_pairs={{0,96},{16,112},{32,0},{48,16},{64,32},{80,48},{96,64},{112,80},{1... | collective-permute-start | bytes 540680 | tf_op jit(solution)/shard_map/ppermute | solution.py:327
  89.1 3.1 %collective-permute-start.25 = (bf16[512,128]{1,0:T(8,128)(2,1)S(1)}, bf16[512,128]{1,0:T(8,128)(2,1)S(1)}, u32[]{:S(2)}, u32[]{:S(2)}) collective-permute-start(bf16[512,128]{1,0:T(8,128)(2,1)S(1)} %get-tuple-element.98.refs_5_), channel_id=1, source_target_pairs={{0,3},{1,2},{2,1},{3,0},{4,7},{5,6},{6,5},{7,4},{8,11},{9,10},{10,... | collective-permute-start | bytes 393224 | tf_op jit(solution)/shard_map/ppermute | solution.py:482
  92.2 2.6 %collective-permute-done.25.refs_6_ = bf16[512,128]{1,0:T(8,128)(2,1)S(1)} collective-permute-done((bf16[512,128]{1,0:T(8,128)(2,1)S(1)}, bf16[512,128]{1,0:T(8,128)(2,1)S(1)}, u32[]{:S(2)}, u32[]{:S(2)}) %collective-permute-start.25) | collective-permute-done | bytes 131104 | tf_op jit(solution)/shard_map/ppermute | solution.py:482
  96.4 2.5 %collective-permute-start.27 = (bf16[2432,128]{1,0:T(8,128)(2,1)S(1)}, bf16[2432,128]{1,0:T(8,128)(2,1)S(1)}, u32[]{:S(2)}, u32[]{:S(2)}) collective-permute-start(bf16[2432,128]{1,0:T(8,128)(2,1)S(1)} %get-tuple-element.100.refs_0_), channel_id=1, source_target_pairs={{0,96},{16,112},{32,0},{48,16},{64,32},{80,48},{96,64},{112,80},{1... | collective-permute-start | bytes 1867784 | tf_op jit(solution)/shard_map/ppermute | solution.py:327
  98.8 11.8 %collective-permute-done.26.refs_1_ = bf16[2432,128]{1,0:T(8,128)(2,1)S(1)} collective-permute-done((bf16[2432,128]{1,0:T(8,128)(2,1)S(1)}, bf16[2432,128]{1,0:T(8,128)(2,1)S(1)}, u32[]{:S(2)}, u32[]{:S(2)}) %collective-permute-start.26) | collective-permute-done | bytes 622624 | tf_op jit(solution)/shard_map/ppermute | solution.py:327
  110.7 3.3 %collective-permute-start.30 = (bf16[2432,128]{1,0:T(8,128)(2,1)S(1)}, bf16[2432,128]{1,0:T(8,128)(2,1)S(1)}, u32[]{:S(2)}, u32[]{:S(2)}) collective-permute-start(bf16[2432,128]{1,0:T(8,128)(2,1)S(1)} %get-tuple-element.100.refs_0_), channel_id=1, source_target_pairs={{0,16},{16,0},{32,48},{48,32},{64,80},{80,64},{96,112},{112,96},{1... | collective-permute-start | bytes 1867784 | tf_op jit(solution)/shard_map/ppermute | solution.py:331
  114.0 2.9 %collective-permute-start.29 = (bf16[1216,128]{1,0:T(8,128)(2,1)S(1)}, bf16[1216,128]{1,0:T(8,128)(2,1)S(1)}, u32[]{:S(2)}, u32[]{:S(2)}) collective-permute-start(bf16[1216,128]{1,0:T(8,128)(2,1)S(1)} %slice.9), channel_id=1, source_target_pairs={{0,96},{16,112},{32,0},{48,16},{64,32},{80,48},{96,64},{112,80},{1... | collective-permute-start | bytes 933896 | tf_op jit(solution)/shard_map/ppermute | solution.py:327
  118.0 4.1 %collective-permute-start.31 = (bf16[2432,128]{1,0:T(8,128)(2,1)S(1)}, bf16[2432,128]{1,0:T(8,128)(2,1)S(1)}, u32[]{:S(2)}, u32[]{:S(2)}) collective-permute-start(bf16[2432,128]{1,0:T(8,128)(2,1)S(1)} %collective-permute-done.26.refs_1_), channel_id=1, source_target_pairs={{0,16},{16,0},{32,48},{48,32},{64,80},{80,64},{96,112},{112,96},{1... | collective-permute-start | bytes 1867784 | tf_op jit(solution)/shard_map/ppermute | solution.py:331
  127.1 3.0 %shard_map.125 = (bf16[2048,512]{1,0:T(8,128)(2,1)}, bf16[512,1792]{1,0:T(8,128)(2,1)}, bf16[4096,128]{1,0:T(8,128)(2,1)}, s32[1]{0:T(128)}) custom-call(bf16[2432,128]{1,0:T(8,128)(2,1)S(1)} %get-tuple-element.100.refs_0_, bf16[2432,128]{1,0:T(8,128)(2,1)S(1)} %collective-permute-done.26.refs_1_, bf16[2432,128]{1,0:T(8,128)(2,1)S(1)} %collective-permute-done.27.refs_2_, ...), custom_call_target="tpu_custom_call" | custom-call | tf_op jit(solution)/shard_map/pallas_call | solution.py:38
  130.2 2.1 %shard_map.121 = (bf16[640,1792]{1,0:T(8,128)(2,1)}, s32[1]{0:T(128)}) custom-call(f32[640,1792]{1,0:T(8,128)S(1)} %get-tuple-element.84.refs_0_, bf16[640,1792]{1,0:T(8,128)(2,1)S(1)} %collective-permute-done.17.refs_1_, bf16[640,1792]{1,0:T(8,128)(2,1)S(1)} %collective-permute-done.18.refs_2_), custom_call_target="tpu_custom_call" | custom-call | tf_op jit(solution)/shard_map/pallas_call | solution.py:38
  (88 shorter events, 37.1 us)
Async XLA Ops:
  10.3 11.1 %collective-permute-start = (bf16[640,128]{1,0:T(8,128)(2,1)S(1)}, bf16[640,128]{1,0:T(8,128)(2,1)S(1)}, u32[]{:S(2)}, u32[]{:S(2)}) collective-permute-start(bf16[640,128]{1,0:T(8,128)(2,1)S(1)} %get-tuple-element.55), channel_id=1, source_target_pairs={{0,4},{4,8},{8,12},{12,0},{1,5},{5,9},{9,13},{13,1},{2,6},{6,10},{... | collective-permute-start | bytes 491528 | tf_op jit(solution)/shard_map/ppermute | solution.py:321
  12.7 9.8 %collective-permute-start.1 = (bf16[640,128]{1,0:T(8,128)(2,1)S(1)}, bf16[640,128]{1,0:T(8,128)(2,1)S(1)}, u32[]{:S(2)}, u32[]{:S(2)}) collective-permute-start(bf16[640,128]{1,0:T(8,128)(2,1)S(1)} %get-tuple-element.55), channel_id=1, source_target_pairs={{0,8},{4,12},{8,0},{12,4},{1,9},{5,13},{9,1},{13,5},{2,10},{6,14},... | collective-permute-start | bytes 491528 | tf_op jit(solution)/shard_map/ppermute | solution.py:321
  15.4 7.1 %collective-permute-start.2 = (bf16[640,128]{1,0:T(8,128)(2,1)S(1)}, bf16[640,128]{1,0:T(8,128)(2,1)S(1)}, u32[]{:S(2)}, u32[]{:S(2)}) collective-permute-start(bf16[640,128]{1,0:T(8,128)(2,1)S(1)} %get-tuple-element.55), channel_id=1, source_target_pairs={{0,12},{4,0},{8,4},{12,8},{1,13},{5,1},{9,5},{13,9},{2,14},{6,2},{... | collective-permute-start | bytes 491528 | tf_op jit(solution)/shard_map/ppermute | solution.py:321
  15.9 13.2 %collective-permute-start.6 = (bf16[640,128]{1,0:T(8,128)(2,1)S(1)}, bf16[640,128]{1,0:T(8,128)(2,1)S(1)}, u32[]{:S(2)}, u32[]{:S(2)}) collective-permute-start(bf16[640,128]{1,0:T(8,128)(2,1)S(1)} %get-tuple-element.59), channel_id=1, source_target_pairs={{0,1},{1,2},{2,3},{3,0},{4,5},{5,6},{6,7},{7,4},{8,9},{9,10},{10,1... | collective-permute-start | bytes 491528 | tf_op jit(solution)/shard_map/ppermute | solution.py:321
  17.4 13.1 %collective-permute-start.7 = (bf16[640,128]{1,0:T(8,128)(2,1)S(1)}, bf16[640,128]{1,0:T(8,128)(2,1)S(1)}, u32[]{:S(2)}, u32[]{:S(2)}) collective-permute-start(bf16[640,128]{1,0:T(8,128)(2,1)S(1)} %get-tuple-element.60), channel_id=1, source_target_pairs={{0,2},{1,3},{2,0},{3,1},{4,6},{5,7},{6,4},{7,5},{8,10},{9,11},{10,... | collective-permute-start | bytes 491528 | tf_op jit(solution)/shard_map/ppermute | solution.py:321
  21.4 9.0 %collective-permute-start.8 = (bf16[640,128]{1,0:T(8,128)(2,1)S(1)}, bf16[640,128]{1,0:T(8,128)(2,1)S(1)}, u32[]{:S(2)}, u32[]{:S(2)}) collective-permute-start(bf16[640,128]{1,0:T(8,128)(2,1)S(1)} %get-tuple-element.61), channel_id=1, source_target_pairs={{0,3},{1,0},{2,1},{3,2},{4,7},{5,4},{6,5},{7,6},{8,11},{9,8},{10,9... | collective-permute-start | bytes 491528 | tf_op jit(solution)/shard_map/ppermute | solution.py:321
  23.8 12.5 %collective-permute-start.3 = (bf16[640,128]{1,0:T(8,128)(2,1)S(1)}, bf16[640,128]{1,0:T(8,128)(2,1)S(1)}, u32[]{:S(2)}, u32[]{:S(2)}) collective-permute-start(bf16[640,128]{1,0:T(8,128)(2,1)S(1)} %get-tuple-element.57.refs_2_.refs_5_), channel_id=1, source_target_pairs={{0,1},{1,2},{2,3},{3,0},{4,5},{5,6},{6,7},{7,4},{8,9},{9,10},{10,1... | collective-permute-start | bytes 491528 | tf_op jit(solution)/shard_map/ppermute | solution.py:321
  24.9 11.4 %collective-permute-start.4 = (bf16[640,128]{1,0:T(8,128)(2,1)S(1)}, bf16[640,128]{1,0:T(8,128)(2,1)S(1)}, u32[]{:S(2)}, u32[]{:S(2)}) collective-permute-start(bf16[640,128]{1,0:T(8,128)(2,1)S(1)} %get-tuple-element.57.refs_2_.refs_5_), channel_id=1, source_target_pairs={{0,2},{1,3},{2,0},{3,1},{4,6},{5,7},{6,4},{7,5},{8,10},{9,11},{10,... | collective-permute-start | bytes 491528 | tf_op jit(solution)/shard_map/ppermute | solution.py:321
  29.1 7.2 %collective-permute-start.5 = (bf16[640,128]{1,0:T(8,128)(2,1)S(1)}, bf16[640,128]{1,0:T(8,128)(2,1)S(1)}, u32[]{:S(2)}, u32[]{:S(2)}) collective-permute-start(bf16[640,128]{1,0:T(8,128)(2,1)S(1)} %get-tuple-element.57.refs_2_.refs_5_), channel_id=1, source_target_pairs={{0,3},{1,0},{2,1},{3,2},{4,7},{5,4},{6,5},{7,6},{8,11},{9,8},{10,9... | collective-permute-start | bytes 491528 | tf_op jit(solution)/shard_map/ppermute | solution.py:321
  33.2 9.2 %collective-permute-start.10 = (bf16[640,128]{1,0:T(8,128)(2,1)S(1)}, bf16[640,128]{1,0:T(8,128)(2,1)S(1)}, u32[]{:S(2)}, u32[]{:S(2)}) collective-permute-start(bf16[640,128]{1,0:T(8,128)(2,1)S(1)} %get-tuple-element.64), channel_id=1, source_target_pairs={{0,8},{4,12},{8,0},{12,4},{1,9},{5,13},{9,1},{13,5},{2,10},{6,14},... | collective-permute-start | bytes 491528 | tf_op jit(solution)/shard_map/ppermute | solution.py:321
  43.6 28.8 %collective-permute-start.12 = (bf16[320,1792]{1,0:T(8,128)(2,1)S(1)}, bf16[320,1792]{1,0:T(8,128)(2,1)S(1)}, u32[]{:S(2)}, u32[]{:S(2)}) collective-permute-start(bf16[320,1792]{1,0:T(8,128)(2,1)S(1)} %get-tuple-element.75), channel_id=1, source_target_pairs={{0,4},{4,8},{8,12},{12,0},{1,5},{5,9},{9,13},{13,1},{2,6},{6,10},{... | collective-permute-start | bytes 3440648 | tf_op jit(solution)/shard_map/ppermute | solution.py:321
  44.5 28.0 %collective-permute-start.13 = (bf16[320,1792]{1,0:T(8,128)(2,1)S(1)}, bf16[320,1792]{1,0:T(8,128)(2,1)S(1)}, u32[]{:S(2)}, u32[]{:S(2)}) collective-permute-start(bf16[320,1792]{1,0:T(8,128)(2,1)S(1)} %get-tuple-element.76), channel_id=1, source_target_pairs={{0,12},{4,0},{8,4},{12,8},{1,13},{5,1},{9,5},{13,9},{2,14},{6,2},{... | collective-permute-start | bytes 3440648 | tf_op jit(solution)/shard_map/ppermute | solution.py:321
  68.1 15.0 %collective-permute-start.19 = (bf16[1664,128]{1,0:T(8,128)(2,1)S(1)}, bf16[1664,128]{1,0:T(8,128)(2,1)S(1)}, u32[]{:S(2)}, u32[]{:S(2)}) collective-permute-start(bf16[1664,128]{1,0:T(8,128)(2,1)S(1)} %get-tuple-element.89), channel_id=1, source_target_pairs={{0,32},{16,48},{32,64},{48,80},{64,96},{80,112},{96,0},{112,16},{1... | collective-permute-start | bytes 1277960 | tf_op jit(solution)/shard_map/ppermute | solution.py:327
  69.4 13.7 %collective-permute-start.20 = (bf16[1664,128]{1,0:T(8,128)(2,1)S(1)}, bf16[1664,128]{1,0:T(8,128)(2,1)S(1)}, u32[]{:S(2)}, u32[]{:S(2)}) collective-permute-start(bf16[1664,128]{1,0:T(8,128)(2,1)S(1)} %get-tuple-element.90), channel_id=1, source_target_pairs={{0,96},{16,112},{32,0},{48,16},{64,32},{80,48},{96,64},{112,80},{1... | collective-permute-start | bytes 1277960 | tf_op jit(solution)/shard_map/ppermute | solution.py:327
  70.9 12.3 %collective-permute-start.21 = (bf16[256,128]{1,0:T(8,128)(2,1)S(1)}, bf16[256,128]{1,0:T(8,128)(2,1)S(1)}, u32[]{:S(2)}, u32[]{:S(2)}) collective-permute-start(bf16[256,128]{1,0:T(8,128)(2,1)S(1)} %get-tuple-element.92), channel_id=1, source_target_pairs={{0,64},{16,80},{32,96},{48,112},{64,0},{80,16},{96,32},{112,48},{1... | collective-permute-start | bytes 196616 | tf_op jit(solution)/shard_map/ppermute | solution.py:327
  73.9 56.3 %collective-permute-start.17 = (bf16[640,1792]{1,0:T(8,128)(2,1)S(1)}, bf16[640,1792]{1,0:T(8,128)(2,1)S(1)}, u32[]{:S(2)}, u32[]{:S(2)}) collective-permute-start(bf16[640,1792]{1,0:T(8,128)(2,1)S(1)} %get-tuple-element.85), channel_id=1, source_target_pairs={{0,4},{4,8},{8,12},{12,0},{1,5},{5,9},{9,13},{13,1},{2,6},{6,10},{... | collective-permute-start | bytes 6881288 | tf_op jit(solution)/shard_map/ppermute | solution.py:321
  74.0 56.2 %collective-permute-start.18 = (bf16[640,1792]{1,0:T(8,128)(2,1)S(1)}, bf16[640,1792]{1,0:T(8,128)(2,1)S(1)}, u32[]{:S(2)}, u32[]{:S(2)}) collective-permute-start(bf16[640,1792]{1,0:T(8,128)(2,1)S(1)} %get-tuple-element.86), channel_id=1, source_target_pairs={{0,12},{4,0},{8,4},{12,8},{1,13},{5,1},{9,5},{13,9},{2,14},{6,2},{... | collective-permute-start | bytes 6881288 | tf_op jit(solution)/shard_map/ppermute | solution.py:321
  84.5 7.7 %collective-permute-start.22 = (bf16[704,128]{1,0:T(8,128)(2,1)S(1)}, bf16[704,128]{1,0:T(8,128)(2,1)S(1)}, u32[]{:S(2)}, u32[]{:S(2)}) collective-permute-start(bf16[704,128]{1,0:T(8,128)(2,1)S(1)} %get-tuple-element.94), channel_id=1, source_target_pairs={{0,32},{16,48},{32,64},{48,80},{64,96},{80,112},{96,0},{112,16},{1... | collective-permute-start | bytes 540680 | tf_op jit(solution)/shard_map/ppermute | solution.py:327
  85.1 7.1 %collective-permute-start.23 = (bf16[704,128]{1,0:T(8,128)(2,1)S(1)}, bf16[704,128]{1,0:T(8,128)(2,1)S(1)}, u32[]{:S(2)}, u32[]{:S(2)}) collective-permute-start(bf16[704,128]{1,0:T(8,128)(2,1)S(1)} %get-tuple-element.95), channel_id=1, source_target_pairs={{0,96},{16,112},{32,0},{48,16},{64,32},{80,48},{96,64},{112,80},{1... | collective-permute-start | bytes 540680 | tf_op jit(solution)/shard_map/ppermute | solution.py:327
  96.1 14.5 %collective-permute-start.26 = (bf16[2432,128]{1,0:T(8,128)(2,1)S(1)}, bf16[2432,128]{1,0:T(8,128)(2,1)S(1)}, u32[]{:S(2)}, u32[]{:S(2)}) collective-permute-start(bf16[2432,128]{1,0:T(8,128)(2,1)S(1)} %get-tuple-element.100.refs_0_), channel_id=1, source_target_pairs={{0,32},{16,48},{32,64},{48,80},{64,96},{80,112},{96,0},{112,16},{1... | collective-permute-start | bytes 1867784 | tf_op jit(solution)/shard_map/ppermute | solution.py:327
  96.4 17.7 %collective-permute-start.27 = (bf16[2432,128]{1,0:T(8,128)(2,1)S(1)}, bf16[2432,128]{1,0:T(8,128)(2,1)S(1)}, u32[]{:S(2)}, u32[]{:S(2)}) collective-permute-start(bf16[2432,128]{1,0:T(8,128)(2,1)S(1)} %get-tuple-element.100.refs_0_), channel_id=1, source_target_pairs={{0,96},{16,112},{32,0},{48,16},{64,32},{80,48},{96,64},{112,80},{1... | collective-permute-start | bytes 1867784 | tf_op jit(solution)/shard_map/ppermute | solution.py:327
  110.6 7.3 %collective-permute-start.28 = (bf16[1216,128]{1,0:T(8,128)(2,1)S(1)}, bf16[1216,128]{1,0:T(8,128)(2,1)S(1)}, u32[]{:S(2)}, u32[]{:S(2)}) collective-permute-start(bf16[1216,128]{1,0:T(8,128)(2,1)S(1)} %slice.8), channel_id=1, source_target_pairs={{0,32},{16,48},{32,64},{48,80},{64,96},{80,112},{96,0},{112,16},{1... | collective-permute-start | bytes 933896 | tf_op jit(solution)/shard_map/ppermute | solution.py:327
  110.7 13.9 %collective-permute-start.30 = (bf16[2432,128]{1,0:T(8,128)(2,1)S(1)}, bf16[2432,128]{1,0:T(8,128)(2,1)S(1)}, u32[]{:S(2)}, u32[]{:S(2)}) collective-permute-start(bf16[2432,128]{1,0:T(8,128)(2,1)S(1)} %get-tuple-element.100.refs_0_), channel_id=1, source_target_pairs={{0,16},{16,0},{32,48},{48,32},{64,80},{80,64},{96,112},{112,96},{1... | collective-permute-start | bytes 1867784 | tf_op jit(solution)/shard_map/ppermute | solution.py:331
  114.0 9.7 %collective-permute-start.29 = (bf16[1216,128]{1,0:T(8,128)(2,1)S(1)}, bf16[1216,128]{1,0:T(8,128)(2,1)S(1)}, u32[]{:S(2)}, u32[]{:S(2)}) collective-permute-start(bf16[1216,128]{1,0:T(8,128)(2,1)S(1)} %slice.9), channel_id=1, source_target_pairs={{0,96},{16,112},{32,0},{48,16},{64,32},{80,48},{96,64},{112,80},{1... | collective-permute-start | bytes 933896 | tf_op jit(solution)/shard_map/ppermute | solution.py:327
  (22 other events, 252.8 us)
where the time goes:
time: 132 us
  starting transfers between devices  56.4 us (43%)
  Pallas kernels  43.4 us (33%)
  waiting for transfers between devices  27.8 us (21%)
  local copies, waits for them, and re-layouts  3.67 us (3%)
    pallas_call x14, Pallas kernels, call(): pl.pallas_call(body, out_shape=(*outs, shape((1,), jnp.int32)), in_specs=...  42.3 us
    ppermute x16, starting transfers between devices, shift(): return lax.ppermute(x, axis, [(i, (i + k) % n) for i in range(n)])  29.1 us
    ppermute x9, waiting for transfers between devices, chip_shift(): return lax.ppermute(x, 'dp', perm)  15.7 us
    ppermute x9, starting transfers between devices, chip_shift(): return lax.ppermute(x, 'dp', perm)  12.8 us
    ppermute x7, starting transfers between devices, core_swap(): return lax.ppermute(x, 'dp', [(i, i ^ 1) for i in range(n_data)])  11.4 us
    ppermute x16, waiting for transfers between devices, shift(): return lax.ppermute(x, axis, [(i, (i + k) % n) for i in range(n)])  6.47 us
    unnamed x25, local copies, waits for them, and re-layouts  3.59 us
    ppermute x1, starting transfers between devices, per_device(): lax.ppermute(left_pair, 'tensor', [(i, n_t - 1 - i) for i in range(n_t)])  3.1 us
  transfers between devices with their start and end apart: 34, of which 11 were waited for; matrix products, arithmetic and copies ran while one was open for 0% of the time, Pallas kernels for 26%

commit v1 on v0

--- a/solution.py
+++ b/solution.py
@@ -119,12 +119,25 @@
         out[...] = total.astype(out.dtype)
 
 
-def residual_kernel(place, q_blocks, steps, counts, rows, cols, tok, vals, *refs):
-    outs, acc = refs[:-1], refs[-1]
-    for step, out in zip(steps, outs):
-        acc[...] = jnp.zeros_like(acc)
-        add_blocks(place, q_blocks, step, counts, rows, cols, tok, vals, acc)
-        out[...] = acc[...].astype(BF16)
+def residual_kernel(place, q_blocks, counts, rows, cols, tok, vals, p1, p3, acc):
+    acc[...] = jnp.zeros_like(acc)
+    n_f, f = place.n_f, place.f
+
+    def body(s, carry):
+        q = cols[s] // q_blocks
+        step = lax.rem(q - f + n_f, n_f)
+
+        @pl.when(lax.rem(step, 2) == 1)
+        def _():
+            acc[step // 2, :, lanes(cols[s] - q * q_blocks)] += jnp.dot(
+                tok[:, lanes(rows[s])], vals[s], preferred_element_type=F32
+            )
+
+        return carry
+
+    lax.fori_loop(0, place.live(counts), body, 0)
+    p1[...] = acc[0].astype(BF16)
+    p3[...] = acc[1].astype(BF16)
 
 
 def blocks_kernel(place, counts, rows, cols, tok, cot, mine, theirs):
@@ -159,10 +172,11 @@
 
 def factors_kernel(
     place, tok, cot, g0, g1, g2, g3, b0, b1, b2, b3, blocks_mine, blocks_theirs,
-    mine, out1, out2, out3, theirs0, left, right,
+    mine, out1, out2, out3, theirs0, tokv, cotv, left, right, sems,
 ):
     quarter = right.shape[1]
     here = pl.ds(pl.multiple_of(place.f * quarter, SIDE), quarter)
+    c_tok, c_cot = fetch((tok, tokv, sems.at[0]), (cot.at[:, here], cotv, sems.at[1]))
     n_l = left.shape[0] // place.n_d
     n_r = right.shape[0] // place.n_d
     n_lr = n_l + quarter // SIDE * n_r
@@ -171,14 +185,16 @@
     for j in range(place.chips):
         mine[j, n_lr:] = blocks_mine[j]
         theirs[j][n_lr : n_lr + blocks_theirs.shape[1]] = blocks_theirs[j]
+    c_tok.wait()
     back = b0[...] + b1[...].astype(F32) + b2[...].astype(F32) + b3[...].astype(F32)
     left[...] = lax.dot_general(
-        back.astype(BF16), tok[...], ROWS, preferred_element_type=F32
+        back.astype(BF16), tokv[...], ROWS, preferred_element_type=F32
     ).T
+    c_cot.wait()
     for k, g in enumerate((g0, g1, g2, g3)):
         at = span(lax.rem(place.t - k + place.n_t, place.n_t), SIDE)
         right[at, :] = lax.dot_general(
-            g[...], cot[:, here], ROWS, preferred_element_type=F32
+            g[...], cotv[...], ROWS, preferred_element_type=F32
         )
     for j in range(place.chips):
         chip = lax.rem(place.chip + j, place.chips)
@@ -371,7 +387,7 @@
             vm((tok_rows, quarter), F32),
             dma((5,)),
         ],
-        mib=50,
+        mib=52,
     )
     rank_in = over(n_f, lambda k: shift(rank_low, "fsdp", n_f, k))
     back_in = [shift(x, "tensor", n_t, k + 1) for k, x in enumerate(back_out)]
@@ -382,6 +398,16 @@
         total_kernel, (wide, narrow), vmem=(back, *back_in), after=(step,)
     )
     backs = [back] + over(n_f, lambda k: shift(back_low, "fsdp", n_f, k))
+
+    n_b = maxb // n_d * SIDE
+    blocks_mine, blocks_theirs, step = call(
+        bind(blocks_kernel),
+        (shape((chips, n_b, SIDE), F32), shape((chips, n_b, SIDE), BF16)),
+        smem=lists,
+        vmem=(tokens, cotangent),
+        after=(step,),
+        mib=20,
+    )
 
     def hand_on(*refs):
         refs[-1][0] = 0
@@ -397,16 +423,6 @@
     from_behind = shift(ahead, "fsdp", n_f, 1)
     from_ahead = shift(behind, "fsdp", n_f, -1)
 
-    n_b = maxb // n_d * SIDE
-    blocks_mine, blocks_theirs, step = call(
-        bind(blocks_kernel),
-        (shape((chips, n_b, SIDE), F32), shape((chips, n_b, SIDE), BF16)),
-        smem=lists,
-        vmem=(tokens, cotangent),
-        after=(step,),
-        mib=20,
-    )
-
     n_l = features // n_d
     n_r = rank_size // n_d
     n_rest = q_blocks * n_r + n_b
@@ -417,24 +433,28 @@
         bind(factors_kernel),
         (shape((chips, n_all, SIDE), F32),)
         + tuple(shape((n_all + n, SIDE), BF16) for n in (extra, extra, n_all - 2 * extra)),
-        vmem=(tokens, cotangent, *ranks, *backs, blocks_mine, blocks_theirs),
+        hbm=(tokens, cotangent),
+        vmem=(*ranks, *backs, blocks_mine, blocks_theirs),
         scratch=[
             vm((n_all, SIDE), BF16),
+            vm((tok_rows, features), BF16),
+            vm((tok_rows, quarter), BF16),
             vm((features, SIDE), F32),
             vm((rank_size, quarter), F32),
+            dma((2,)),
         ],
         after=(step,),
         mib=36,
     )
     got = [core_swap(x, n_d) for x in theirs]
     p1, p3, step = call(
-        bind(residual_kernel, q_blocks, (1, 3)),
+        bind(residual_kernel, q_blocks),
         (whole, whole),
         smem=lists,
         vmem=(tokens, block_values),
-        scratch=[vm((tok_rows, quarter), F32)],
-        after=(step,),
-        mib=20,
+        scratch=[vm((2, tok_rows, quarter), F32)],
+        after=(step,),
+        mib=24,
     )
     own, c_near, c_ahead, c_behind, c_far, step = call(
         lambda *refs: cores_kernel(n_l, *refs),
@@ -458,6 +478,19 @@
     )
     last_behind = shift(ahead, "fsdp", n_f, 1)
     last_ahead = shift(behind, "fsdp", n_f, -1)
+    left, c_ahead, c_behind, step = call(
+        relay_kernel,
+        (shape((n_l, SIDE), BF16),) + (shape((n_rest // 2, SIDE), BF16),) * 2,
+        vmem=(own, c_near, c_from_behind, c_from_ahead, c_from_far),
+        after=(step,),
+    )
+    left_near = lax.ppermute(left, "tensor", [(i, i ^ 1) for i in range(n_t)])
+    c_last_behind = chip_shift(c_ahead, n_d, 1)
+    c_last_ahead = chip_shift(c_behind, n_d, -1)
+    left_pair, step = call(
+        stack_kernel, (shape((2 * n_l, SIDE), BF16),), vmem=(left, left_near), after=(step,)
+    )
+    left_far = lax.ppermute(left_pair, "tensor", [(i, n_t - 1 - i) for i in range(n_t)])
     low, step = call(
         bind(low_kernel, q_blocks),
         (shape((tok_rows, quarter), F32),),
@@ -466,20 +499,6 @@
         after=(step,),
         mib=20,
     )
-
-    left, c_ahead, c_behind, step = call(
-        relay_kernel,
-        (shape((n_l, SIDE), BF16),) + (shape((n_rest // 2, SIDE), BF16),) * 2,
-        vmem=(own, c_near, c_from_behind, c_from_ahead, c_from_far),
-        after=(step,),
-    )
-    left_near = lax.ppermute(left, "tensor", [(i, i ^ 1) for i in range(n_t)])
-    c_last_behind = chip_shift(c_ahead, n_d, 1)
-    c_last_ahead = chip_shift(c_behind, n_d, -1)
-    left_pair, step = call(
-        stack_kernel, (shape((2 * n_l, SIDE), BF16),), vmem=(left, left_near), after=(step,)
-    )
-    left_far = lax.ppermute(left_pair, "tensor", [(i, n_t - 1 - i) for i in range(n_t)])
     n_msg = n_t * n_l + n_rest
     message, step = call(
         chunk_kernel,

time: 132 us -> 132 us (level)
  starting transfers between devices: 56.4 us -> 60.5 us
  Pallas kernels: 43.4 us -> 39.4 us
  waiting for transfers between devices: 27.8 us -> 26.3 us
    pallas_call x14, Pallas kernels: 42.3 us -> 38.1 us  [call(): pl.pallas_call(body, out_shape=(*outs, shape((1,), jnp.int32)), in_specs=...]
    ppermute x16, starting transfers between devices: 29.1 us -> 32.4 us  [shift(): return lax.ppermute(x, axis, [(i, (i + k) % n) for i in range(n)])]
    ppermute x1, waiting for transfers between devices: 2.65 us -> 0.01 us  [per_device(): lax.ppermute(left_pair, 'tensor', [(i, n_t - 1 - i) for i in range(n_t)])]
    ppermute x16, waiting for transfers between devices: 6.47 us -> 8.8 us  [shift(): return lax.ppermute(x, axis, [(i, (i + k) % n) for i in range(n)])]
    unnamed x25 -> x29, local copies, waits for them, and re-layouts: 3.59 us -> 4.08 us
  transfers between devices with their start and end apart: 34 -> 34, of which waited for: 11 -> 8; matrix products, arithmetic and copies ran while one was open for 0% -> 0% of each run, Pallas kernels for 26% -> 22%
where the time goes in v1:
time: 132 us
  starting transfers between devices  60.5 us (46%)
  Pallas kernels  39.4 us (30%)
  waiting for transfers between devices  26.3 us (20%)
  local copies, waits for them, and re-layouts  4.16 us (3%)
    pallas_call x14, Pallas kernels, call(): pl.pallas_call(body, out_shape=(*outs, shape((1,), jnp.int32)), in_specs=...  38.1 us
    ppermute x16, starting transfers between devices, shift(): return lax.ppermute(x, axis, [(i, (i + k) % n) for i in range(n)])  32.4 us
    ppermute x9, waiting for transfers between devices, chip_shift(): return lax.ppermute(x, 'dp', perm)  15 us
    ppermute x9, starting transfers between devices, chip_shift(): return lax.ppermute(x, 'dp', perm)  12.7 us
    ppermute x7, starting transfers between devices, core_swap(): return lax.ppermute(x, 'dp', [(i, i ^ 1) for i in range(n_data)])  10.3 us
    ppermute x16, waiting for transfers between devices, shift(): return lax.ppermute(x, axis, [(i, (i + k) % n) for i in range(n)])  8.8 us
    unnamed x29, local copies, waits for them, and re-layouts  4.08 us
    ppermute x1, starting transfers between devices, per_device(): lax.ppermute(left_pair, 'tensor', [(i, n_t - 1 - i) for i in range(n_t)])  3.94 us
  transfers between devices with their start and end apart: 34, of which 8 were waited for; matrix products, arithmetic and copies ran while one was open for 0% of the time, Pallas kernels for 22%

profile of v1, /device:TPU:1, one launch (start us, length us, event | category | flops | bytes accessed | tf_op | source)
XLA Modules:
  0.0 131.5 jit_solution(4546607300995187306)
XLA Ops:
  2.9 5.9 %shard_map.111 = (f32[640,128]{1,0:T(8,128)S(1)}, bf16[640,128]{1,0:T(8,128)(2,1)S(1)}, f32[640,128]{1,0:T(8,128)S(1)}, bf16[640,128]{1,0:T(8,128)(2,1)S(1)}, bf...) custom-call(s32[16]{0:T(128)S(1)} %copy-done.6, ...), custom_call_target="tpu_custom_call" | custom-call | tf_op jit(solution)/shard_map/pallas_call | solution.py:38
  8.9 4.2 %collective-permute-start.2 = (bf16[640,128]{1,0:T(8,128)(2,1)S(1)}, bf16[640,128]{1,0:T(8,128)(2,1)S(1)}, u32[]{:S(2)}, u32[]{:S(2)}) collective-permute-start(bf16[640,128]{1,0:T(8,128)(2,1)S(1)} %get-tuple-element.55), channel_id=1, source_target_pairs={{0,12},{4,0},{8,4},{12,8},{1,13},{5,1},{9,5},{13,9},{2,14},{6,2},{... | collective-permute-start | bytes 491528 | tf_op jit(solution)/shard_map/ppermute | solution.py:337
  16.0 3.1 %collective-permute-start.7 = (bf16[640,128]{1,0:T(8,128)(2,1)S(1)}, bf16[640,128]{1,0:T(8,128)(2,1)S(1)}, u32[]{:S(2)}, u32[]{:S(2)}) collective-permute-start(bf16[640,128]{1,0:T(8,128)(2,1)S(1)} %get-tuple-element.60), channel_id=1, source_target_pairs={{0,2},{1,3},{2,0},{3,1},{4,6},{5,7},{6,4},{7,5},{8,10},{9,11},{10,... | collective-permute-start | bytes 491528 | tf_op jit(solution)/shard_map/ppermute | solution.py:337
  19.1 4.7 %collective-permute-start.8 = (bf16[640,128]{1,0:T(8,128)(2,1)S(1)}, bf16[640,128]{1,0:T(8,128)(2,1)S(1)}, u32[]{:S(2)}, u32[]{:S(2)}) collective-permute-start(bf16[640,128]{1,0:T(8,128)(2,1)S(1)} %get-tuple-element.61), channel_id=1, source_target_pairs={{0,3},{1,0},{2,1},{3,2},{4,7},{5,4},{6,5},{7,6},{8,11},{9,8},{10,9... | collective-permute-start | bytes 491528 | tf_op jit(solution)/shard_map/ppermute | solution.py:337
  27.4 3.6 %collective-permute-start.11 = (bf16[640,128]{1,0:T(8,128)(2,1)S(1)}, bf16[640,128]{1,0:T(8,128)(2,1)S(1)}, u32[]{:S(2)}, u32[]{:S(2)}) collective-permute-start(bf16[640,128]{1,0:T(8,128)(2,1)S(1)} %get-tuple-element.64), channel_id=1, source_target_pairs={{0,12},{4,0},{8,4},{12,8},{1,13},{5,1},{9,5},{13,9},{2,14},{6,2},{... | collective-permute-start | bytes 491528 | tf_op jit(solution)/shard_map/ppermute | solution.py:337
  31.6 3.4 %collective-permute-start.5 = (bf16[640,128]{1,0:T(8,128)(2,1)S(1)}, bf16[640,128]{1,0:T(8,128)(2,1)S(1)}, u32[]{:S(2)}, u32[]{:S(2)}) collective-permute-start(bf16[640,128]{1,0:T(8,128)(2,1)S(1)} %get-tuple-element.57.refs_2_.refs_5_), channel_id=1, source_target_pairs={{0,3},{1,0},{2,1},{3,2},{4,7},{5,4},{6,5},{7,6},{8,11},{9,8},{10,9... | collective-permute-start | bytes 491528 | tf_op jit(solution)/shard_map/ppermute | solution.py:337
  35.1 3.2 %collective-permute-start.3 = (bf16[640,128]{1,0:T(8,128)(2,1)S(1)}, bf16[640,128]{1,0:T(8,128)(2,1)S(1)}, u32[]{:S(2)}, u32[]{:S(2)}) collective-permute-start(bf16[640,128]{1,0:T(8,128)(2,1)S(1)} %get-tuple-element.57.refs_2_.refs_5_), channel_id=1, source_target_pairs={{0,1},{1,2},{2,3},{3,0},{4,5},{5,6},{6,7},{7,4},{8,9},{9,10},{10,1... | collective-permute-start | bytes 491528 | tf_op jit(solution)/shard_map/ppermute | solution.py:337
  40.0 5.9 %shard_map.114 = (f32[4,512,128]{2,1,0:T(8,128)S(1)}, bf16[4,512,128]{2,1,0:T(8,128)(2,1)S(1)}, s32[1]{0:T(128)}) custom-call(s32[16]{0:T(128)S(1)} %copy-done.7, s32[32]{0:T(128)S(1)} %copy-done.9, s32[32]{0:T(128)S(1)} %copy-done.10, bf16[640,2048]{1,0:T(8,128)(2,1)S(1)} %copy-done, bf16[640,7168]{1,0:T(8,128)(2,1)S(1)} %bitcast.5, s32[1]{0:T(128)} %get-tuple-element.65.refs_5_), custom_call_target="tpu_custom_call" | custom-call | tf_op jit(solution)/shard_map/pallas_call | solution.py:38
  47.5 3.6 %collective-permute-start.19 = (bf16[320,1792]{1,0:T(8,128)(2,1)S(1)}, bf16[320,1792]{1,0:T(8,128)(2,1)S(1)}, u32[]{:S(2)}, u32[]{:S(2)}) collective-permute-start(bf16[320,1792]{1,0:T(8,128)(2,1)S(1)} %get-tuple-element.86), channel_id=1, source_target_pairs={{0,12},{4,0},{8,4},{12,8},{1,13},{5,1},{9,5},{13,9},{2,14},{6,2},{... | collective-permute-start | bytes 3440648 | tf_op jit(solution)/shard_map/ppermute | solution.py:337
  51.1 4.8 %shard_map.116 = (f32[4,1664,128]{2,1,0:T(8,128)S(1)}, bf16[2224,128]{1,0:T(8,128)(2,1)S(1)}, bf16[2224,128]{1,0:T(8,128)(2,1)S(1)}, bf16[2208,128]{1,0:T(8,128)(2,1)S(1)}, s32[1]{0:T(128)}) custom-call(bf16[640,2048]{1,0:T(8,128)(2,1)S(1)} %copy-done.1, bf16[640,7168]{1,0:T(8,128)(2,1)} %refs_1_.7, bf16[640,128]{1,0:T(8,128)(2,1)S(1)} %get-tuple-element.57.refs_2_.refs_5_, ...), custom_call_target="tpu_custom_call" | custom-call | tf_op jit(solution)/shard_map/pallas_call | solution.py:38
  55.9 2.1 %collective-permute-start.12 = (bf16[2224,128]{1,0:T(8,128)(2,1)S(1)}, bf16[2224,128]{1,0:T(8,128)(2,1)S(1)}, u32[]{:S(2)}, u32[]{:S(2)}) collective-permute-start(bf16[2224,128]{1,0:T(8,128)(2,1)S(1)} %get-tuple-element.73), channel_id=1, source_target_pairs={{0,16},{16,0},{32,48},{48,32},{64,80},{80,64},{96,112},{112,96},{1... | collective-permute-start | bytes 1708040 | tf_op jit(solution)/shard_map/ppermute | solution.py:347
  58.5 2.8 %shard_map.117 = (bf16[640,1792]{1,0:T(8,128)(2,1)S(1)}, bf16[640,1792]{1,0:T(8,128)(2,1)S(1)}, s32[1]{0:T(128)}) custom-call(s32[16]{0:T(128)S(1)} %copy-done.7, s32[32]{0:T(128)S(1)} %copy-done.9, s32[32]{0:T(128)S(1)} %copy-done.10, bf16[640,2048]{1,0:T(8,128)(2,1)S(1)} %copy-done.1, bf16[32,128,128]{2,1,0:T(8,128)(2,1)S(1)} %copy-done.2, ...), custom_call_target="tpu_custom_call" | custom-call | tf_op jit(solution)/shard_map/pallas_call | solution.py:38
  67.1 7.7 %collective-permute-done.18.refs_2_ = bf16[320,1792]{1,0:T(8,128)(2,1)S(1)} collective-permute-done((bf16[320,1792]{1,0:T(8,128)(2,1)S(1)}, bf16[320,1792]{1,0:T(8,128)(2,1)S(1)}, u32[]{:S(2)}, u32[]{:S(2)}) %collective-permute-start.18) | collective-permute-done | bytes 1146912 | tf_op jit(solution)/shard_map/ppermute | solution.py:337
  76.8 2.1 %collective-permute-start.22 = (bf16[640,1792]{1,0:T(8,128)(2,1)S(1)}, bf16[640,1792]{1,0:T(8,128)(2,1)S(1)}, u32[]{:S(2)}, u32[]{:S(2)}) collective-permute-start(bf16[640,1792]{1,0:T(8,128)(2,1)S(1)} %get-tuple-element.94), channel_id=1, source_target_pairs={{0,12},{4,0},{8,4},{12,8},{1,13},{5,1},{9,5},{13,9},{2,14},{6,2},{... | collective-permute-start | bytes 6881288 | tf_op jit(solution)/shard_map/ppermute | solution.py:337
  81.6 2.4 %collective-permute-start.24 = (bf16[704,128]{1,0:T(8,128)(2,1)S(1)}, bf16[704,128]{1,0:T(8,128)(2,1)S(1)}, u32[]{:S(2)}, u32[]{:S(2)}) collective-permute-start(bf16[704,128]{1,0:T(8,128)(2,1)S(1)} %get-tuple-element.97), channel_id=1, source_target_pairs={{0,96},{16,112},{32,0},{48,16},{64,32},{80,48},{96,64},{112,80},{1... | collective-permute-start | bytes 540680 | tf_op jit(solution)/shard_map/ppermute | solution.py:343
  85.2 3.9 %collective-permute-start.25 = (bf16[512,128]{1,0:T(8,128)(2,1)S(1)}, bf16[512,128]{1,0:T(8,128)(2,1)S(1)}, u32[]{:S(2)}, u32[]{:S(2)}) collective-permute-start(bf16[512,128]{1,0:T(8,128)(2,1)S(1)} %get-tuple-element.98.refs_5_), channel_id=1, source_target_pairs={{0,3},{1,2},{2,1},{3,0},{4,7},{5,6},{6,5},{7,4},{8,11},{9,10},{10,... | collective-permute-start | bytes 393224 | tf_op jit(solution)/shard_map/ppermute | solution.py:493
  89.2 4.7 %shard_map.122 = (f32[640,1792]{1,0:T(8,128)S(1)}, s32[1]{0:T(128)}) custom-call(s32[16]{0:T(128)S(1)} %copy-done.7, s32[32]{0:T(128)S(1)} %copy-done.9, s32[32]{0:T(128)S(1)} %copy-done.10, bf16[640,2048]{1,0:T(8,128)(2,1)S(1)} %copy-done.1, bf16[32,128,128]{2,1,0:T(8,128)(2,1)S(1)} %copy-done.2, bf16[640,128]{1,0:T(8,128)(2,1)S(1)} %get-tuple-element.57.refs_2_.refs_5_, ...), custom_call_target="tpu_custom_call" | custom-call | tf_op jit(solution)/shard_map/pallas_call | solution.py:38
  95.5 2.4 %collective-permute-start.27 = (bf16[2432,128]{1,0:T(8,128)(2,1)S(1)}, bf16[2432,128]{1,0:T(8,128)(2,1)S(1)}, u32[]{:S(2)}, u32[]{:S(2)}) collective-permute-start(bf16[2432,128]{1,0:T(8,128)(2,1)S(1)} %get-tuple-element.100.refs_0_), channel_id=1, source_target_pairs={{0,96},{16,112},{32,0},{48,16},{64,32},{80,48},{96,64},{112,80},{1... | collective-permute-start | bytes 1867784 | tf_op jit(solution)/shard_map/ppermute | solution.py:343
  98.0 12.0 %collective-permute-done.26.refs_1_ = bf16[2432,128]{1,0:T(8,128)(2,1)S(1)} collective-permute-done((bf16[2432,128]{1,0:T(8,128)(2,1)S(1)}, bf16[2432,128]{1,0:T(8,128)(2,1)S(1)}, u32[]{:S(2)}, u32[]{:S(2)}) %collective-permute-start.26) | collective-permute-done | bytes 622624 | tf_op jit(solution)/shard_map/ppermute | solution.py:343
  110.1 3.0 %collective-permute-start.30 = (bf16[2432,128]{1,0:T(8,128)(2,1)S(1)}, bf16[2432,128]{1,0:T(8,128)(2,1)S(1)}, u32[]{:S(2)}, u32[]{:S(2)}) collective-permute-start(bf16[2432,128]{1,0:T(8,128)(2,1)S(1)} %get-tuple-element.100.refs_0_), channel_id=1, source_target_pairs={{0,16},{16,0},{32,48},{48,32},{64,80},{80,64},{96,112},{112,96},{1... | collective-permute-start | bytes 1867784 | tf_op jit(solution)/shard_map/ppermute | solution.py:347
  113.2 2.9 %collective-permute-start.29 = (bf16[1216,128]{1,0:T(8,128)(2,1)S(1)}, bf16[1216,128]{1,0:T(8,128)(2,1)S(1)}, u32[]{:S(2)}, u32[]{:S(2)}) collective-permute-start(bf16[1216,128]{1,0:T(8,128)(2,1)S(1)} %slice.9), channel_id=1, source_target_pairs={{0,96},{16,112},{32,0},{48,16},{64,32},{80,48},{96,64},{112,80},{1... | collective-permute-start | bytes 933896 | tf_op jit(solution)/shard_map/ppermute | solution.py:343
  117.4 3.8 %collective-permute-start.32 = (bf16[2432,128]{1,0:T(8,128)(2,1)S(1)}, bf16[2432,128]{1,0:T(8,128)(2,1)S(1)}, u32[]{:S(2)}, u32[]{:S(2)}) collective-permute-start(bf16[2432,128]{1,0:T(8,128)(2,1)S(1)} %collective-permute-done.27.refs_2_), channel_id=1, source_target_pairs={{0,16},{16,0},{32,48},{48,32},{64,80},{80,64},{96,112},{112,96},{1... | collective-permute-start | bytes 1867784 | tf_op jit(solution)/shard_map/ppermute | solution.py:347
  126.2 3.0 %shard_map.125 = (bf16[2048,512]{1,0:T(8,128)(2,1)}, bf16[512,1792]{1,0:T(8,128)(2,1)}, bf16[4096,128]{1,0:T(8,128)(2,1)}, s32[1]{0:T(128)}) custom-call(bf16[2432,128]{1,0:T(8,128)(2,1)S(1)} %get-tuple-element.100.refs_0_, bf16[2432,128]{1,0:T(8,128)(2,1)S(1)} %collective-permute-done.26.refs_1_, bf16[2432,128]{1,0:T(8,128)(2,1)S(1)} %collective-permute-done.27.refs_2_, ...), custom_call_target="tpu_custom_call" | custom-call | tf_op jit(solution)/shard_map/pallas_call | solution.py:38
  129.3 2.1 %shard_map.123 = (bf16[640,1792]{1,0:T(8,128)(2,1)}, s32[1]{0:T(128)}) custom-call(f32[640,1792]{1,0:T(8,128)S(1)} %get-tuple-element.92.refs_0_, bf16[640,1792]{1,0:T(8,128)(2,1)S(1)} %collective-permute-done.21.refs_1_, bf16[640,1792]{1,0:T(8,128)(2,1)S(1)} %collective-permute-done.22.refs_2_), custom_call_target="tpu_custom_call" | custom-call | tf_op jit(solution)/shard_map/pallas_call | solution.py:38
  (92 shorter events, 32.6 us)
Async XLA Ops:
  8.9 10.3 %collective-permute-start.2 = (bf16[640,128]{1,0:T(8,128)(2,1)S(1)}, bf16[640,128]{1,0:T(8,128)(2,1)S(1)}, u32[]{:S(2)}, u32[]{:S(2)}) collective-permute-start(bf16[640,128]{1,0:T(8,128)(2,1)S(1)} %get-tuple-element.55), channel_id=1, source_target_pairs={{0,12},{4,0},{8,4},{12,8},{1,13},{5,1},{9,5},{13,9},{2,14},{6,2},{... | collective-permute-start | bytes 491528 | tf_op jit(solution)/shard_map/ppermute | solution.py:337
  13.1 10.8 %collective-permute-start.1 = (bf16[640,128]{1,0:T(8,128)(2,1)S(1)}, bf16[640,128]{1,0:T(8,128)(2,1)S(1)}, u32[]{:S(2)}, u32[]{:S(2)}) collective-permute-start(bf16[640,128]{1,0:T(8,128)(2,1)S(1)} %get-tuple-element.55), channel_id=1, source_target_pairs={{0,8},{4,12},{8,0},{12,4},{1,9},{5,13},{9,1},{13,5},{2,10},{6,14},... | collective-permute-start | bytes 491528 | tf_op jit(solution)/shard_map/ppermute | solution.py:337
  14.2 9.9 %collective-permute-start = (bf16[640,128]{1,0:T(8,128)(2,1)S(1)}, bf16[640,128]{1,0:T(8,128)(2,1)S(1)}, u32[]{:S(2)}, u32[]{:S(2)}) collective-permute-start(bf16[640,128]{1,0:T(8,128)(2,1)S(1)} %get-tuple-element.55), channel_id=1, source_target_pairs={{0,4},{4,8},{8,12},{12,0},{1,5},{5,9},{9,13},{13,1},{2,6},{6,10},{... | collective-permute-start | bytes 491528 | tf_op jit(solution)/shard_map/ppermute | solution.py:337
  14.2 11.1 %collective-permute-start.6 = (bf16[640,128]{1,0:T(8,128)(2,1)S(1)}, bf16[640,128]{1,0:T(8,128)(2,1)S(1)}, u32[]{:S(2)}, u32[]{:S(2)}) collective-permute-start(bf16[640,128]{1,0:T(8,128)(2,1)S(1)} %get-tuple-element.59), channel_id=1, source_target_pairs={{0,1},{1,2},{2,3},{3,0},{4,5},{5,6},{6,7},{7,4},{8,9},{9,10},{10,1... | collective-permute-start | bytes 491528 | tf_op jit(solution)/shard_map/ppermute | solution.py:337
  16.0 9.3 %collective-permute-start.7 = (bf16[640,128]{1,0:T(8,128)(2,1)S(1)}, bf16[640,128]{1,0:T(8,128)(2,1)S(1)}, u32[]{:S(2)}, u32[]{:S(2)}) collective-permute-start(bf16[640,128]{1,0:T(8,128)(2,1)S(1)} %get-tuple-element.60), channel_id=1, source_target_pairs={{0,2},{1,3},{2,0},{3,1},{4,6},{5,7},{6,4},{7,5},{8,10},{9,11},{10,... | collective-permute-start | bytes 491528 | tf_op jit(solution)/shard_map/ppermute | solution.py:337
  31.0 15.0 %collective-permute-start.10 = (bf16[640,128]{1,0:T(8,128)(2,1)S(1)}, bf16[640,128]{1,0:T(8,128)(2,1)S(1)}, u32[]{:S(2)}, u32[]{:S(2)}) collective-permute-start(bf16[640,128]{1,0:T(8,128)(2,1)S(1)} %get-tuple-element.64), channel_id=1, source_target_pairs={{0,8},{4,12},{8,0},{12,4},{1,9},{5,13},{9,1},{13,5},{2,10},{6,14},... | collective-permute-start | bytes 491528 | tf_op jit(solution)/shard_map/ppermute | solution.py:337
  31.0 15.0 %collective-permute-start.9 = (bf16[640,128]{1,0:T(8,128)(2,1)S(1)}, bf16[640,128]{1,0:T(8,128)(2,1)S(1)}, u32[]{:S(2)}, u32[]{:S(2)}) collective-permute-start(bf16[640,128]{1,0:T(8,128)(2,1)S(1)} %get-tuple-element.64), channel_id=1, source_target_pairs={{0,4},{4,8},{8,12},{12,0},{1,5},{5,9},{9,13},{13,1},{2,6},{6,10},{... | collective-permute-start | bytes 491528 | tf_op jit(solution)/shard_map/ppermute | solution.py:337
  31.6 14.4 %collective-permute-start.5 = (bf16[640,128]{1,0:T(8,128)(2,1)S(1)}, bf16[640,128]{1,0:T(8,128)(2,1)S(1)}, u32[]{:S(2)}, u32[]{:S(2)}) collective-permute-start(bf16[640,128]{1,0:T(8,128)(2,1)S(1)} %get-tuple-element.57.refs_2_.refs_5_), channel_id=1, source_target_pairs={{0,3},{1,0},{2,1},{3,2},{4,7},{5,4},{6,5},{7,6},{8,11},{9,8},{10,9... | collective-permute-start | bytes 491528 | tf_op jit(solution)/shard_map/ppermute | solution.py:337
  35.1 10.9 %collective-permute-start.4 = (bf16[640,128]{1,0:T(8,128)(2,1)S(1)}, bf16[640,128]{1,0:T(8,128)(2,1)S(1)}, u32[]{:S(2)}, u32[]{:S(2)}) collective-permute-start(bf16[640,128]{1,0:T(8,128)(2,1)S(1)} %get-tuple-element.57.refs_2_.refs_5_), channel_id=1, source_target_pairs={{0,2},{1,3},{2,0},{3,1},{4,6},{5,7},{6,4},{7,5},{8,10},{9,11},{10,... | collective-permute-start | bytes 491528 | tf_op jit(solution)/shard_map/ppermute | solution.py:337
  35.1 10.9 %collective-permute-start.3 = (bf16[640,128]{1,0:T(8,128)(2,1)S(1)}, bf16[640,128]{1,0:T(8,128)(2,1)S(1)}, u32[]{:S(2)}, u32[]{:S(2)}) collective-permute-start(bf16[640,128]{1,0:T(8,128)(2,1)S(1)} %get-tuple-element.57.refs_2_.refs_5_), channel_id=1, source_target_pairs={{0,1},{1,2},{2,3},{3,0},{4,5},{5,6},{6,7},{7,4},{8,9},{9,10},{10,1... | collective-permute-start | bytes 491528 | tf_op jit(solution)/shard_map/ppermute | solution.py:337
  47.4 27.5 %collective-permute-start.18 = (bf16[320,1792]{1,0:T(8,128)(2,1)S(1)}, bf16[320,1792]{1,0:T(8,128)(2,1)S(1)}, u32[]{:S(2)}, u32[]{:S(2)}) collective-permute-start(bf16[320,1792]{1,0:T(8,128)(2,1)S(1)} %get-tuple-element.85), channel_id=1, source_target_pairs={{0,4},{4,8},{8,12},{12,0},{1,5},{5,9},{9,13},{13,1},{2,6},{6,10},{... | collective-permute-start | bytes 3440648 | tf_op jit(solution)/shard_map/ppermute | solution.py:337
  47.5 27.4 %collective-permute-start.19 = (bf16[320,1792]{1,0:T(8,128)(2,1)S(1)}, bf16[320,1792]{1,0:T(8,128)(2,1)S(1)}, u32[]{:S(2)}, u32[]{:S(2)}) collective-permute-start(bf16[320,1792]{1,0:T(8,128)(2,1)S(1)} %get-tuple-element.86), channel_id=1, source_target_pairs={{0,12},{4,0},{8,4},{12,8},{1,13},{5,1},{9,5},{13,9},{2,14},{6,2},{... | collective-permute-start | bytes 3440648 | tf_op jit(solution)/shard_map/ppermute | solution.py:337
  62.8 16.1 %collective-permute-start.15 = (bf16[1664,128]{1,0:T(8,128)(2,1)S(1)}, bf16[1664,128]{1,0:T(8,128)(2,1)S(1)}, u32[]{:S(2)}, u32[]{:S(2)}) collective-permute-start(bf16[1664,128]{1,0:T(8,128)(2,1)S(1)} %get-tuple-element.80), channel_id=1, source_target_pairs={{0,32},{16,48},{32,64},{48,80},{64,96},{80,112},{96,0},{112,16},{1... | collective-permute-start | bytes 1277960 | tf_op jit(solution)/shard_map/ppermute | solution.py:343
  64.1 14.8 %collective-permute-start.16 = (bf16[1664,128]{1,0:T(8,128)(2,1)S(1)}, bf16[1664,128]{1,0:T(8,128)(2,1)S(1)}, u32[]{:S(2)}, u32[]{:S(2)}) collective-permute-start(bf16[1664,128]{1,0:T(8,128)(2,1)S(1)} %get-tuple-element.81), channel_id=1, source_target_pairs={{0,96},{16,112},{32,0},{48,16},{64,32},{80,48},{96,64},{112,80},{1... | collective-permute-start | bytes 1277960 | tf_op jit(solution)/shard_map/ppermute | solution.py:343
  65.6 13.3 %collective-permute-start.17 = (bf16[256,128]{1,0:T(8,128)(2,1)S(1)}, bf16[256,128]{1,0:T(8,128)(2,1)S(1)}, u32[]{:S(2)}, u32[]{:S(2)}) collective-permute-start(bf16[256,128]{1,0:T(8,128)(2,1)S(1)} %get-tuple-element.82), channel_id=1, source_target_pairs={{0,64},{16,80},{32,96},{48,112},{64,0},{80,16},{96,32},{112,48},{1... | collective-permute-start | bytes 196616 | tf_op jit(solution)/shard_map/ppermute | solution.py:343
  76.2 53.1 %collective-permute-start.21 = (bf16[640,1792]{1,0:T(8,128)(2,1)S(1)}, bf16[640,1792]{1,0:T(8,128)(2,1)S(1)}, u32[]{:S(2)}, u32[]{:S(2)}) collective-permute-start(bf16[640,1792]{1,0:T(8,128)(2,1)S(1)} %get-tuple-element.93), channel_id=1, source_target_pairs={{0,4},{4,8},{8,12},{12,0},{1,5},{5,9},{9,13},{13,1},{2,6},{6,10},{... | collective-permute-start | bytes 6881288 | tf_op jit(solution)/shard_map/ppermute | solution.py:337
  76.8 52.5 %collective-permute-start.22 = (bf16[640,1792]{1,0:T(8,128)(2,1)S(1)}, bf16[640,1792]{1,0:T(8,128)(2,1)S(1)}, u32[]{:S(2)}, u32[]{:S(2)}) collective-permute-start(bf16[640,1792]{1,0:T(8,128)(2,1)S(1)} %get-tuple-element.94), channel_id=1, source_target_pairs={{0,12},{4,0},{8,4},{12,8},{1,13},{5,1},{9,5},{13,9},{2,14},{6,2},{... | collective-permute-start | bytes 6881288 | tf_op jit(solution)/shard_map/ppermute | solution.py:337
  81.4 12.6 %collective-permute-start.23 = (bf16[704,128]{1,0:T(8,128)(2,1)S(1)}, bf16[704,128]{1,0:T(8,128)(2,1)S(1)}, u32[]{:S(2)}, u32[]{:S(2)}) collective-permute-start(bf16[704,128]{1,0:T(8,128)(2,1)S(1)} %get-tuple-element.96), channel_id=1, source_target_pairs={{0,32},{16,48},{32,64},{48,80},{64,96},{80,112},{96,0},{112,16},{1... | collective-permute-start | bytes 540680 | tf_op jit(solution)/shard_map/ppermute | solution.py:343
  81.6 12.3 %collective-permute-start.24 = (bf16[704,128]{1,0:T(8,128)(2,1)S(1)}, bf16[704,128]{1,0:T(8,128)(2,1)S(1)}, u32[]{:S(2)}, u32[]{:S(2)}) collective-permute-start(bf16[704,128]{1,0:T(8,128)(2,1)S(1)} %get-tuple-element.97), channel_id=1, source_target_pairs={{0,96},{16,112},{32,0},{48,16},{64,32},{80,48},{96,64},{112,80},{1... | collective-permute-start | bytes 540680 | tf_op jit(solution)/shard_map/ppermute | solution.py:343
  85.2 8.7 %collective-permute-start.25 = (bf16[512,128]{1,0:T(8,128)(2,1)S(1)}, bf16[512,128]{1,0:T(8,128)(2,1)S(1)}, u32[]{:S(2)}, u32[]{:S(2)}) collective-permute-start(bf16[512,128]{1,0:T(8,128)(2,1)S(1)} %get-tuple-element.98.refs_5_), channel_id=1, source_target_pairs={{0,3},{1,2},{2,1},{3,0},{4,7},{5,6},{6,5},{7,4},{8,11},{9,10},{10,... | collective-permute-start | bytes 393224 | tf_op jit(solution)/shard_map/ppermute | solution.py:493
  95.2 14.8 %collective-permute-start.26 = (bf16[2432,128]{1,0:T(8,128)(2,1)S(1)}, bf16[2432,128]{1,0:T(8,128)(2,1)S(1)}, u32[]{:S(2)}, u32[]{:S(2)}) collective-permute-start(bf16[2432,128]{1,0:T(8,128)(2,1)S(1)} %get-tuple-element.100.refs_0_), channel_id=1, source_target_pairs={{0,32},{16,48},{32,64},{48,80},{64,96},{80,112},{96,0},{112,16},{1... | collective-permute-start | bytes 1867784 | tf_op jit(solution)/shard_map/ppermute | solution.py:343
  95.5 17.6 %collective-permute-start.27 = (bf16[2432,128]{1,0:T(8,128)(2,1)S(1)}, bf16[2432,128]{1,0:T(8,128)(2,1)S(1)}, u32[]{:S(2)}, u32[]{:S(2)}) collective-permute-start(bf16[2432,128]{1,0:T(8,128)(2,1)S(1)} %get-tuple-element.100.refs_0_), channel_id=1, source_target_pairs={{0,96},{16,112},{32,0},{48,16},{64,32},{80,48},{96,64},{112,80},{1... | collective-permute-start | bytes 1867784 | tf_op jit(solution)/shard_map/ppermute | solution.py:343
  110.1 13.6 %collective-permute-start.30 = (bf16[2432,128]{1,0:T(8,128)(2,1)S(1)}, bf16[2432,128]{1,0:T(8,128)(2,1)S(1)}, u32[]{:S(2)}, u32[]{:S(2)}) collective-permute-start(bf16[2432,128]{1,0:T(8,128)(2,1)S(1)} %get-tuple-element.100.refs_0_), channel_id=1, source_target_pairs={{0,16},{16,0},{32,48},{48,32},{64,80},{80,64},{96,112},{112,96},{1... | collective-permute-start | bytes 1867784 | tf_op jit(solution)/shard_map/ppermute | solution.py:347
  113.2 9.7 %collective-permute-start.29 = (bf16[1216,128]{1,0:T(8,128)(2,1)S(1)}, bf16[1216,128]{1,0:T(8,128)(2,1)S(1)}, u32[]{:S(2)}, u32[]{:S(2)}) collective-permute-start(bf16[1216,128]{1,0:T(8,128)(2,1)S(1)} %slice.9), channel_id=1, source_target_pairs={{0,96},{16,112},{32,0},{48,16},{64,32},{80,48},{96,64},{112,80},{1... | collective-permute-start | bytes 933896 | tf_op jit(solution)/shard_map/ppermute | solution.py:343
  (24 other events, 270.1 us)

commit v2 on v1

--- a/solution.py
+++ b/solution.py
@@ -27,7 +27,7 @@
     return jax.ShapeDtypeStruct(dims, dtype)
 
 
-def call(kernel, outs, smem=(), hbm=(), vmem=(), scratch=(), after=(), mib=8):
+def call(kernel, outs, smem=(), hbm=(), vmem=(), scratch=(), after=(), mib=8, hbm_outs=0):
     n_in, n_out = len(smem) + len(hbm) + len(vmem), len(outs)
 
     def body(*refs):
@@ -39,7 +39,7 @@
         body,
         out_shape=(*outs, shape((1,), jnp.int32)),
         in_specs=[SMEM] * len(smem) + [HBM] * len(hbm) + [VMEM] * len(vmem) + [SMEM] * len(after),
-        out_specs=(VMEM,) * n_out + (SMEM,),
+        out_specs=(VMEM,) * (n_out - hbm_outs) + (HBM,) * hbm_outs + (SMEM,),
         scratch_shapes=list(scratch),
         cost_estimate=pl.CostEstimate(flops=0, bytes_accessed=0, transcendentals=0),
         compiler_params=pltpu.CompilerParams(vmem_limit_bytes=mib << 20),
@@ -84,7 +84,7 @@
 def front_kernel(
     place, q_blocks, counts, rows, cols, tok, left, cot, right, vals,
     rank, low, back, s1, s2, s3, ahead, behind,
-    tokv, leftv, cotv, rightv, valv, full, acc, sems,
+    tokv, leftv, cotv, rightv, valv, full, acc, stage, sems,
 ):
     quarter = cotv.shape[1]
     here = pl.ds(pl.multiple_of(place.f * quarter, SIDE), quarter)
@@ -103,14 +103,16 @@
     c_val.wait()
     add_blocks(place, q_blocks, place.n_f // 2, counts, rows, cols, tokv, valv, acc)
     half = ahead.shape[0]
-    ahead[...] = acc[:half].astype(BF16)
-    behind[...] = acc[half:].astype(BF16)
+    stage[...] = acc[...].astype(BF16)
+    c_out = fetch((stage.at[:half], ahead, sems.at[5]), (stage.at[half:], behind, sems.at[6]))
     c_cot.wait()
     c_right.wait()
     full[...] = lax.dot_general(cotv[...], rightv[...], COLS, preferred_element_type=F32)
     back[...] = full[:, lanes(place.t)]
     for k, out in ((1, s1), (2, s2), (3, s3)):
         out[...] = full[:, lanes(lax.rem(place.t + k, place.n_t))].astype(BF16)
+    for copy in c_out:
+        copy.wait()
 
 
 def total_kernel(own, g1, g2, g3, *outs):
@@ -263,9 +265,12 @@
     ).astype(BF16)
 
 
-def stack_kernel(a, b, out):
-    out[: a.shape[0]] = a[...]
-    out[a.shape[0] :] = b[...]
+def stack_kernel(*refs):
+    parts, out = refs[:-1], refs[-1]
+    row = 0
+    for part in parts:
+        out[row : row + part.shape[0]] = part[...]
+        row += part.shape[0]
 
 
 def pass_kernel(p1, p3, from_behind, from_ahead, ahead, behind):
@@ -274,6 +279,15 @@
     ahead[half:] = p1[half:]
     behind[:half] = p3[:half]
     behind[half:] = (p3[half:].astype(F32) + from_ahead[...].astype(F32)).astype(BF16)
+
+
+def pair_kernel(own, behind, ahead, first, rest):
+    n = own.shape[0]
+    first[:n] = own[...]
+    first[n : 2 * n] = behind[...]
+    cut = first.shape[0] - 2 * n
+    first[2 * n :] = ahead[:cut]
+    rest[...] = ahead[cut:]
 
 
 def low_kernel(place, q_blocks, counts, rows, cols, tok, vals, g0, g1, g2, g3, right, out):
@@ -302,27 +316,25 @@
     order = (t, near_t, far_t, place.n_t - 1 - near_t)
     n = len(refs) // 2
     for core, mine in ((place.core, refs[:n]), (1 - place.core, refs[n:])):
-        own, behind, ahead, last = mine
+        first, rest, last = mine
         half = last.shape[0] // 2
-        last_behind, last_ahead = last.at[:half], last.at[half:]
-        for j, whole in ((0, own), (-1, behind), (1, ahead), (2, None)):
+        behind, ahead = first.at[2 * half : 4 * half], first.at[4 * half :]
+        cut = ahead.shape[0]
+        for j, segments in (
+            (0, ((0, first),)),
+            (-1, ((0, behind),)),
+            (1, ((0, ahead), (cut, rest))),
+            (2, ((0, last),)),
+        ):
             at = lax.rem(place.chip + j + place.chips, place.chips) * 2 + core
 
             def copy(dst, where, lo, hi):
-                cuts = [lo, hi] if whole is not None or not lo < half < hi else [lo, half, hi]
-                for a, b in zip(cuts, cuts[1:]):
-                    if whole is not None:
-                        piece = whole[a:b]
-                    elif a < half:
-                        piece = last_behind[a:b]
-                    else:
-                        piece = last_ahead[a - half : b - half]
-                    start = where[0] * (hi - lo) + (a - lo)
-                    rows = pl.ds(pl.multiple_of(start, 16), b - a)
-                    if where[1] is None:
-                        dst[rows, :] = piece
-                    else:
-                        dst[rows, where[1]] = piece
+                base, src = [s for s in segments if s[0] <= lo][-1]
+                rows = span(where[0], hi - lo)
+                if where[1] is None:
+                    dst[rows, :] = src[lo - base : hi - base]
+                else:
+                    dst[rows, where[1]] = src[lo - base : hi - base]
 
             for k in range(place.n_t):
                 copy(left, (at, lanes(order[k])), k * n_l, (k + 1) * n_l)
@@ -385,9 +397,11 @@
             vm((maxb, SIDE, SIDE), BF16),
             vm((tok_rows, rank_size), F32),
             vm((tok_rows, quarter), F32),
-            dma((5,)),
+            vm((tok_rows, quarter), BF16),
+            dma((7,)),
         ],
         mib=52,
+        hbm_outs=2,
     )
     rank_in = over(n_f, lambda k: shift(rank_low, "fsdp", n_f, k))
     back_in = [shift(x, "tensor", n_t, k + 1) for k, x in enumerate(back_out)]
@@ -491,6 +505,18 @@
         stack_kernel, (shape((2 * n_l, SIDE), BF16),), vmem=(left, left_near), after=(step,)
     )
     left_far = lax.ppermute(left_pair, "tensor", [(i, n_t - 1 - i) for i in range(n_t)])
+    n_msg = n_t * n_l + n_rest
+    message, step = call(
+        chunk_kernel,
+        (shape((n_msg, SIDE), BF16),),
+        vmem=(own, c_from_behind, c_from_ahead, c_last_behind, c_last_ahead, left_pair, left_far),
+        after=(step,),
+    )
+
+    m_behind = chip_shift(message, n_d, 1)
+    m_ahead = chip_shift(message, n_d, -1)
+    m_last_behind = chip_shift(m_behind[: n_msg // 2], n_d, 1)
+    m_last_ahead = chip_shift(m_ahead[n_msg // 2 :], n_d, -1)
     low, step = call(
         bind(low_kernel, q_blocks),
         (shape((tok_rows, quarter), F32),),
@@ -499,19 +525,18 @@
         after=(step,),
         mib=20,
     )
-    n_msg = n_t * n_l + n_rest
-    message, step = call(
-        chunk_kernel,
+    m_last, step = call(
+        stack_kernel,
         (shape((n_msg, SIDE), BF16),),
-        vmem=(own, c_from_behind, c_from_ahead, c_last_behind, c_last_ahead, left_pair, left_far),
-        after=(step,),
-    )
-
-    m_behind = chip_shift(message, n_d, 1)
-    m_ahead = chip_shift(message, n_d, -1)
-    m_last_behind = chip_shift(m_behind[: n_msg // 2], n_d, 1)
-    m_last_ahead = chip_shift(m_ahead[n_msg // 2 :], n_d, -1)
-    ours = (message, m_behind, m_ahead, jnp.concatenate([m_last_behind, m_last_ahead], axis=0))
+        vmem=(m_last_behind, m_last_ahead),
+        after=(step,),
+    )
+    first, rest, _ = call(
+        pair_kernel,
+        (shape((2 * n_msg + 3 * n_l, SIDE), BF16), shape((n_msg - 3 * n_l, SIDE), BF16)),
+        vmem=(message, m_behind, m_ahead),
+    )
+    ours = (first, rest, m_last)
     partner = [core_swap(x, n_d) for x in ours]
 
     out_left, out_right, out_blocks, step = call(

time: 132 us -> 129 us (0.977); the launches traced: 132 us -> 130 us
  starting transfers between devices: 60.5 us -> 48.9 us
  Pallas kernels: 39.4 us -> 46.2 us
  waiting for transfers between devices: 26.3 us -> 29.6 us
    pallas_call x14 -> x16, Pallas kernels: 38.1 us -> 44.9 us  [call(): pl.pallas_call(body, out_shape=(*outs, shape((1,), jnp.int32)), in_specs=...]
    ppermute x16, waiting for transfers between devices: 8.8 us -> 2.09 us  [shift(): return lax.ppermute(x, axis, [(i, (i + k) % n) for i in range(n)])]
    ppermute x9, waiting for transfers between devices: 15 us -> 21.2 us  [chip_shift(): return lax.ppermute(x, 'dp', perm)]
    ppermute x16, starting transfers between devices: 32.4 us -> 26.5 us  [shift(): return lax.ppermute(x, axis, [(i, (i + k) % n) for i in range(n)])]
    ppermute x1, starting transfers between devices: 3.94 us -> 0.09 us  [per_device(): lax.ppermute(left_pair, 'tensor', [(i, n_t - 1 - i) for i in range(n_t)])]
    ppermute x1, waiting for transfers between devices: 0.01 us -> 3.5 us  [per_device(): lax.ppermute(left_pair, 'tensor', [(i, n_t - 1 - i) for i in range(n_t)])]
    ppermute x7 -> x6, starting transfers between devices: 10.3 us -> 9.63 us  [core_swap(): return lax.ppermute(x, 'dp', [(i, i ^ 1) for i in range(n_data)])]
    unnamed x29 -> x24, local copies, waits for them, and re-layouts: 4.08 us -> 4.05 us
  transfers between devices with their start and end apart: 34 -> 33, of which waited for: 8 -> 9; matrix products, arithmetic and copies ran while one was open for 0% -> 0% of each run, Pallas kernels for 22% -> 28%
where the time goes in v2:
time: 129 us; the launch traced here: 130 us
  starting transfers between devices  48.9 us (38%)
  Pallas kernels  46.2 us (36%)
  waiting for transfers between devices  29.6 us (23%)
  local copies, waits for them, and re-layouts  4.1 us (3%)
    pallas_call x16, Pallas kernels, call(): pl.pallas_call(body, out_shape=(*outs, shape((1,), jnp.int32)), in_specs=...  44.9 us
    ppermute x16, starting transfers between devices, shift(): return lax.ppermute(x, axis, [(i, (i + k) % n) for i in range(n)])  26.5 us
    ppermute x9, waiting for transfers between devices, chip_shift(): return lax.ppermute(x, 'dp', perm)  21.2 us
    ppermute x9, starting transfers between devices, chip_shift(): return lax.ppermute(x, 'dp', perm)  12.6 us
    ppermute x6, starting transfers between devices, core_swap(): return lax.ppermute(x, 'dp', [(i, i ^ 1) for i in range(n_data)])  9.63 us
    unnamed x24, local copies, waits for them, and re-layouts  4.05 us
    ppermute x1, waiting for transfers between devices, per_device(): lax.ppermute(left_pair, 'tensor', [(i, n_t - 1 - i) for i in range(n_t)])  3.5 us
  transfers between devices with their start and end apart: 33, of which 9 were waited for; matrix products, arithmetic and copies ran while one was open for 0% of the time, Pallas kernels for 28%

profile of v2, /device:TPU:1, one launch (start us, length us, event | category | flops | bytes accessed | tf_op | source)
XLA Modules:
  0.0 130.0 jit_solution(8313449487110808703)
XLA Ops:
  2.9 6.8 %shard_map.111 = (f32[640,128]{1,0:T(8,128)S(1)}, bf16[640,128]{1,0:T(8,128)(2,1)S(1)}, f32[640,128]{1,0:T(8,128)S(1)}, bf16[640,128]{1,0:T(8,128)(2,1)S(1)}, bf...) custom-call(s32[16]{0:T(128)S(1)} %copy-done.6, ...), custom_call_target="tpu_custom_call" | custom-call | tf_op jit(solution)/shard_map/pallas_call | solution.py:38
  9.7 2.7 %collective-permute-start = (bf16[640,128]{1,0:T(8,128)(2,1)S(1)}, bf16[640,128]{1,0:T(8,128)(2,1)S(1)}, u32[]{:S(2)}, u32[]{:S(2)}) collective-permute-start(bf16[640,128]{1,0:T(8,128)(2,1)S(1)} %get-tuple-element.59), channel_id=1, source_target_pairs={{0,4},{4,8},{8,12},{12,0},{1,5},{5,9},{9,13},{13,1},{2,6},{6,10},{... | collective-permute-start | bytes 491528 | tf_op jit(solution)/shard_map/ppermute | solution.py:349
  12.4 3.7 %collective-permute-start.1 = (bf16[640,128]{1,0:T(8,128)(2,1)S(1)}, bf16[640,128]{1,0:T(8,128)(2,1)S(1)}, u32[]{:S(2)}, u32[]{:S(2)}) collective-permute-start(bf16[640,128]{1,0:T(8,128)(2,1)S(1)} %get-tuple-element.59), channel_id=1, source_target_pairs={{0,8},{4,12},{8,0},{12,4},{1,9},{5,13},{9,1},{13,5},{2,10},{6,14},... | collective-permute-start | bytes 491528 | tf_op jit(solution)/shard_map/ppermute | solution.py:349
  17.1 3.5 %collective-permute-start.7 = (bf16[640,128]{1,0:T(8,128)(2,1)S(1)}, bf16[640,128]{1,0:T(8,128)(2,1)S(1)}, u32[]{:S(2)}, u32[]{:S(2)}) collective-permute-start(bf16[640,128]{1,0:T(8,128)(2,1)S(1)} %get-tuple-element.64), channel_id=1, source_target_pairs={{0,2},{1,3},{2,0},{3,1},{4,6},{5,7},{6,4},{7,5},{8,10},{9,11},{10,... | collective-permute-start | bytes 491528 | tf_op jit(solution)/shard_map/ppermute | solution.py:349
  21.3 1.9 %collective-permute-done.1.refs_2_ = bf16[640,128]{1,0:T(8,128)(2,1)S(1)} collective-permute-done((bf16[640,128]{1,0:T(8,128)(2,1)S(1)}, bf16[640,128]{1,0:T(8,128)(2,1)S(1)}, u32[]{:S(2)}, u32[]{:S(2)}) %collective-permute-start.1) | collective-permute-done | bytes 163872 | tf_op jit(solution)/shard_map/ppermute | solution.py:349
  25.3 2.3 %collective-permute-start.4 = (bf16[640,128]{1,0:T(8,128)(2,1)S(1)}, bf16[640,128]{1,0:T(8,128)(2,1)S(1)}, u32[]{:S(2)}, u32[]{:S(2)}) collective-permute-start(bf16[640,128]{1,0:T(8,128)(2,1)S(1)} %get-tuple-element.61.refs_2_.refs_5_), channel_id=1, source_target_pairs={{0,2},{1,3},{2,0},{3,1},{4,6},{5,7},{6,4},{7,5},{8,10},{9,11},{10,... | collective-permute-start | bytes 491528 | tf_op jit(solution)/shard_map/ppermute | solution.py:349
  31.8 2.1 %collective-permute-start.10 = (bf16[640,128]{1,0:T(8,128)(2,1)S(1)}, bf16[640,128]{1,0:T(8,128)(2,1)S(1)}, u32[]{:S(2)}, u32[]{:S(2)}) collective-permute-start(bf16[640,128]{1,0:T(8,128)(2,1)S(1)} %get-tuple-element.68), channel_id=1, source_target_pairs={{0,8},{4,12},{8,0},{12,4},{1,9},{5,13},{9,1},{13,5},{2,10},{6,14},... | collective-permute-start | bytes 491528 | tf_op jit(solution)/shard_map/ppermute | solution.py:349
  36.9 5.9 %shard_map.114 = (f32[4,512,128]{2,1,0:T(8,128)S(1)}, bf16[4,512,128]{2,1,0:T(8,128)(2,1)S(1)}, s32[1]{0:T(128)}) custom-call(s32[16]{0:T(128)S(1)} %copy-done.6, s32[32]{0:T(128)S(1)} %copy-done.7, s32[32]{0:T(128)S(1)} %copy-done.8, bf16[640,2048]{1,0:T(8,128)(2,1)S(1)} %copy-done, bf16[640,7168]{1,0:T(8,128)(2,1)S(1)} %bitcast.5, s32[1]{0:T(128)} %get-tuple-element.69.refs_5_), custom_call_target="tpu_custom_call" | custom-call | tf_op jit(solution)/shard_map/pallas_call | solution.py:38
  44.6 2.4 %collective-permute-start.19 = (bf16[320,1792]{1,0:T(8,128)(2,1)S(1)}, bf16[320,1792]{1,0:T(8,128)(2,1)S(1)}, u32[]{:S(2)}, u32[]{:S(2)}) collective-permute-start(bf16[320,1792]{1,0:T(8,128)(2,1)S(1)} %get-tuple-element.90), channel_id=1, source_target_pairs={{0,12},{4,0},{8,4},{12,8},{1,13},{5,1},{9,5},{13,9},{2,14},{6,2},{... | collective-permute-start | bytes 3440648 | tf_op jit(solution)/shard_map/ppermute | solution.py:349
  47.0 4.8 %shard_map.116 = (f32[4,1664,128]{2,1,0:T(8,128)S(1)}, bf16[2224,128]{1,0:T(8,128)(2,1)S(1)}, bf16[2224,128]{1,0:T(8,128)(2,1)S(1)}, bf16[2208,128]{1,0:T(8,128)(2,1)S(1)}, s32[1]{0:T(128)}) custom-call(bf16[640,2048]{1,0:T(8,128)(2,1)S(1)} %copy-done.1, bf16[640,7168]{1,0:T(8,128)(2,1)} %refs_1_.7, bf16[640,128]{1,0:T(8,128)(2,1)S(1)} %get-tuple-element.61.refs_2_.refs_5_, ...), custom_call_target="tpu_custom_call" | custom-call | tf_op jit(solution)/shard_map/pallas_call | solution.py:38
  51.8 4.6 %collective-permute-start.12 = (bf16[2224,128]{1,0:T(8,128)(2,1)S(1)}, bf16[2224,128]{1,0:T(8,128)(2,1)S(1)}, u32[]{:S(2)}, u32[]{:S(2)}) collective-permute-start(bf16[2224,128]{1,0:T(8,128)(2,1)S(1)} %get-tuple-element.77), channel_id=1, source_target_pairs={{0,16},{16,0},{32,48},{48,32},{64,80},{80,64},{96,112},{112,96},{1... | collective-permute-start | bytes 1708040 | tf_op jit(solution)/shard_map/ppermute | solution.py:359
  56.8 5.5 %shard_map.117 = (bf16[640,1792]{1,0:T(8,128)(2,1)S(1)}, bf16[640,1792]{1,0:T(8,128)(2,1)S(1)}, s32[1]{0:T(128)}) custom-call(s32[16]{0:T(128)S(1)} %copy-done.6, s32[32]{0:T(128)S(1)} %copy-done.7, s32[32]{0:T(128)S(1)} %copy-done.8, bf16[640,2048]{1,0:T(8,128)(2,1)S(1)} %copy-done.1, bf16[32,128,128]{2,1,0:T(8,128)(2,1)S(1)} %copy-done.2, ...), custom_call_target="tpu_custom_call" | custom-call | tf_op jit(solution)/shard_map/pallas_call | solution.py:38
  69.8 2.6 %collective-permute-start.25 = (bf16[640,1792]{1,0:T(8,128)(2,1)S(1)}, bf16[640,1792]{1,0:T(8,128)(2,1)S(1)}, u32[]{:S(2)}, u32[]{:S(2)}) collective-permute-start(bf16[640,1792]{1,0:T(8,128)(2,1)S(1)} %get-tuple-element.102), channel_id=1, source_target_pairs={{0,12},{4,0},{8,4},{12,8},{1,13},{5,1},{9,5},{13,9},{2,14},{6,2},{... | collective-permute-start | bytes 6881288 | tf_op jit(solution)/shard_map/ppermute | solution.py:349
  72.4 6.6 %collective-permute-done.17.refs_4_ = bf16[256,128]{1,0:T(8,128)(2,1)S(1)} collective-permute-done((bf16[256,128]{1,0:T(8,128)(2,1)S(1)}, bf16[256,128]{1,0:T(8,128)(2,1)S(1)}, u32[]{:S(2)}, u32[]{:S(2)}) %collective-permute-start.17) | collective-permute-done | bytes 65568 | tf_op jit(solution)/shard_map/ppermute | solution.py:355
  80.6 2.4 %collective-permute-start.21 = (bf16[704,128]{1,0:T(8,128)(2,1)S(1)}, bf16[704,128]{1,0:T(8,128)(2,1)S(1)}, u32[]{:S(2)}, u32[]{:S(2)}) collective-permute-start(bf16[704,128]{1,0:T(8,128)(2,1)S(1)} %get-tuple-element.94), channel_id=1, source_target_pairs={{0,96},{16,112},{32,0},{48,16},{64,32},{80,48},{96,64},{112,80},{1... | collective-permute-start | bytes 540680 | tf_op jit(solution)/shard_map/ppermute | solution.py:355
  86.8 3.5 %collective-permute-done.23.refs_6_ = bf16[512,128]{1,0:T(8,128)(2,1)S(1)} collective-permute-done((bf16[512,128]{1,0:T(8,128)(2,1)S(1)}, bf16[512,128]{1,0:T(8,128)(2,1)S(1)}, u32[]{:S(2)}, u32[]{:S(2)}) %collective-permute-start.23) | collective-permute-done | bytes 131104 | tf_op jit(solution)/shard_map/ppermute | solution.py:507
  91.9 2.4 %collective-permute-start.27 = (bf16[2432,128]{1,0:T(8,128)(2,1)S(1)}, bf16[2432,128]{1,0:T(8,128)(2,1)S(1)}, u32[]{:S(2)}, u32[]{:S(2)}) collective-permute-start(bf16[2432,128]{1,0:T(8,128)(2,1)S(1)} %get-tuple-element.104.refs_0_), channel_id=1, source_target_pairs={{0,96},{16,112},{32,0},{48,16},{64,32},{80,48},{96,64},{112,80},{1... | collective-permute-start | bytes 1867784 | tf_op jit(solution)/shard_map/ppermute | solution.py:355
  94.3 11.5 %collective-permute-done.26.refs_1_ = bf16[2432,128]{1,0:T(8,128)(2,1)S(1)} collective-permute-done((bf16[2432,128]{1,0:T(8,128)(2,1)S(1)}, bf16[2432,128]{1,0:T(8,128)(2,1)S(1)}, u32[]{:S(2)}, u32[]{:S(2)}) %collective-permute-start.26) | collective-permute-done | bytes 622624 | tf_op jit(solution)/shard_map/ppermute | solution.py:355
  106.4 3.6 %collective-permute-start.30 = (bf16[5632,128]{1,0:T(8,128)(2,1)S(1)}, bf16[5632,128]{1,0:T(8,128)(2,1)S(1)}, u32[]{:S(2)}, u32[]{:S(2)}) collective-permute-start(bf16[5632,128]{1,0:T(8,128)(2,1)S(1)} %get-tuple-element.105.refs_0_), channel_id=1, source_target_pairs={{0,16},{16,0},{32,48},{48,32},{64,80},{80,64},{96,112},{112,96},{1... | collective-permute-start | bytes 4325384 | tf_op jit(solution)/shard_map/ppermute | solution.py:359
  110.1 2.7 %collective-permute-start.29 = (bf16[1216,128]{1,0:T(8,128)(2,1)S(1)}, bf16[1216,128]{1,0:T(8,128)(2,1)S(1)}, u32[]{:S(2)}, u32[]{:S(2)}) collective-permute-start(bf16[1216,128]{1,0:T(8,128)(2,1)S(1)} %slice.9), channel_id=1, source_target_pairs={{0,96},{16,112},{32,0},{48,16},{64,32},{80,48},{96,64},{112,80},{1... | collective-permute-start | bytes 933896 | tf_op jit(solution)/shard_map/ppermute | solution.py:355
  112.9 6.1 %shard_map.123 = (f32[640,1792]{1,0:T(8,128)S(1)}, s32[1]{0:T(128)}) custom-call(s32[16]{0:T(128)S(1)} %copy-done.6, s32[32]{0:T(128)S(1)} %copy-done.7, s32[32]{0:T(128)S(1)} %copy-done.8, bf16[640,2048]{1,0:T(8,128)(2,1)S(1)} %copy-done.1, bf16[32,128,128]{2,1,0:T(8,128)(2,1)S(1)} %copy-done.2, bf16[640,128]{1,0:T(8,128)(2,1)S(1)} %get-tuple-element.61.refs_2_.refs_5_, ...), custom_call_target="tpu_custom_call" | custom-call | tf_op jit(solution)/shard_map/pallas_call | solution.py:38
  122.5 2.2 %collective-permute-done.31.refs_4_ = bf16[1664,128]{1,0:T(8,128)(2,1)S(1)} collective-permute-done((bf16[1664,128]{1,0:T(8,128)(2,1)S(1)}, bf16[1664,128]{1,0:T(8,128)(2,1)S(1)}, u32[]{:S(2)}, u32[]{:S(2)}) %collective-permute-start.31) | collective-permute-done | bytes 426016 | tf_op jit(solution)/shard_map/ppermute | solution.py:359
  124.7 3.0 %shard_map.127 = (bf16[2048,512]{1,0:T(8,128)(2,1)}, bf16[512,1792]{1,0:T(8,128)(2,1)}, bf16[4096,128]{1,0:T(8,128)(2,1)}, s32[1]{0:T(128)}) custom-call(bf16[5632,128]{1,0:T(8,128)(2,1)S(1)} %get-tuple-element.105.refs_0_, bf16[1664,128]{1,0:T(8,128)(2,1)S(1)} %get-tuple-element.106.refs_1_, bf16[2432,128]{1,0:T(8,128)(2,1)S(1)} %get-tuple-element.108.refs_2_, ...), custom_call_target="tpu_custom_call" | custom-call | tf_op jit(solution)/shard_map/pallas_call | solution.py:38
  127.7 2.1 %shard_map.124 = (bf16[640,1792]{1,0:T(8,128)(2,1)}, s32[1]{0:T(128)}) custom-call(f32[640,1792]{1,0:T(8,128)S(1)} %get-tuple-element.100.refs_0_, bf16[640,1792]{1,0:T(8,128)(2,1)S(1)} %collective-permute-done.24.refs_1_, bf16[640,1792]{1,0:T(8,128)(2,1)S(1)} %collective-permute-done.25.refs_2_), custom_call_target="tpu_custom_call" | custom-call | tf_op jit(solution)/shard_map/pallas_call | solution.py:38
  (86 shorter events, 34.0 us)
Async XLA Ops:
  9.7 10.8 %collective-permute-start = (bf16[640,128]{1,0:T(8,128)(2,1)S(1)}, bf16[640,128]{1,0:T(8,128)(2,1)S(1)}, u32[]{:S(2)}, u32[]{:S(2)}) collective-permute-start(bf16[640,128]{1,0:T(8,128)(2,1)S(1)} %get-tuple-element.59), channel_id=1, source_target_pairs={{0,4},{4,8},{8,12},{12,0},{1,5},{5,9},{9,13},{13,1},{2,6},{6,10},{... | collective-permute-start | bytes 491528 | tf_op jit(solution)/shard_map/ppermute | solution.py:349
  12.4 10.8 %collective-permute-start.1 = (bf16[640,128]{1,0:T(8,128)(2,1)S(1)}, bf16[640,128]{1,0:T(8,128)(2,1)S(1)}, u32[]{:S(2)}, u32[]{:S(2)}) collective-permute-start(bf16[640,128]{1,0:T(8,128)(2,1)S(1)} %get-tuple-element.59), channel_id=1, source_target_pairs={{0,8},{4,12},{8,0},{12,4},{1,9},{5,13},{9,1},{13,5},{2,10},{6,14},... | collective-permute-start | bytes 491528 | tf_op jit(solution)/shard_map/ppermute | solution.py:349
  16.1 11.4 %collective-permute-start.6 = (bf16[640,128]{1,0:T(8,128)(2,1)S(1)}, bf16[640,128]{1,0:T(8,128)(2,1)S(1)}, u32[]{:S(2)}, u32[]{:S(2)}) collective-permute-start(bf16[640,128]{1,0:T(8,128)(2,1)S(1)} %get-tuple-element.63), channel_id=1, source_target_pairs={{0,1},{1,2},{2,3},{3,0},{4,5},{5,6},{6,7},{7,4},{8,9},{9,10},{10,1... | collective-permute-start | bytes 491528 | tf_op jit(solution)/shard_map/ppermute | solution.py:349
  17.1 11.9 %collective-permute-start.7 = (bf16[640,128]{1,0:T(8,128)(2,1)S(1)}, bf16[640,128]{1,0:T(8,128)(2,1)S(1)}, u32[]{:S(2)}, u32[]{:S(2)}) collective-permute-start(bf16[640,128]{1,0:T(8,128)(2,1)S(1)} %get-tuple-element.64), channel_id=1, source_target_pairs={{0,2},{1,3},{2,0},{3,1},{4,6},{5,7},{6,4},{7,5},{8,10},{9,11},{10,... | collective-permute-start | bytes 491528 | tf_op jit(solution)/shard_map/ppermute | solution.py:349
  20.6 8.4 %collective-permute-start.8 = (bf16[640,128]{1,0:T(8,128)(2,1)S(1)}, bf16[640,128]{1,0:T(8,128)(2,1)S(1)}, u32[]{:S(2)}, u32[]{:S(2)}) collective-permute-start(bf16[640,128]{1,0:T(8,128)(2,1)S(1)} %get-tuple-element.65), channel_id=1, source_target_pairs={{0,3},{1,0},{2,1},{3,2},{4,7},{5,4},{6,5},{7,6},{8,11},{9,8},{10,9... | collective-permute-start | bytes 491528 | tf_op jit(solution)/shard_map/ppermute | solution.py:349
  24.4 9.5 %collective-permute-start.3 = (bf16[640,128]{1,0:T(8,128)(2,1)S(1)}, bf16[640,128]{1,0:T(8,128)(2,1)S(1)}, u32[]{:S(2)}, u32[]{:S(2)}) collective-permute-start(bf16[640,128]{1,0:T(8,128)(2,1)S(1)} %get-tuple-element.61.refs_2_.refs_5_), channel_id=1, source_target_pairs={{0,1},{1,2},{2,3},{3,0},{4,5},{5,6},{6,7},{7,4},{8,9},{9,10},{10,1... | collective-permute-start | bytes 491528 | tf_op jit(solution)/shard_map/ppermute | solution.py:349
  25.3 17.5 %collective-permute-start.4 = (bf16[640,128]{1,0:T(8,128)(2,1)S(1)}, bf16[640,128]{1,0:T(8,128)(2,1)S(1)}, u32[]{:S(2)}, u32[]{:S(2)}) collective-permute-start(bf16[640,128]{1,0:T(8,128)(2,1)S(1)} %get-tuple-element.61.refs_2_.refs_5_), channel_id=1, source_target_pairs={{0,2},{1,3},{2,0},{3,1},{4,6},{5,7},{6,4},{7,5},{8,10},{9,11},{10,... | collective-permute-start | bytes 491528 | tf_op jit(solution)/shard_map/ppermute | solution.py:349
  27.6 15.3 %collective-permute-start.5 = (bf16[640,128]{1,0:T(8,128)(2,1)S(1)}, bf16[640,128]{1,0:T(8,128)(2,1)S(1)}, u32[]{:S(2)}, u32[]{:S(2)}) collective-permute-start(bf16[640,128]{1,0:T(8,128)(2,1)S(1)} %get-tuple-element.61.refs_2_.refs_5_), channel_id=1, source_target_pairs={{0,3},{1,0},{2,1},{3,2},{4,7},{5,4},{6,5},{7,6},{8,11},{9,8},{10,9... | collective-permute-start | bytes 491528 | tf_op jit(solution)/shard_map/ppermute | solution.py:349
  30.2 12.7 %collective-permute-start.9 = (bf16[640,128]{1,0:T(8,128)(2,1)S(1)}, bf16[640,128]{1,0:T(8,128)(2,1)S(1)}, u32[]{:S(2)}, u32[]{:S(2)}) collective-permute-start(bf16[640,128]{1,0:T(8,128)(2,1)S(1)} %get-tuple-element.68), channel_id=1, source_target_pairs={{0,4},{4,8},{8,12},{12,0},{1,5},{5,9},{9,13},{13,1},{2,6},{6,10},{... | collective-permute-start | bytes 491528 | tf_op jit(solution)/shard_map/ppermute | solution.py:349
  31.8 11.0 %collective-permute-start.10 = (bf16[640,128]{1,0:T(8,128)(2,1)S(1)}, bf16[640,128]{1,0:T(8,128)(2,1)S(1)}, u32[]{:S(2)}, u32[]{:S(2)}) collective-permute-start(bf16[640,128]{1,0:T(8,128)(2,1)S(1)} %get-tuple-element.68), channel_id=1, source_target_pairs={{0,8},{4,12},{8,0},{12,4},{1,9},{5,13},{9,1},{13,5},{2,10},{6,14},... | collective-permute-start | bytes 491528 | tf_op jit(solution)/shard_map/ppermute | solution.py:349
  33.9 8.9 %collective-permute-start.11 = (bf16[640,128]{1,0:T(8,128)(2,1)S(1)}, bf16[640,128]{1,0:T(8,128)(2,1)S(1)}, u32[]{:S(2)}, u32[]{:S(2)}) collective-permute-start(bf16[640,128]{1,0:T(8,128)(2,1)S(1)} %get-tuple-element.68), channel_id=1, source_target_pairs={{0,12},{4,0},{8,4},{12,8},{1,13},{5,1},{9,5},{13,9},{2,14},{6,2},{... | collective-permute-start | bytes 491528 | tf_op jit(solution)/shard_map/ppermute | solution.py:349
  44.2 24.1 %collective-permute-start.18 = (bf16[320,1792]{1,0:T(8,128)(2,1)S(1)}, bf16[320,1792]{1,0:T(8,128)(2,1)S(1)}, u32[]{:S(2)}, u32[]{:S(2)}) collective-permute-start(bf16[320,1792]{1,0:T(8,128)(2,1)S(1)} %get-tuple-element.89), channel_id=1, source_target_pairs={{0,4},{4,8},{8,12},{12,0},{1,5},{5,9},{9,13},{13,1},{2,6},{6,10},{... | collective-permute-start | bytes 3440648 | tf_op jit(solution)/shard_map/ppermute | solution.py:349
  44.6 23.8 %collective-permute-start.19 = (bf16[320,1792]{1,0:T(8,128)(2,1)S(1)}, bf16[320,1792]{1,0:T(8,128)(2,1)S(1)}, u32[]{:S(2)}, u32[]{:S(2)}) collective-permute-start(bf16[320,1792]{1,0:T(8,128)(2,1)S(1)} %get-tuple-element.90), channel_id=1, source_target_pairs={{0,12},{4,0},{8,4},{12,8},{1,13},{5,1},{9,5},{13,9},{2,14},{6,2},{... | collective-permute-start | bytes 3440648 | tf_op jit(solution)/shard_map/ppermute | solution.py:349
  51.8 10.7 %collective-permute-start.12 = (bf16[2224,128]{1,0:T(8,128)(2,1)S(1)}, bf16[2224,128]{1,0:T(8,128)(2,1)S(1)}, u32[]{:S(2)}, u32[]{:S(2)}) collective-permute-start(bf16[2224,128]{1,0:T(8,128)(2,1)S(1)} %get-tuple-element.77), channel_id=1, source_target_pairs={{0,16},{16,0},{32,48},{48,32},{64,80},{80,64},{96,112},{112,96},{1... | collective-permute-start | bytes 1708040 | tf_op jit(solution)/shard_map/ppermute | solution.py:359
  63.9 15.0 %collective-permute-start.15 = (bf16[1664,128]{1,0:T(8,128)(2,1)S(1)}, bf16[1664,128]{1,0:T(8,128)(2,1)S(1)}, u32[]{:S(2)}, u32[]{:S(2)}) collective-permute-start(bf16[1664,128]{1,0:T(8,128)(2,1)S(1)} %get-tuple-element.83), channel_id=1, source_target_pairs={{0,32},{16,48},{32,64},{48,80},{64,96},{80,112},{96,0},{112,16},{1... | collective-permute-start | bytes 1277960 | tf_op jit(solution)/shard_map/ppermute | solution.py:355
  65.2 13.7 %collective-permute-start.16 = (bf16[1664,128]{1,0:T(8,128)(2,1)S(1)}, bf16[1664,128]{1,0:T(8,128)(2,1)S(1)}, u32[]{:S(2)}, u32[]{:S(2)}) collective-permute-start(bf16[1664,128]{1,0:T(8,128)(2,1)S(1)} %get-tuple-element.84), channel_id=1, source_target_pairs={{0,96},{16,112},{32,0},{48,16},{64,32},{80,48},{96,64},{112,80},{1... | collective-permute-start | bytes 1277960 | tf_op jit(solution)/shard_map/ppermute | solution.py:355
  66.7 12.3 %collective-permute-start.17 = (bf16[256,128]{1,0:T(8,128)(2,1)S(1)}, bf16[256,128]{1,0:T(8,128)(2,1)S(1)}, u32[]{:S(2)}, u32[]{:S(2)}) collective-permute-start(bf16[256,128]{1,0:T(8,128)(2,1)S(1)} %get-tuple-element.86), channel_id=1, source_target_pairs={{0,64},{16,80},{32,96},{48,112},{64,0},{80,16},{96,32},{112,48},{1... | collective-permute-start | bytes 196616 | tf_op jit(solution)/shard_map/ppermute | solution.py:355
  69.6 58.1 %collective-permute-start.24 = (bf16[640,1792]{1,0:T(8,128)(2,1)S(1)}, bf16[640,1792]{1,0:T(8,128)(2,1)S(1)}, u32[]{:S(2)}, u32[]{:S(2)}) collective-permute-start(bf16[640,1792]{1,0:T(8,128)(2,1)S(1)} %get-tuple-element.101), channel_id=1, source_target_pairs={{0,4},{4,8},{8,12},{12,0},{1,5},{5,9},{9,13},{13,1},{2,6},{6,10},{... | collective-permute-start | bytes 6881288 | tf_op jit(solution)/shard_map/ppermute | solution.py:349
  69.8 57.9 %collective-permute-start.25 = (bf16[640,1792]{1,0:T(8,128)(2,1)S(1)}, bf16[640,1792]{1,0:T(8,128)(2,1)S(1)}, u32[]{:S(2)}, u32[]{:S(2)}) collective-permute-start(bf16[640,1792]{1,0:T(8,128)(2,1)S(1)} %get-tuple-element.102), channel_id=1, source_target_pairs={{0,12},{4,0},{8,4},{12,8},{1,13},{5,1},{9,5},{13,9},{2,14},{6,2},{... | collective-permute-start | bytes 6881288 | tf_op jit(solution)/shard_map/ppermute | solution.py:349
  91.6 14.2 %collective-permute-start.26 = (bf16[2432,128]{1,0:T(8,128)(2,1)S(1)}, bf16[2432,128]{1,0:T(8,128)(2,1)S(1)}, u32[]{:S(2)}, u32[]{:S(2)}) collective-permute-start(bf16[2432,128]{1,0:T(8,128)(2,1)S(1)} %get-tuple-element.104.refs_0_), channel_id=1, source_target_pairs={{0,32},{16,48},{32,64},{48,80},{64,96},{80,112},{96,0},{112,16},{1... | collective-permute-start | bytes 1867784 | tf_op jit(solution)/shard_map/ppermute | solution.py:355
  91.9 13.9 %collective-permute-start.27 = (bf16[2432,128]{1,0:T(8,128)(2,1)S(1)}, bf16[2432,128]{1,0:T(8,128)(2,1)S(1)}, u32[]{:S(2)}, u32[]{:S(2)}) collective-permute-start(bf16[2432,128]{1,0:T(8,128)(2,1)S(1)} %get-tuple-element.104.refs_0_), channel_id=1, source_target_pairs={{0,96},{16,112},{32,0},{48,16},{64,32},{80,48},{96,64},{112,80},{1... | collective-permute-start | bytes 1867784 | tf_op jit(solution)/shard_map/ppermute | solution.py:355
  106.4 18.3 %collective-permute-start.30 = (bf16[5632,128]{1,0:T(8,128)(2,1)S(1)}, bf16[5632,128]{1,0:T(8,128)(2,1)S(1)}, u32[]{:S(2)}, u32[]{:S(2)}) collective-permute-start(bf16[5632,128]{1,0:T(8,128)(2,1)S(1)} %get-tuple-element.105.refs_0_), channel_id=1, source_target_pairs={{0,16},{16,0},{32,48},{48,32},{64,80},{80,64},{96,112},{112,96},{1... | collective-permute-start | bytes 4325384 | tf_op jit(solution)/shard_map/ppermute | solution.py:359
  110.0 10.3 %collective-permute-start.28 = (bf16[1216,128]{1,0:T(8,128)(2,1)S(1)}, bf16[1216,128]{1,0:T(8,128)(2,1)S(1)}, u32[]{:S(2)}, u32[]{:S(2)}) collective-permute-start(bf16[1216,128]{1,0:T(8,128)(2,1)S(1)} %slice.8), channel_id=1, source_target_pairs={{0,32},{16,48},{32,64},{48,80},{64,96},{80,112},{96,0},{112,16},{1... | collective-permute-start | bytes 933896 | tf_op jit(solution)/shard_map/ppermute | solution.py:355
  110.1 10.2 %collective-permute-start.29 = (bf16[1216,128]{1,0:T(8,128)(2,1)S(1)}, bf16[1216,128]{1,0:T(8,128)(2,1)S(1)}, u32[]{:S(2)}, u32[]{:S(2)}) collective-permute-start(bf16[1216,128]{1,0:T(8,128)(2,1)S(1)} %slice.9), channel_id=1, source_target_pairs={{0,96},{16,112},{32,0},{48,16},{64,32},{80,48},{96,64},{112,80},{1... | collective-permute-start | bytes 933896 | tf_op jit(solution)/shard_map/ppermute | solution.py:355
  (21 other events, 196.5 us)

commit v3 on v2

--- a/solution.py
+++ b/solution.py
@@ -115,12 +115,6 @@
         copy.wait()
 
 
-def total_kernel(own, g1, g2, g3, *outs):
-    total = own[...] + g1[...].astype(F32) + g2[...].astype(F32) + g3[...].astype(F32)
-    for out in outs:
-        out[...] = total.astype(out.dtype)
-
-
 def residual_kernel(place, q_blocks, counts, rows, cols, tok, vals, p1, p3, acc):
     acc[...] = jnp.zeros_like(acc)
     n_f, f = place.n_f, place.f
@@ -142,7 +136,7 @@
     p3[...] = acc[1].astype(BF16)
 
 
-def blocks_kernel(place, counts, rows, cols, tok, cot, mine, theirs):
+def blocks_kernel(place, counts, rows, cols, tok, cot, _, mine, theirs):
     live = place.live(counts)
     per = mine.shape[1] // SIDE
 
@@ -299,12 +293,9 @@
     add_blocks(place, q_blocks, 0, counts, rows, cols, tok, vals, out)
 
 
-def finish_kernel(low, from_behind, from_ahead, out):
-    out[...] = (low[...] + from_behind[...].astype(F32) + from_ahead[...].astype(F32)).astype(BF16)
-
-
-def spread_kernel(place, *refs):
-    refs, (left, right, blocks) = refs[:-3], refs[-3:]
+def last_kernel(place, low, from_behind, from_ahead, *refs):
+    (mixed_out, left_out, right_out, blocks), (mixed, left, right, sems) = refs[-8:-4], refs[-4:]
+    refs = refs[:-8]
     n_l = left.shape[0] // place.n_d
     n_r = right.shape[0] // place.n_d
     n_b = blocks.shape[0] // place.n_d
@@ -314,35 +305,52 @@
     near_t = t + 1 - 2 * lax.rem(t, 2)
     far_t = place.n_t - 1 - t
     order = (t, near_t, far_t, place.n_t - 1 - near_t)
+    copies = []
+
+    def send(pair):
+        copies.extend(fetch((*pair, sems.at[len(copies)])))
+
+    chunks = []
     n = len(refs) // 2
-    for core, mine in ((place.core, refs[:n]), (1 - place.core, refs[n:])):
-        first, rest, last = mine
+    for core, (first, rest, last) in (
+        (place.core, refs[:n]),
+        (1 - place.core, refs[n:]),
+    ):
         half = last.shape[0] // 2
         behind, ahead = first.at[2 * half : 4 * half], first.at[4 * half :]
-        cut = ahead.shape[0]
         for j, segments in (
             (0, ((0, first),)),
             (-1, ((0, behind),)),
-            (1, ((0, ahead), (cut, rest))),
+            (1, ((0, ahead), (ahead.shape[0], rest))),
             (2, ((0, last),)),
         ):
             at = lax.rem(place.chip + j + place.chips, place.chips) * 2 + core
-
-            def copy(dst, where, lo, hi):
-                base, src = [s for s in segments if s[0] <= lo][-1]
-                rows = span(where[0], hi - lo)
-                if where[1] is None:
-                    dst[rows, :] = src[lo - base : hi - base]
-                else:
-                    dst[rows, where[1]] = src[lo - base : hi - base]
-
-            for k in range(place.n_t):
-                copy(left, (at, lanes(order[k])), k * n_l, (k + 1) * n_l)
-            for p in range(panels):
-                lo = n_left + p * n_r
-                copy(right, (at, pl.ds(p * SIDE, SIDE)), lo, lo + n_r)
-            lo = n_left + panels * n_r
-            copy(blocks, (at, None), lo, lo + n_b)
+            chunks.append((at, segments))
+
+    def piece(segments, lo, hi):
+        base, src = [s for s in segments if s[0] <= lo][-1]
+        return src.at[lo - base : hi - base]
+
+    base = n_left + panels * n_r
+    for at, segments in chunks:
+        send((piece(segments, base, base + n_b), blocks.at[span(at, n_b)]))
+    for at, segments in chunks:
+        for k in range(place.n_t):
+            left[span(at, n_l), lanes(order[k])] = piece(segments, k * n_l, (k + 1) * n_l)[...]
+    send((left, left_out))
+    for at, segments in chunks:
+        for p in range(panels):
+            lo = n_left + p * n_r
+            right[span(at, n_r), p * SIDE : (p + 1) * SIDE] = piece(segments, lo, lo + n_r)[...]
+    send((right, right_out))
+    size = mixed.shape[0] // 4
+    for i in range(4):
+        rows = pl.ds(i * size, size)
+        total = low[rows, :] + from_behind[rows, :].astype(F32) + from_ahead[rows, :].astype(F32)
+        mixed[rows, :] = total.astype(BF16)
+        send((mixed.at[rows], mixed_out.at[rows]))
+    for copy in copies:
+        copy.wait()
 
 
 def shift(x, axis, n, k):
@@ -406,11 +414,13 @@
     rank_in = over(n_f, lambda k: shift(rank_low, "fsdp", n_f, k))
     back_in = [shift(x, "tensor", n_t, k + 1) for k, x in enumerate(back_out)]
 
-    rank, step = call(total_kernel, (narrow,), vmem=(rank, *rank_in), after=(step,))
+    for x in rank_in:
+        rank = rank + x.astype(F32)
+    rank = rank.astype(BF16)
     ranks = [rank] + over(n_t, lambda k: shift(rank, "tensor", n_t, k))
-    back, back_low, step = call(
-        total_kernel, (wide, narrow), vmem=(back, *back_in), after=(step,)
-    )
+    for x in back_in:
+        back = back + x.astype(F32)
+    back_low = back.astype(BF16)
     backs = [back] + over(n_f, lambda k: shift(back_low, "fsdp", n_f, k))
 
     n_b = maxb // n_d * SIDE
@@ -418,7 +428,7 @@
         bind(blocks_kernel),
         (shape((chips, n_b, SIDE), F32), shape((chips, n_b, SIDE), BF16)),
         smem=lists,
-        vmem=(tokens, cotangent),
+        vmem=(tokens, cotangent, back_low),
         after=(step,),
         mib=20,
     )
@@ -539,18 +549,23 @@
     ours = (first, rest, m_last)
     partner = [core_swap(x, n_d) for x in ours]
 
-    out_left, out_right, out_blocks, step = call(
-        bind(spread_kernel),
+    mixed, out_left, out_right, out_blocks, _ = call(
+        bind(last_kernel),
         (
+            whole,
             shape((features, rank_size), BF16),
             shape((rank_size, quarter), BF16),
             shape((maxb * SIDE, SIDE), BF16),
         ),
-        vmem=(*ours, *partner),
-        mib=14,
-    )
-    mixed, _ = call(
-        finish_kernel, (whole,), vmem=(low, last_behind, last_ahead), mib=12
+        vmem=(low, last_behind, last_ahead, *ours, *partner),
+        scratch=[
+            vm((tok_rows, quarter), BF16),
+            vm((features, rank_size), BF16),
+            vm((rank_size, quarter), BF16),
+            dma((n_d + 6,)),
+        ],
+        mib=32,
+        hbm_outs=4,
     )
     return (
         mixed.reshape(tok_rows, 1, quarter),

time: 129 us -> 128 us (level); the launches traced: 130 us -> 127 us
  Pallas kernels: 46.2 us -> 38.9 us
  waiting for transfers between devices: 29.6 us -> 33.3 us
    ppermute x16, waiting for transfers between devices: 2.09 us -> 12.6 us  [shift(): return lax.ppermute(x, axis, [(i, (i + k) % n) for i in range(n)])]
    pallas_call x16 -> x13, Pallas kernels: 44.9 us -> 37.6 us  [call(): pl.pallas_call(body, out_shape=(*outs, shape((1,), jnp.int32)), in_specs=...]
    ppermute x9, waiting for transfers between devices: 21.2 us -> 15.4 us  [chip_shift(): return lax.ppermute(x, 'dp', perm)]
    ppermute x9, starting transfers between devices: 12.6 us -> 10.1 us  [chip_shift(): return lax.ppermute(x, 'dp', perm)]
    ppermute x1, starting transfers between devices: 0.09 us -> 2.29 us  [per_device(): left_near = lax.ppermute(left, 'tensor', [(i, i ^ 1) for i in range(n_t)])]
    ppermute x1, starting transfers between devices: 0.09 us -> 1.61 us  [per_device(): lax.ppermute(left_pair, 'tensor', [(i, n_t - 1 - i) for i in range(n_t)])]
    ppermute x16, starting transfers between devices: 26.5 us -> 25.2 us  [shift(): return lax.ppermute(x, axis, [(i, (i + k) % n) for i in range(n)])]
    unnamed x24 -> x30, local copies, waits for them, and re-layouts: 4.05 us -> 4.07 us
  transfers between devices with their start and end apart: 33 -> 33, of which waited for: 9 -> 10; matrix products, arithmetic and copies ran while one was open for 0% -> 0% of each run, Pallas kernels for 28% -> 21%
where the time goes in v3:
time: 128 us; the launch traced here: 127 us
  starting transfers between devices  49.1 us (38%)
  Pallas kernels  38.9 us (30%)
  waiting for transfers between devices  33.3 us (26%)
  local copies, waits for them, and re-layouts  4.11 us (3%)
    pallas_call x13, Pallas kernels, call(): pl.pallas_call(body, out_shape=(*outs, shape((1,), jnp.int32)), in_specs=...  37.6 us
    ppermute x16, starting transfers between devices, shift(): return lax.ppermute(x, axis, [(i, (i + k) % n) for i in range(n)])  25.2 us
    ppermute x9, waiting for transfers between devices, chip_shift(): return lax.ppermute(x, 'dp', perm)  15.4 us
    ppermute x16, waiting for transfers between devices, shift(): return lax.ppermute(x, axis, [(i, (i + k) % n) for i in range(n)])  12.6 us
    ppermute x9, starting transfers between devices, chip_shift(): return lax.ppermute(x, 'dp', perm)  10.1 us
    ppermute x6, starting transfers between devices, core_swap(): return lax.ppermute(x, 'dp', [(i, i ^ 1) for i in range(n_data)])  9.98 us
    unnamed x30, local copies, waits for them, and re-layouts  4.07 us
    ppermute x1, waiting for transfers between devices, per_device(): lax.ppermute(left_pair, 'tensor', [(i, n_t - 1 - i) for i in range(n_t)])  3.15 us
  transfers between devices with their start and end apart: 33, of which 10 were waited for; matrix products, arithmetic and copies ran while one was open for 0% of the time, Pallas kernels for 21%

profile of v3, /device:TPU:1, one launch (start us, length us, event | category | flops | bytes accessed | tf_op | source)
XLA Modules:
  0.0 126.7 jit_solution(10472787188681792596)
XLA Ops:
  2.9 6.4 %shard_map.111 = (f32[640,128]{1,0:T(8,128)S(1)}, bf16[640,128]{1,0:T(8,128)(2,1)S(1)}, f32[640,128]{1,0:T(8,128)S(1)}, bf16[640,128]{1,0:T(8,128)(2,1)S(1)}, bf...) custom-call(s32[16]{0:T(128)S(1)} %copy-done.6, ...), custom_call_target="tpu_custom_call" | custom-call | tf_op jit(solution)/shard_map/pallas_call | solution.py:38
  9.4 4.3 %collective-permute-start.6 = (bf16[640,128]{1,0:T(8,128)(2,1)S(1)}, bf16[640,128]{1,0:T(8,128)(2,1)S(1)}, u32[]{:S(2)}, u32[]{:S(2)}) collective-permute-start(bf16[640,128]{1,0:T(8,128)(2,1)S(1)} %get-tuple-element.56), channel_id=1, source_target_pairs={{0,1},{1,2},{2,3},{3,0},{4,5},{5,6},{6,7},{7,4},{8,9},{9,10},{10,1... | collective-permute-start | bytes 491528 | tf_op jit(solution)/shard_map/ppermute | solution.py:357
  13.6 1.9 %collective-permute-start.7 = (bf16[640,128]{1,0:T(8,128)(2,1)S(1)}, bf16[640,128]{1,0:T(8,128)(2,1)S(1)}, u32[]{:S(2)}, u32[]{:S(2)}) collective-permute-start(bf16[640,128]{1,0:T(8,128)(2,1)S(1)} %get-tuple-element.57), channel_id=1, source_target_pairs={{0,2},{1,3},{2,0},{3,1},{4,6},{5,7},{6,4},{7,5},{8,10},{9,11},{10,... | collective-permute-start | bytes 491528 | tf_op jit(solution)/shard_map/ppermute | solution.py:357
  16.1 3.1 %collective-permute-start.2 = (bf16[640,128]{1,0:T(8,128)(2,1)S(1)}, bf16[640,128]{1,0:T(8,128)(2,1)S(1)}, u32[]{:S(2)}, u32[]{:S(2)}) collective-permute-start(bf16[640,128]{1,0:T(8,128)(2,1)S(1)} %get-tuple-element.54), channel_id=1, source_target_pairs={{0,12},{4,0},{8,4},{12,8},{1,13},{5,1},{9,5},{13,9},{2,14},{6,2},{... | collective-permute-start | bytes 491528 | tf_op jit(solution)/shard_map/ppermute | solution.py:357
  19.8 2.9 %collective-permute-done.7 = bf16[640,128]{1,0:T(8,128)(2,1)S(1)} collective-permute-done((bf16[640,128]{1,0:T(8,128)(2,1)S(1)}, bf16[640,128]{1,0:T(8,128)(2,1)S(1)}, u32[]{:S(2)}, u32[]{:S(2)}) %collective-permute-start.7) | collective-permute-done | bytes 163872 | tf_op jit(solution)/shard_map/ppermute | solution.py:357
  22.7 3.1 %collective-permute-start.11 = (bf16[640,128]{1,0:T(8,128)(2,1)S(1)}, bf16[640,128]{1,0:T(8,128)(2,1)S(1)}, u32[]{:S(2)}, u32[]{:S(2)}) collective-permute-start(bf16[640,128]{1,0:T(8,128)(2,1)S(1)} %get-tuple-element.102.refs_5_), channel_id=1, source_target_pairs={{0,12},{4,0},{8,4},{12,8},{1,13},{5,1},{9,5},{13,9},{2,14},{6,2},{... | collective-permute-start | bytes 491528 | tf_op jit(solution)/shard_map/ppermute | solution.py:357
  26.9 2.5 %collective-permute-done = bf16[640,128]{1,0:T(8,128)(2,1)S(1)} collective-permute-done((bf16[640,128]{1,0:T(8,128)(2,1)S(1)}, bf16[640,128]{1,0:T(8,128)(2,1)S(1)}, u32[]{:S(2)}, u32[]{:S(2)}) %collective-permute-start) | collective-permute-done | bytes 163872 | tf_op jit(solution)/shard_map/ppermute | solution.py:357
  30.0 2.6 %collective-permute-start.4 = (bf16[640,128]{1,0:T(8,128)(2,1)S(1)}, bf16[640,128]{1,0:T(8,128)(2,1)S(1)}, u32[]{:S(2)}, u32[]{:S(2)}) collective-permute-start(bf16[640,128]{1,0:T(8,128)(2,1)S(1)} %add_convert_fusion.refs_2_.refs_5_), channel_id=1, source_target_pairs={{0,2},{1,3},{2,0},{3,1},{4,6},{5,7},{6,4},{7,5},{8,10},{9,11},{10,... | collective-permute-start | bytes 491528 | tf_op jit(solution)/shard_map/ppermute | solution.py:357
  35.5 5.9 %shard_map.112 = (f32[4,512,128]{2,1,0:T(8,128)S(1)}, bf16[4,512,128]{2,1,0:T(8,128)(2,1)S(1)}, s32[1]{0:T(128)}) custom-call(s32[16]{0:T(128)S(1)} %copy-done.6, s32[32]{0:T(128)S(1)} %copy-done.8, s32[32]{0:T(128)S(1)} %copy-done.10, bf16[640,2048]{1,0:T(8,128)(2,1)S(1)} %copy-done, bf16[640,7168]{1,0:T(8,128)(2,1)S(1)} %bitcast.5, ...), custom_call_target="tpu_custom_call" | custom-call | tf_op jit(solution)/shard_map/pallas_call | solution.py:38
  42.9 3.6 %collective-permute-start.19 = (bf16[320,1792]{1,0:T(8,128)(2,1)S(1)}, bf16[320,1792]{1,0:T(8,128)(2,1)S(1)}, u32[]{:S(2)}, u32[]{:S(2)}) collective-permute-start(bf16[320,1792]{1,0:T(8,128)(2,1)S(1)} %get-tuple-element.80), channel_id=1, source_target_pairs={{0,12},{4,0},{8,4},{12,8},{1,13},{5,1},{9,5},{13,9},{2,14},{6,2},{... | collective-permute-start | bytes 3440648 | tf_op jit(solution)/shard_map/ppermute | solution.py:357
  46.5 4.8 %shard_map.114 = (f32[4,1664,128]{2,1,0:T(8,128)S(1)}, bf16[2224,128]{1,0:T(8,128)(2,1)S(1)}, bf16[2224,128]{1,0:T(8,128)(2,1)S(1)}, bf16[2208,128]{1,0:T(8,128)(2,1)S(1)}, s32[1]{0:T(128)}) custom-call(bf16[640,2048]{1,0:T(8,128)(2,1)S(1)} %copy-done.1, bf16[640,7168]{1,0:T(8,128)(2,1)} %refs_1_.7, bf16[640,128]{1,0:T(8,128)(2,1)S(1)} %add_convert_fusion.refs_2_.refs_5_, ...), custom_call_target="tpu_custom_call" | custom-call | tf_op jit(solution)/shard_map/pallas_call | solution.py:38
  51.3 2.2 %collective-permute-start.12 = (bf16[2224,128]{1,0:T(8,128)(2,1)S(1)}, bf16[2224,128]{1,0:T(8,128)(2,1)S(1)}, u32[]{:S(2)}, u32[]{:S(2)}) collective-permute-start(bf16[2224,128]{1,0:T(8,128)(2,1)S(1)} %get-tuple-element.67), channel_id=1, source_target_pairs={{0,16},{16,0},{32,48},{48,32},{64,80},{80,64},{96,112},{112,96},{1... | collective-permute-start | bytes 1708040 | tf_op jit(solution)/shard_map/ppermute | solution.py:367
  54.0 3.3 %shard_map.115 = (bf16[640,1792]{1,0:T(8,128)(2,1)S(1)}, bf16[640,1792]{1,0:T(8,128)(2,1)S(1)}, s32[1]{0:T(128)}) custom-call(s32[16]{0:T(128)S(1)} %copy-done.6, s32[32]{0:T(128)S(1)} %copy-done.8, s32[32]{0:T(128)S(1)} %copy-done.10, bf16[640,2048]{1,0:T(8,128)(2,1)S(1)} %copy-done.1, bf16[32,128,128]{2,1,0:T(8,128)(2,1)S(1)} %copy-done.2, ...), custom_call_target="tpu_custom_call" | custom-call | tf_op jit(solution)/shard_map/pallas_call | solution.py:38
  63.1 7.1 %collective-permute-done.18.refs_2_ = bf16[320,1792]{1,0:T(8,128)(2,1)S(1)} collective-permute-done((bf16[320,1792]{1,0:T(8,128)(2,1)S(1)}, bf16[320,1792]{1,0:T(8,128)(2,1)S(1)}, u32[]{:S(2)}, u32[]{:S(2)}) %collective-permute-start.18) | collective-permute-done | bytes 1146912 | tf_op jit(solution)/shard_map/ppermute | solution.py:357
  72.2 2.1 %collective-permute-start.25 = (bf16[640,1792]{1,0:T(8,128)(2,1)S(1)}, bf16[640,1792]{1,0:T(8,128)(2,1)S(1)}, u32[]{:S(2)}, u32[]{:S(2)}) collective-permute-start(bf16[640,1792]{1,0:T(8,128)(2,1)S(1)} %get-tuple-element.92), channel_id=1, source_target_pairs={{0,12},{4,0},{8,4},{12,8},{1,13},{5,1},{9,5},{13,9},{2,14},{6,2},{... | collective-permute-start | bytes 6881288 | tf_op jit(solution)/shard_map/ppermute | solution.py:357
  75.5 2.3 %collective-permute-start.22 = (bf16[256,128]{1,0:T(8,128)(2,1)S(1)}, bf16[256,128]{1,0:T(8,128)(2,1)S(1)}, u32[]{:S(2)}, u32[]{:S(2)}) collective-permute-start(bf16[256,128]{1,0:T(8,128)(2,1)S(1)} %get-tuple-element.85.refs_0_), channel_id=1, source_target_pairs={{0,1},{1,0},{2,3},{3,2},{4,5},{5,4},{6,7},{7,6},{8,9},{9,8},{10,11... | collective-permute-start | bytes 196616 | tf_op jit(solution)/shard_map/ppermute | solution.py:511
  78.1 2.4 %collective-permute-start.21 = (bf16[704,128]{1,0:T(8,128)(2,1)S(1)}, bf16[704,128]{1,0:T(8,128)(2,1)S(1)}, u32[]{:S(2)}, u32[]{:S(2)}) collective-permute-start(bf16[704,128]{1,0:T(8,128)(2,1)S(1)} %get-tuple-element.84), channel_id=1, source_target_pairs={{0,96},{16,112},{32,0},{48,16},{64,32},{80,48},{96,64},{112,80},{1... | collective-permute-start | bytes 540680 | tf_op jit(solution)/shard_map/ppermute | solution.py:363
  83.9 3.2 %collective-permute-done.23.refs_6_ = bf16[512,128]{1,0:T(8,128)(2,1)S(1)} collective-permute-done((bf16[512,128]{1,0:T(8,128)(2,1)S(1)}, bf16[512,128]{1,0:T(8,128)(2,1)S(1)}, u32[]{:S(2)}, u32[]{:S(2)}) %collective-permute-start.23) | collective-permute-done | bytes 131104 | tf_op jit(solution)/shard_map/ppermute | solution.py:517
  89.9 10.8 %collective-permute-done.27.refs_2_ = bf16[2432,128]{1,0:T(8,128)(2,1)S(1)} collective-permute-done((bf16[2432,128]{1,0:T(8,128)(2,1)S(1)}, bf16[2432,128]{1,0:T(8,128)(2,1)S(1)}, u32[]{:S(2)}, u32[]{:S(2)}) %collective-permute-start.27) | collective-permute-done | bytes 622624 | tf_op jit(solution)/shard_map/ppermute | solution.py:363
  101.8 6.0 %collective-permute-start.30 = (bf16[5632,128]{1,0:T(8,128)(2,1)S(1)}, bf16[5632,128]{1,0:T(8,128)(2,1)S(1)}, u32[]{:S(2)}, u32[]{:S(2)}) collective-permute-start(bf16[5632,128]{1,0:T(8,128)(2,1)S(1)} %get-tuple-element.94.refs_3_), channel_id=1, source_target_pairs={{0,16},{16,0},{32,48},{48,32},{64,80},{80,64},{96,112},{112,96},{1... | collective-permute-start | bytes 4325384 | tf_op jit(solution)/shard_map/ppermute | solution.py:367
  109.5 4.9 %shard_map.121 = (f32[640,1792]{1,0:T(8,128)S(1)}, s32[1]{0:T(128)}) custom-call(s32[16]{0:T(128)S(1)} %copy-done.7, s32[32]{0:T(128)S(1)} %copy-done.9, s32[32]{0:T(128)S(1)} %copy-done.11, bf16[640,2048]{1,0:T(8,128)(2,1)S(1)} %copy-done.1, bf16[32,128,128]{2,1,0:T(8,128)(2,1)S(1)} %copy-done.2, bf16[640,128]{1,0:T(8,128)(2,1)S(1)} %add_convert_fusion.refs_2_.refs_5_, ...), custom_call_target="tpu_custom_call" | custom-call | tf_op jit(solution)/shard_map/pallas_call | solution.py:38
  114.4 2.4 %collective-permute-done.29.refs_1_ = bf16[1216,128]{1,0:T(8,128)(2,1)S(1)} collective-permute-done((bf16[1216,128]{1,0:T(8,128)(2,1)S(1)}, bf16[1216,128]{1,0:T(8,128)(2,1)S(1)}, u32[]{:S(2)}, u32[]{:S(2)}) %collective-permute-start.29) | collective-permute-done | bytes 311328 | tf_op jit(solution)/shard_map/ppermute | solution.py:363
  120.4 2.2 %collective-permute-done.31.refs_7_ = bf16[1664,128]{1,0:T(8,128)(2,1)S(1)} collective-permute-done((bf16[1664,128]{1,0:T(8,128)(2,1)S(1)}, bf16[1664,128]{1,0:T(8,128)(2,1)S(1)}, u32[]{:S(2)}, u32[]{:S(2)}) %collective-permute-start.31) | collective-permute-done | bytes 426016 | tf_op jit(solution)/shard_map/ppermute | solution.py:367
  122.6 3.9 %shard_map.124 = (bf16[640,1792]{1,0:T(8,128)(2,1)}, bf16[2048,512]{1,0:T(8,128)(2,1)}, bf16[512,1792]{1,0:T(8,128)(2,1)}, bf16[4096,128]{1,0:T(8,128)(2,1)}, s32[1]{0:T(128)}) custom-call(f32[640,1792]{1,0:T(8,128)S(1)} %get-tuple-element.90.refs_0_, bf16[640,1792]{1,0:T(8,128)(2,1)S(1)} %collective-permute-done.24.refs_1_, ...), custom_call_target="tpu_custom_call" | custom-call | tf_op jit(solution)/shard_map/pallas_call | solution.py:38
  (91 shorter events, 31.7 us)
Async XLA Ops:
  9.4 9.8 %collective-permute-start.6 = (bf16[640,128]{1,0:T(8,128)(2,1)S(1)}, bf16[640,128]{1,0:T(8,128)(2,1)S(1)}, u32[]{:S(2)}, u32[]{:S(2)}) collective-permute-start(bf16[640,128]{1,0:T(8,128)(2,1)S(1)} %get-tuple-element.56), channel_id=1, source_target_pairs={{0,1},{1,2},{2,3},{3,0},{4,5},{5,6},{6,7},{7,4},{8,9},{9,10},{10,1... | collective-permute-start | bytes 491528 | tf_op jit(solution)/shard_map/ppermute | solution.py:357
  13.6 9.0 %collective-permute-start.7 = (bf16[640,128]{1,0:T(8,128)(2,1)S(1)}, bf16[640,128]{1,0:T(8,128)(2,1)S(1)}, u32[]{:S(2)}, u32[]{:S(2)}) collective-permute-start(bf16[640,128]{1,0:T(8,128)(2,1)S(1)} %get-tuple-element.57), channel_id=1, source_target_pairs={{0,2},{1,3},{2,0},{3,1},{4,6},{5,7},{6,4},{7,5},{8,10},{9,11},{10,... | collective-permute-start | bytes 491528 | tf_op jit(solution)/shard_map/ppermute | solution.py:357
  15.5 7.1 %collective-permute-start.8 = (bf16[640,128]{1,0:T(8,128)(2,1)S(1)}, bf16[640,128]{1,0:T(8,128)(2,1)S(1)}, u32[]{:S(2)}, u32[]{:S(2)}) collective-permute-start(bf16[640,128]{1,0:T(8,128)(2,1)S(1)} %get-tuple-element.58), channel_id=1, source_target_pairs={{0,3},{1,0},{2,1},{3,2},{4,7},{5,4},{6,5},{7,6},{8,11},{9,8},{10,9... | collective-permute-start | bytes 491528 | tf_op jit(solution)/shard_map/ppermute | solution.py:357
  16.1 10.0 %collective-permute-start.2 = (bf16[640,128]{1,0:T(8,128)(2,1)S(1)}, bf16[640,128]{1,0:T(8,128)(2,1)S(1)}, u32[]{:S(2)}, u32[]{:S(2)}) collective-permute-start(bf16[640,128]{1,0:T(8,128)(2,1)S(1)} %get-tuple-element.54), channel_id=1, source_target_pairs={{0,12},{4,0},{8,4},{12,8},{1,13},{5,1},{9,5},{13,9},{2,14},{6,2},{... | collective-permute-start | bytes 491528 | tf_op jit(solution)/shard_map/ppermute | solution.py:357
  19.2 7.7 %collective-permute-start.1 = (bf16[640,128]{1,0:T(8,128)(2,1)S(1)}, bf16[640,128]{1,0:T(8,128)(2,1)S(1)}, u32[]{:S(2)}, u32[]{:S(2)}) collective-permute-start(bf16[640,128]{1,0:T(8,128)(2,1)S(1)} %get-tuple-element.54), channel_id=1, source_target_pairs={{0,8},{4,12},{8,0},{12,4},{1,9},{5,13},{9,1},{13,5},{2,10},{6,14},... | collective-permute-start | bytes 491528 | tf_op jit(solution)/shard_map/ppermute | solution.py:357
  19.2 10.3 %collective-permute-start = (bf16[640,128]{1,0:T(8,128)(2,1)S(1)}, bf16[640,128]{1,0:T(8,128)(2,1)S(1)}, u32[]{:S(2)}, u32[]{:S(2)}) collective-permute-start(bf16[640,128]{1,0:T(8,128)(2,1)S(1)} %get-tuple-element.54), channel_id=1, source_target_pairs={{0,4},{4,8},{8,12},{12,0},{1,5},{5,9},{9,13},{13,1},{2,6},{6,10},{... | collective-permute-start | bytes 491528 | tf_op jit(solution)/shard_map/ppermute | solution.py:357
  22.7 9.8 %collective-permute-start.11 = (bf16[640,128]{1,0:T(8,128)(2,1)S(1)}, bf16[640,128]{1,0:T(8,128)(2,1)S(1)}, u32[]{:S(2)}, u32[]{:S(2)}) collective-permute-start(bf16[640,128]{1,0:T(8,128)(2,1)S(1)} %get-tuple-element.102.refs_5_), channel_id=1, source_target_pairs={{0,12},{4,0},{8,4},{12,8},{1,13},{5,1},{9,5},{13,9},{2,14},{6,2},{... | collective-permute-start | bytes 491528 | tf_op jit(solution)/shard_map/ppermute | solution.py:357
  25.8 15.6 %collective-permute-start.10 = (bf16[640,128]{1,0:T(8,128)(2,1)S(1)}, bf16[640,128]{1,0:T(8,128)(2,1)S(1)}, u32[]{:S(2)}, u32[]{:S(2)}) collective-permute-start(bf16[640,128]{1,0:T(8,128)(2,1)S(1)} %get-tuple-element.102.refs_5_), channel_id=1, source_target_pairs={{0,8},{4,12},{8,0},{12,4},{1,9},{5,13},{9,1},{13,5},{2,10},{6,14},... | collective-permute-start | bytes 491528 | tf_op jit(solution)/shard_map/ppermute | solution.py:357
  26.2 15.3 %collective-permute-start.9 = (bf16[640,128]{1,0:T(8,128)(2,1)S(1)}, bf16[640,128]{1,0:T(8,128)(2,1)S(1)}, u32[]{:S(2)}, u32[]{:S(2)}) collective-permute-start(bf16[640,128]{1,0:T(8,128)(2,1)S(1)} %get-tuple-element.102.refs_5_), channel_id=1, source_target_pairs={{0,4},{4,8},{8,12},{12,0},{1,5},{5,9},{9,13},{13,1},{2,6},{6,10},{... | collective-permute-start | bytes 491528 | tf_op jit(solution)/shard_map/ppermute | solution.py:357
  29.6 11.9 %collective-permute-start.5 = (bf16[640,128]{1,0:T(8,128)(2,1)S(1)}, bf16[640,128]{1,0:T(8,128)(2,1)S(1)}, u32[]{:S(2)}, u32[]{:S(2)}) collective-permute-start(bf16[640,128]{1,0:T(8,128)(2,1)S(1)} %add_convert_fusion.refs_2_.refs_5_), channel_id=1, source_target_pairs={{0,3},{1,0},{2,1},{3,2},{4,7},{5,4},{6,5},{7,6},{8,11},{9,8},{10,9... | collective-permute-start | bytes 491528 | tf_op jit(solution)/shard_map/ppermute | solution.py:357
  30.0 11.4 %collective-permute-start.4 = (bf16[640,128]{1,0:T(8,128)(2,1)S(1)}, bf16[640,128]{1,0:T(8,128)(2,1)S(1)}, u32[]{:S(2)}, u32[]{:S(2)}) collective-permute-start(bf16[640,128]{1,0:T(8,128)(2,1)S(1)} %add_convert_fusion.refs_2_.refs_5_), channel_id=1, source_target_pairs={{0,2},{1,3},{2,0},{3,1},{4,6},{5,7},{6,4},{7,5},{8,10},{9,11},{10,... | collective-permute-start | bytes 491528 | tf_op jit(solution)/shard_map/ppermute | solution.py:357
  32.6 8.9 %collective-permute-start.3 = (bf16[640,128]{1,0:T(8,128)(2,1)S(1)}, bf16[640,128]{1,0:T(8,128)(2,1)S(1)}, u32[]{:S(2)}, u32[]{:S(2)}) collective-permute-start(bf16[640,128]{1,0:T(8,128)(2,1)S(1)} %add_convert_fusion.refs_2_.refs_5_), channel_id=1, source_target_pairs={{0,1},{1,2},{2,3},{3,0},{4,5},{5,6},{6,7},{7,4},{8,9},{9,10},{10,1... | collective-permute-start | bytes 491528 | tf_op jit(solution)/shard_map/ppermute | solution.py:357
  42.8 27.4 %collective-permute-start.18 = (bf16[320,1792]{1,0:T(8,128)(2,1)S(1)}, bf16[320,1792]{1,0:T(8,128)(2,1)S(1)}, u32[]{:S(2)}, u32[]{:S(2)}) collective-permute-start(bf16[320,1792]{1,0:T(8,128)(2,1)S(1)} %get-tuple-element.79), channel_id=1, source_target_pairs={{0,4},{4,8},{8,12},{12,0},{1,5},{5,9},{9,13},{13,1},{2,6},{6,10},{... | collective-permute-start | bytes 3440648 | tf_op jit(solution)/shard_map/ppermute | solution.py:357
  42.9 27.3 %collective-permute-start.19 = (bf16[320,1792]{1,0:T(8,128)(2,1)S(1)}, bf16[320,1792]{1,0:T(8,128)(2,1)S(1)}, u32[]{:S(2)}, u32[]{:S(2)}) collective-permute-start(bf16[320,1792]{1,0:T(8,128)(2,1)S(1)} %get-tuple-element.80), channel_id=1, source_target_pairs={{0,12},{4,0},{8,4},{12,8},{1,13},{5,1},{9,5},{13,9},{2,14},{6,2},{... | collective-permute-start | bytes 3440648 | tf_op jit(solution)/shard_map/ppermute | solution.py:357
  58.8 15.5 %collective-permute-start.15 = (bf16[1664,128]{1,0:T(8,128)(2,1)S(1)}, bf16[1664,128]{1,0:T(8,128)(2,1)S(1)}, u32[]{:S(2)}, u32[]{:S(2)}) collective-permute-start(bf16[1664,128]{1,0:T(8,128)(2,1)S(1)} %get-tuple-element.73), channel_id=1, source_target_pairs={{0,32},{16,48},{32,64},{48,80},{64,96},{80,112},{96,0},{112,16},{1... | collective-permute-start | bytes 1277960 | tf_op jit(solution)/shard_map/ppermute | solution.py:363
  60.1 14.2 %collective-permute-start.16 = (bf16[1664,128]{1,0:T(8,128)(2,1)S(1)}, bf16[1664,128]{1,0:T(8,128)(2,1)S(1)}, u32[]{:S(2)}, u32[]{:S(2)}) collective-permute-start(bf16[1664,128]{1,0:T(8,128)(2,1)S(1)} %get-tuple-element.74), channel_id=1, source_target_pairs={{0,96},{16,112},{32,0},{48,16},{64,32},{80,48},{96,64},{112,80},{1... | collective-permute-start | bytes 1277960 | tf_op jit(solution)/shard_map/ppermute | solution.py:363
  61.6 12.7 %collective-permute-start.17 = (bf16[256,128]{1,0:T(8,128)(2,1)S(1)}, bf16[256,128]{1,0:T(8,128)(2,1)S(1)}, u32[]{:S(2)}, u32[]{:S(2)}) collective-permute-start(bf16[256,128]{1,0:T(8,128)(2,1)S(1)} %get-tuple-element.76), channel_id=1, source_target_pairs={{0,64},{16,80},{32,96},{48,112},{64,0},{80,16},{96,32},{112,48},{1... | collective-permute-start | bytes 196616 | tf_op jit(solution)/shard_map/ppermute | solution.py:363
  71.5 51.1 %collective-permute-start.24 = (bf16[640,1792]{1,0:T(8,128)(2,1)S(1)}, bf16[640,1792]{1,0:T(8,128)(2,1)S(1)}, u32[]{:S(2)}, u32[]{:S(2)}) collective-permute-start(bf16[640,1792]{1,0:T(8,128)(2,1)S(1)} %get-tuple-element.91), channel_id=1, source_target_pairs={{0,4},{4,8},{8,12},{12,0},{1,5},{5,9},{9,13},{13,1},{2,6},{6,10},{... | collective-permute-start | bytes 6881288 | tf_op jit(solution)/shard_map/ppermute | solution.py:357
  72.2 50.4 %collective-permute-start.25 = (bf16[640,1792]{1,0:T(8,128)(2,1)S(1)}, bf16[640,1792]{1,0:T(8,128)(2,1)S(1)}, u32[]{:S(2)}, u32[]{:S(2)}) collective-permute-start(bf16[640,1792]{1,0:T(8,128)(2,1)S(1)} %get-tuple-element.92), channel_id=1, source_target_pairs={{0,12},{4,0},{8,4},{12,8},{1,13},{5,1},{9,5},{13,9},{2,14},{6,2},{... | collective-permute-start | bytes 6881288 | tf_op jit(solution)/shard_map/ppermute | solution.py:357
  88.4 12.3 %collective-permute-start.27 = (bf16[2432,128]{1,0:T(8,128)(2,1)S(1)}, bf16[2432,128]{1,0:T(8,128)(2,1)S(1)}, u32[]{:S(2)}, u32[]{:S(2)}) collective-permute-start(bf16[2432,128]{1,0:T(8,128)(2,1)S(1)} %get-tuple-element.93.refs_0_), channel_id=1, source_target_pairs={{0,96},{16,112},{32,0},{48,16},{64,32},{80,48},{96,64},{112,80},{1... | collective-permute-start | bytes 1867784 | tf_op jit(solution)/shard_map/ppermute | solution.py:363
  89.4 11.7 %collective-permute-start.26 = (bf16[2432,128]{1,0:T(8,128)(2,1)S(1)}, bf16[2432,128]{1,0:T(8,128)(2,1)S(1)}, u32[]{:S(2)}, u32[]{:S(2)}) collective-permute-start(bf16[2432,128]{1,0:T(8,128)(2,1)S(1)} %get-tuple-element.93.refs_0_), channel_id=1, source_target_pairs={{0,32},{16,48},{32,64},{48,80},{64,96},{80,112},{96,0},{112,16},{1... | collective-permute-start | bytes 1867784 | tf_op jit(solution)/shard_map/ppermute | solution.py:363
  101.8 20.8 %collective-permute-start.30 = (bf16[5632,128]{1,0:T(8,128)(2,1)S(1)}, bf16[5632,128]{1,0:T(8,128)(2,1)S(1)}, u32[]{:S(2)}, u32[]{:S(2)}) collective-permute-start(bf16[5632,128]{1,0:T(8,128)(2,1)S(1)} %get-tuple-element.94.refs_3_), channel_id=1, source_target_pairs={{0,16},{16,0},{32,48},{48,32},{64,80},{80,64},{96,112},{112,96},{1... | collective-permute-start | bytes 4325384 | tf_op jit(solution)/shard_map/ppermute | solution.py:367
  107.8 9.0 %collective-permute-start.29 = (bf16[1216,128]{1,0:T(8,128)(2,1)S(1)}, bf16[1216,128]{1,0:T(8,128)(2,1)S(1)}, u32[]{:S(2)}, u32[]{:S(2)}) collective-permute-start(bf16[1216,128]{1,0:T(8,128)(2,1)S(1)} %slice.9), channel_id=1, source_target_pairs={{0,96},{16,112},{32,0},{48,16},{64,32},{80,48},{96,64},{112,80},{1... | collective-permute-start | bytes 933896 | tf_op jit(solution)/shard_map/ppermute | solution.py:363
  108.0 10.0 %collective-permute-start.28 = (bf16[1216,128]{1,0:T(8,128)(2,1)S(1)}, bf16[1216,128]{1,0:T(8,128)(2,1)S(1)}, u32[]{:S(2)}, u32[]{:S(2)}) collective-permute-start(bf16[1216,128]{1,0:T(8,128)(2,1)S(1)} %slice.8), channel_id=1, source_target_pairs={{0,32},{16,48},{32,64},{48,80},{64,96},{80,112},{96,0},{112,16},{1... | collective-permute-start | bytes 933896 | tf_op jit(solution)/shard_map/ppermute | solution.py:363
  (24 other events, 249.5 us)

commit v4 on v3

--- a/solution.py
+++ b/solution.py
@@ -293,9 +293,7 @@
     add_blocks(place, q_blocks, 0, counts, rows, cols, tok, vals, out)
 
 
-def last_kernel(place, low, from_behind, from_ahead, *refs):
-    (mixed_out, left_out, right_out, blocks), (mixed, left, right, sems) = refs[-8:-4], refs[-4:]
-    refs = refs[:-8]
+def put_chunks(place, chunks, left, right, blocks, sems):
     n_l = left.shape[0] // place.n_d
     n_r = right.shape[0] // place.n_d
     n_b = blocks.shape[0] // place.n_d
@@ -306,49 +304,57 @@
     far_t = place.n_t - 1 - t
     order = (t, near_t, far_t, place.n_t - 1 - near_t)
     copies = []
-
-    def send(pair):
-        copies.extend(fetch((*pair, sems.at[len(copies)])))
-
-    chunks = []
-    n = len(refs) // 2
-    for core, (first, rest, last) in (
-        (place.core, refs[:n]),
-        (1 - place.core, refs[n:]),
-    ):
-        half = last.shape[0] // 2
-        behind, ahead = first.at[2 * half : 4 * half], first.at[4 * half :]
-        for j, segments in (
-            (0, ((0, first),)),
-            (-1, ((0, behind),)),
-            (1, ((0, ahead), (ahead.shape[0], rest))),
-            (2, ((0, last),)),
-        ):
-            at = lax.rem(place.chip + j + place.chips, place.chips) * 2 + core
-            chunks.append((at, segments))
-
-    def piece(segments, lo, hi):
-        base, src = [s for s in segments if s[0] <= lo][-1]
-        return src.at[lo - base : hi - base]
-
-    base = n_left + panels * n_r
     for at, segments in chunks:
-        send((piece(segments, base, base + n_b), blocks.at[span(at, n_b)]))
-    for at, segments in chunks:
+
+        def put(lo, hi, dst):
+            base, src = [s for s in segments if s[0] <= lo][-1]
+            copies.extend(fetch((src.at[lo - base : hi - base], dst, sems.at[len(copies)])))
+
         for k in range(place.n_t):
-            left[span(at, n_l), lanes(order[k])] = piece(segments, k * n_l, (k + 1) * n_l)[...]
-    send((left, left_out))
-    for at, segments in chunks:
+            put(k * n_l, (k + 1) * n_l, left.at[span(at, n_l), lanes(order[k])])
         for p in range(panels):
             lo = n_left + p * n_r
-            right[span(at, n_r), p * SIDE : (p + 1) * SIDE] = piece(segments, lo, lo + n_r)[...]
-    send((right, right_out))
+            put(lo, lo + n_r, right.at[span(at, n_r), pl.ds(p * SIDE, SIDE)])
+        lo = n_left + panels * n_r
+        put(lo, lo + n_b, blocks.at[span(at, n_b)])
+    return copies
+
+
+def chunk_at(place, j, core):
+    return lax.rem(place.chip + j + place.chips, place.chips) * 2 + core
+
+
+def three_chunks(place, core, first, rest):
+    n = (first.shape[0] + rest.shape[0]) // 3
+    ahead = first.at[2 * n :]
+    return [
+        (chunk_at(place, 0, core), ((0, first),)),
+        (chunk_at(place, -1, core), ((0, first.at[n : 2 * n]),)),
+        (chunk_at(place, 1, core), ((0, ahead), (ahead.shape[0], rest))),
+    ]
+
+
+def three_kernel(place, first, rest, left, right, blocks, sems):
+    chunks = three_chunks(place, place.core, first, rest)
+    for copy in put_chunks(place, chunks, left, right, blocks, sems):
+        copy.wait()
+
+
+def last_kernel(
+    place, low, from_behind, from_ahead, last, last2, first2, rest2, l_in, r_in, b_in,
+    mixed_out, left, right, blocks, mixed, sems, mixed_sems,
+):
+    chunks = [
+        (chunk_at(place, 2, core), ((0, one),))
+        for core, one in ((place.core, last), (1 - place.core, last2))
+    ] + three_chunks(place, 1 - place.core, first2, rest2)
+    copies = put_chunks(place, chunks, left, right, blocks, sems)
     size = mixed.shape[0] // 4
     for i in range(4):
         rows = pl.ds(i * size, size)
         total = low[rows, :] + from_behind[rows, :].astype(F32) + from_ahead[rows, :].astype(F32)
         mixed[rows, :] = total.astype(BF16)
-        send((mixed.at[rows], mixed_out.at[rows]))
+        copies.extend(fetch((mixed.at[rows], mixed_out.at[rows], mixed_sems.at[i])))
     for copy in copies:
         copy.wait()
 
@@ -416,7 +422,7 @@
 
     for x in rank_in:
         rank = rank + x.astype(F32)
-    rank = rank.astype(BF16)
+    rank, back = lax.optimization_barrier((rank.astype(BF16), back))
     ranks = [rank] + over(n_t, lambda k: shift(rank, "tensor", n_t, k))
     for x in back_in:
         back = back + x.astype(F32)
@@ -535,38 +541,42 @@
         after=(step,),
         mib=20,
     )
+    first, rest, step = call(
+        pair_kernel,
+        (shape((2 * n_msg + 3 * n_l, SIDE), BF16), shape((n_msg - 3 * n_l, SIDE), BF16)),
+        vmem=(message, m_behind, m_ahead),
+        after=(step,),
+    )
+    per_chunk = n_t + q_blocks + 1
+    outs = (
+        shape((features, rank_size), BF16),
+        shape((rank_size, quarter), BF16),
+        shape((maxb * SIDE, SIDE), BF16),
+    )
+    *grads, step = call(
+        bind(three_kernel),
+        outs,
+        vmem=(first, rest),
+        scratch=[dma((3 * per_chunk,))],
+        after=(step,),
+        mib=16,
+        hbm_outs=3,
+    )
     m_last, step = call(
         stack_kernel,
         (shape((n_msg, SIDE), BF16),),
         vmem=(m_last_behind, m_last_ahead),
         after=(step,),
     )
-    first, rest, _ = call(
-        pair_kernel,
-        (shape((2 * n_msg + 3 * n_l, SIDE), BF16), shape((n_msg - 3 * n_l, SIDE), BF16)),
-        vmem=(message, m_behind, m_ahead),
-    )
-    ours = (first, rest, m_last)
-    partner = [core_swap(x, n_d) for x in ours]
-
-    mixed, out_left, out_right, out_blocks, _ = call(
+    mixed, out_left, out_right, out_blocks = pl.pallas_call(
         bind(last_kernel),
-        (
-            whole,
-            shape((features, rank_size), BF16),
-            shape((rank_size, quarter), BF16),
-            shape((maxb * SIDE, SIDE), BF16),
-        ),
-        vmem=(low, last_behind, last_ahead, *ours, *partner),
-        scratch=[
-            vm((tok_rows, quarter), BF16),
-            vm((features, rank_size), BF16),
-            vm((rank_size, quarter), BF16),
-            dma((n_d + 6,)),
-        ],
-        mib=32,
-        hbm_outs=4,
-    )
+        out_shape=(whole, *outs),
+        in_specs=[VMEM] * 7 + [HBM] * 3,
+        out_specs=(HBM,) * 4,
+        scratch_shapes=[vm((tok_rows, quarter), BF16), dma((5 * per_chunk,)), dma((4,))],
+        input_output_aliases={7: 1, 8: 2, 9: 3},
+        compiler_params=pltpu.CompilerParams(vmem_limit_bytes=20 << 20),
+    )(low, last_behind, last_ahead, m_last, *(core_swap(x, n_d) for x in (m_last, first, rest)), *grads)
     return (
         mixed.reshape(tok_rows, 1, quarter),
         out_left,

time: 128 us -> 131 us (1.023)
  Pallas kernels: 38.9 us -> 45.3 us
  waiting for transfers between devices: 33.3 us -> 30.9 us
    ppermute x16, waiting for transfers between devices: 12.6 us -> 6.81 us  [shift(): return lax.ppermute(x, axis, [(i, (i + k) % n) for i in range(n)])]
    pallas_call x0 -> x1, Pallas kernels: none -> 3.29 us  [per_device(): pl.pallas_call(bind(last_kernel), out_shape=(whole, *outs), in_specs=[VME...]
    ppermute x9, waiting for transfers between devices: 15.4 us -> 18.5 us  [chip_shift(): return lax.ppermute(x, 'dp', perm)]
    pallas_call x13, Pallas kernels: 37.6 us -> 40.7 us  [call(): pl.pallas_call(body, out_shape=(*outs, shape((1,), jnp.int32)), in_specs=...]
    ppermute x1, starting transfers between devices: 2.29 us -> 0.09 us  [per_device(): left_near = lax.ppermute(left, 'tensor', [(i, i ^ 1) for i in range(n_t)])]
    ppermute x6, starting transfers between devices: 9.98 us -> 11.7 us  [core_swap(): return lax.ppermute(x, 'dp', [(i, i ^ 1) for i in range(n_data)])]
    ppermute x16, starting transfers between devices: 25.2 us -> 23.5 us  [shift(): return lax.ppermute(x, axis, [(i, (i + k) % n) for i in range(n)])]
  transfers between devices with their start and end apart: 33 -> 33, of which waited for: 10 -> 12; matrix products, arithmetic and copies ran while one was open for 0% -> 0% of each run, Pallas kernels for 21% -> 26%
where the time goes in v4:
time: 131 us; the launch traced here: 130 us
  starting transfers between devices  48.1 us (37%)
  Pallas kernels  45.3 us (35%)
  waiting for transfers between devices  30.9 us (24%)
  local copies, waits for them, and re-layouts  4.11 us (3%)
    pallas_call x13, Pallas kernels, call(): pl.pallas_call(body, out_shape=(*outs, shape((1,), jnp.int32)), in_specs=...  40.7 us
    ppermute x16, starting transfers between devices, shift(): return lax.ppermute(x, axis, [(i, (i + k) % n) for i in range(n)])  23.5 us
    ppermute x9, waiting for transfers between devices, chip_shift(): return lax.ppermute(x, 'dp', perm)  18.5 us
    ppermute x6, starting transfers between devices, core_swap(): return lax.ppermute(x, 'dp', [(i, i ^ 1) for i in range(n_data)])  11.7 us
    ppermute x9, starting transfers between devices, chip_shift(): return lax.ppermute(x, 'dp', perm)  10.2 us
    ppermute x16, waiting for transfers between devices, shift(): return lax.ppermute(x, axis, [(i, (i + k) % n) for i in range(n)])  6.81 us
    unnamed x30, local copies, waits for them, and re-layouts  4.07 us
    pallas_call x1, Pallas kernels, per_device(): pl.pallas_call(bind(last_kernel), out_shape=(whole, *outs), in_specs=[VME...  3.29 us
  transfers between devices with their start and end apart: 33, of which 12 were waited for; matrix products, arithmetic and copies ran while one was open for 0% of the time, Pallas kernels for 26%

profile of v4, /device:TPU:1, one launch (start us, length us, event | category | flops | bytes accessed | tf_op | source)
XLA Modules:
  0.0 129.7 jit_solution(3856871125623718603)
XLA Ops:
  2.9 6.8 %shard_map.111 = (f32[640,128]{1,0:T(8,128)S(1)}, bf16[640,128]{1,0:T(8,128)(2,1)S(1)}, f32[640,128]{1,0:T(8,128)S(1)}, bf16[640,128]{1,0:T(8,128)(2,1)S(1)}, bf...) custom-call(s32[16]{0:T(128)S(1)} %copy-done.6, ...), custom_call_target="tpu_custom_call" | custom-call | tf_op jit(solution)/shard_map/pallas_call | solution.py:38
  9.7 3.8 %collective-permute-start.2 = (bf16[640,128]{1,0:T(8,128)(2,1)S(1)}, bf16[640,128]{1,0:T(8,128)(2,1)S(1)}, u32[]{:S(2)}, u32[]{:S(2)}) collective-permute-start(bf16[640,128]{1,0:T(8,128)(2,1)S(1)} %get-tuple-element.61), channel_id=1, source_target_pairs={{0,12},{4,0},{8,4},{12,8},{1,13},{5,1},{9,5},{13,9},{2,14},{6,2},{... | collective-permute-start | bytes 491528 | tf_op jit(solution)/shard_map/ppermute | solution.py:363
  15.9 4.5 %collective-permute-start.7 = (bf16[640,128]{1,0:T(8,128)(2,1)S(1)}, bf16[640,128]{1,0:T(8,128)(2,1)S(1)}, u32[]{:S(2)}, u32[]{:S(2)}) collective-permute-start(bf16[640,128]{1,0:T(8,128)(2,1)S(1)} %get-tuple-element.66), channel_id=1, source_target_pairs={{0,2},{1,3},{2,0},{3,1},{4,6},{5,7},{6,4},{7,5},{8,10},{9,11},{10,... | collective-permute-start | bytes 491528 | tf_op jit(solution)/shard_map/ppermute | solution.py:363
  20.5 4.1 %collective-permute-done = bf16[640,128]{1,0:T(8,128)(2,1)S(1)} collective-permute-done((bf16[640,128]{1,0:T(8,128)(2,1)S(1)}, bf16[640,128]{1,0:T(8,128)(2,1)S(1)}, u32[]{:S(2)}, u32[]{:S(2)}) %collective-permute-start) | collective-permute-done | bytes 163872 | tf_op jit(solution)/shard_map/ppermute | solution.py:363
  26.8 2.6 %collective-permute-start.11 = (bf16[640,128]{1,0:T(8,128)(2,1)S(1)}, bf16[640,128]{1,0:T(8,128)(2,1)S(1)}, u32[]{:S(2)}, u32[]{:S(2)}) collective-permute-start(bf16[640,128]{1,0:T(8,128)(2,1)S(1)} %get-tuple-element.116.refs_5_), channel_id=1, source_target_pairs={{0,12},{4,0},{8,4},{12,8},{1,13},{5,1},{9,5},{13,9},{2,14},{6,2},{... | collective-permute-start | bytes 491528 | tf_op jit(solution)/shard_map/ppermute | solution.py:363
  30.0 3.1 %collective-permute-start.5 = (bf16[640,128]{1,0:T(8,128)(2,1)S(1)}, bf16[640,128]{1,0:T(8,128)(2,1)S(1)}, u32[]{:S(2)}, u32[]{:S(2)}) collective-permute-start(bf16[640,128]{1,0:T(8,128)(2,1)S(1)} %add_convert_fusion.refs_2_.refs_5_), channel_id=1, source_target_pairs={{0,3},{1,0},{2,1},{3,2},{4,7},{5,4},{6,5},{7,6},{8,11},{9,8},{10,9... | collective-permute-start | bytes 491528 | tf_op jit(solution)/shard_map/ppermute | solution.py:363
  35.6 5.9 %shard_map.112 = (f32[4,512,128]{2,1,0:T(8,128)S(1)}, bf16[4,512,128]{2,1,0:T(8,128)(2,1)S(1)}, s32[1]{0:T(128)}) custom-call(s32[16]{0:T(128)S(1)} %copy-done.7, s32[32]{0:T(128)S(1)} %copy-done.9, s32[32]{0:T(128)S(1)} %copy-done.11, bf16[640,2048]{1,0:T(8,128)(2,1)S(1)} %copy-done, bf16[640,7168]{1,0:T(8,128)(2,1)S(1)} %bitcast.5, ...), custom_call_target="tpu_custom_call" | custom-call | tf_op jit(solution)/shard_map/pallas_call | solution.py:38
  42.9 2.0 %collective-permute-start.18 = (bf16[320,1792]{1,0:T(8,128)(2,1)S(1)}, bf16[320,1792]{1,0:T(8,128)(2,1)S(1)}, u32[]{:S(2)}, u32[]{:S(2)}) collective-permute-start(bf16[320,1792]{1,0:T(8,128)(2,1)S(1)} %get-tuple-element.88), channel_id=1, source_target_pairs={{0,4},{4,8},{8,12},{12,0},{1,5},{5,9},{9,13},{13,1},{2,6},{6,10},{... | collective-permute-start | bytes 3440648 | tf_op jit(solution)/shard_map/ppermute | solution.py:363
  44.9 1.8 %collective-permute-start.19 = (bf16[320,1792]{1,0:T(8,128)(2,1)S(1)}, bf16[320,1792]{1,0:T(8,128)(2,1)S(1)}, u32[]{:S(2)}, u32[]{:S(2)}) collective-permute-start(bf16[320,1792]{1,0:T(8,128)(2,1)S(1)} %get-tuple-element.89), channel_id=1, source_target_pairs={{0,12},{4,0},{8,4},{12,8},{1,13},{5,1},{9,5},{13,9},{2,14},{6,2},{... | collective-permute-start | bytes 3440648 | tf_op jit(solution)/shard_map/ppermute | solution.py:363
  46.7 4.8 %shard_map.114 = (f32[4,1664,128]{2,1,0:T(8,128)S(1)}, bf16[2224,128]{1,0:T(8,128)(2,1)S(1)}, bf16[2224,128]{1,0:T(8,128)(2,1)S(1)}, bf16[2208,128]{1,0:T(8,128)(2,1)S(1)}, s32[1]{0:T(128)}) custom-call(bf16[640,2048]{1,0:T(8,128)(2,1)S(1)} %copy-done.1, bf16[640,7168]{1,0:T(8,128)(2,1)} %refs_1_.7, bf16[640,128]{1,0:T(8,128)(2,1)S(1)} %add_convert_fusion.refs_2_.refs_5_, ...), custom_call_target="tpu_custom_call" | custom-call | tf_op jit(solution)/shard_map/pallas_call | solution.py:38
  51.5 5.2 %collective-permute-start.12 = (bf16[2224,128]{1,0:T(8,128)(2,1)S(1)}, bf16[2224,128]{1,0:T(8,128)(2,1)S(1)}, u32[]{:S(2)}, u32[]{:S(2)}) collective-permute-start(bf16[2224,128]{1,0:T(8,128)(2,1)S(1)} %get-tuple-element.76), channel_id=1, source_target_pairs={{0,16},{16,0},{32,48},{48,32},{64,80},{80,64},{96,112},{112,96},{1... | collective-permute-start | bytes 1708040 | tf_op jit(solution)/shard_map/ppermute | solution.py:373
  57.1 5.1 %shard_map.115 = (bf16[640,1792]{1,0:T(8,128)(2,1)S(1)}, bf16[640,1792]{1,0:T(8,128)(2,1)S(1)}, s32[1]{0:T(128)}) custom-call(s32[16]{0:T(128)S(1)} %copy-done.7, s32[32]{0:T(128)S(1)} %copy-done.9, s32[32]{0:T(128)S(1)} %copy-done.11, bf16[640,2048]{1,0:T(8,128)(2,1)S(1)} %copy-done.1, bf16[32,128,128]{2,1,0:T(8,128)(2,1)S(1)} %copy-done.2, ...), custom_call_target="tpu_custom_call" | custom-call | tf_op jit(solution)/shard_map/pallas_call | solution.py:38
  69.5 2.6 %collective-permute-start.25 = (bf16[640,1792]{1,0:T(8,128)(2,1)S(1)}, bf16[640,1792]{1,0:T(8,128)(2,1)S(1)}, u32[]{:S(2)}, u32[]{:S(2)}) collective-permute-start(bf16[640,1792]{1,0:T(8,128)(2,1)S(1)} %get-tuple-element.101), channel_id=1, source_target_pairs={{0,12},{4,0},{8,4},{12,8},{1,13},{5,1},{9,5},{13,9},{2,14},{6,2},{... | collective-permute-start | bytes 6881288 | tf_op jit(solution)/shard_map/ppermute | solution.py:363
  72.2 6.7 %collective-permute-done.17.refs_4_ = bf16[256,128]{1,0:T(8,128)(2,1)S(1)} collective-permute-done((bf16[256,128]{1,0:T(8,128)(2,1)S(1)}, bf16[256,128]{1,0:T(8,128)(2,1)S(1)}, u32[]{:S(2)}, u32[]{:S(2)}) %collective-permute-start.17) | collective-permute-done | bytes 65568 | tf_op jit(solution)/shard_map/ppermute | solution.py:369
  80.7 2.4 %collective-permute-start.21 = (bf16[704,128]{1,0:T(8,128)(2,1)S(1)}, bf16[704,128]{1,0:T(8,128)(2,1)S(1)}, u32[]{:S(2)}, u32[]{:S(2)}) collective-permute-start(bf16[704,128]{1,0:T(8,128)(2,1)S(1)} %get-tuple-element.93), channel_id=1, source_target_pairs={{0,96},{16,112},{32,0},{48,16},{64,32},{80,48},{96,64},{112,80},{1... | collective-permute-start | bytes 540680 | tf_op jit(solution)/shard_map/ppermute | solution.py:369
  84.9 2.6 %collective-permute-start.23 = (bf16[512,128]{1,0:T(8,128)(2,1)S(1)}, bf16[512,128]{1,0:T(8,128)(2,1)S(1)}, u32[]{:S(2)}, u32[]{:S(2)}) collective-permute-start(bf16[512,128]{1,0:T(8,128)(2,1)S(1)} %get-tuple-element.96.refs_5_), channel_id=1, source_target_pairs={{0,3},{1,2},{2,1},{3,0},{4,7},{5,6},{6,5},{7,4},{8,11},{9,10},{10,... | collective-permute-start | bytes 393224 | tf_op jit(solution)/shard_map/ppermute | solution.py:523
  87.6 2.8 %collective-permute-done.23.refs_6_ = bf16[512,128]{1,0:T(8,128)(2,1)S(1)} collective-permute-done((bf16[512,128]{1,0:T(8,128)(2,1)S(1)}, bf16[512,128]{1,0:T(8,128)(2,1)S(1)}, u32[]{:S(2)}, u32[]{:S(2)}) %collective-permute-start.23) | collective-permute-done | bytes 131104 | tf_op jit(solution)/shard_map/ppermute | solution.py:523
  93.1 6.1 %shard_map.121 = (f32[640,1792]{1,0:T(8,128)S(1)}, s32[1]{0:T(128)}) custom-call(s32[16]{0:T(128)S(1)} %copy-done.7, s32[32]{0:T(128)S(1)} %copy-done.9, s32[32]{0:T(128)S(1)} %copy-done.11, bf16[640,2048]{1,0:T(8,128)(2,1)S(1)} %copy-done.1, bf16[32,128,128]{2,1,0:T(8,128)(2,1)S(1)} %copy-done.2, bf16[640,128]{1,0:T(8,128)(2,1)S(1)} %add_convert_fusion.refs_2_.refs_5_, ...), custom_call_target="tpu_custom_call" | custom-call | tf_op jit(solution)/shard_map/pallas_call | solution.py:38
  99.2 5.4 %collective-permute-done.28.refs_2_ = bf16[2432,128]{1,0:T(8,128)(2,1)S(1)} collective-permute-done((bf16[2432,128]{1,0:T(8,128)(2,1)S(1)}, bf16[2432,128]{1,0:T(8,128)(2,1)S(1)}, u32[]{:S(2)}, u32[]{:S(2)}) %collective-permute-start.28) | collective-permute-done | bytes 622624 | tf_op jit(solution)/shard_map/ppermute | solution.py:369
  106.7 4.7 %collective-permute-start.31 = (bf16[5632,128]{1,0:T(8,128)(2,1)S(1)}, bf16[5632,128]{1,0:T(8,128)(2,1)S(1)}, u32[]{:S(2)}, u32[]{:S(2)}) collective-permute-start(bf16[5632,128]{1,0:T(8,128)(2,1)S(1)} %get-tuple-element.104.refs_0_), channel_id=1, source_target_pairs={{0,16},{16,0},{32,48},{48,32},{64,80},{80,64},{96,112},{112,96},{1... | collective-permute-start | bytes 4325384 | tf_op jit(solution)/shard_map/ppermute | solution.py:373
  113.1 2.9 %shard_map.123 = (bf16[2048,512]{1,0:T(8,128)(2,1)}, bf16[512,1792]{1,0:T(8,128)(2,1)}, bf16[4096,128]{1,0:T(8,128)(2,1)}, s32[1]{0:T(128)}) custom-call(bf16[5632,128]{1,0:T(8,128)(2,1)S(1)} %get-tuple-element.104.refs_0_, bf16[1664,128]{1,0:T(8,128)(2,1)S(1)} %get-tuple-element.105.refs_1_, s32[1]{0:T(128)} %get-tuple-element.106.refs_2_), custom_call_target="tpu_custom_call" | custom-call | tf_op jit(solution)/shard_map/pallas_call | solution.py:38
  116.0 4.5 %collective-permute-done.29.refs_1_ = bf16[1216,128]{1,0:T(8,128)(2,1)S(1)} collective-permute-done((bf16[1216,128]{1,0:T(8,128)(2,1)S(1)}, bf16[1216,128]{1,0:T(8,128)(2,1)S(1)}, u32[]{:S(2)}, u32[]{:S(2)}) %collective-permute-start.29) | collective-permute-done | bytes 311328 | tf_op jit(solution)/shard_map/ppermute | solution.py:369
  124.0 2.2 %collective-permute-done.32.refs_6_ = bf16[1664,128]{1,0:T(8,128)(2,1)S(1)} collective-permute-done((bf16[1664,128]{1,0:T(8,128)(2,1)S(1)}, bf16[1664,128]{1,0:T(8,128)(2,1)S(1)}, u32[]{:S(2)}, u32[]{:S(2)}) %collective-permute-start.32) | collective-permute-done | bytes 426016 | tf_op jit(solution)/shard_map/ppermute | solution.py:373
  126.3 3.3 %shard_map.125 = (bf16[640,1792]{1,0:T(8,128)(2,1)}, bf16[2048,512]{1,0:T(8,128)(2,1)}, bf16[512,1792]{1,0:T(8,128)(2,1)}, bf16[4096,128]{1,0:T(8,128)(2,1)}) custom-call(f32[640,1792]{1,0:T(8,128)S(1)} %get-tuple-element.99.refs_0_, ...), custom_call_target="tpu_custom_call", output_to_operand_aliasing={{1}: (7, {}), {2}: (8, {}), {3}: (9, {})} | custom-call | tf_op jit(solution)/shard_map/pallas_call | solution.py:571
  (92 shorter events, 32.6 us)
Async XLA Ops:
  9.7 10.7 %collective-permute-start.2 = (bf16[640,128]{1,0:T(8,128)(2,1)S(1)}, bf16[640,128]{1,0:T(8,128)(2,1)S(1)}, u32[]{:S(2)}, u32[]{:S(2)}) collective-permute-start(bf16[640,128]{1,0:T(8,128)(2,1)S(1)} %get-tuple-element.61), channel_id=1, source_target_pairs={{0,12},{4,0},{8,4},{12,8},{1,13},{5,1},{9,5},{13,9},{2,14},{6,2},{... | collective-permute-start | bytes 491528 | tf_op jit(solution)/shard_map/ppermute | solution.py:363
  14.6 10.0 %collective-permute-start = (bf16[640,128]{1,0:T(8,128)(2,1)S(1)}, bf16[640,128]{1,0:T(8,128)(2,1)S(1)}, u32[]{:S(2)}, u32[]{:S(2)}) collective-permute-start(bf16[640,128]{1,0:T(8,128)(2,1)S(1)} %get-tuple-element.61), channel_id=1, source_target_pairs={{0,4},{4,8},{8,12},{12,0},{1,5},{5,9},{9,13},{13,1},{2,6},{6,10},{... | collective-permute-start | bytes 491528 | tf_op jit(solution)/shard_map/ppermute | solution.py:363
  14.6 10.1 %collective-permute-start.6 = (bf16[640,128]{1,0:T(8,128)(2,1)S(1)}, bf16[640,128]{1,0:T(8,128)(2,1)S(1)}, u32[]{:S(2)}, u32[]{:S(2)}) collective-permute-start(bf16[640,128]{1,0:T(8,128)(2,1)S(1)} %get-tuple-element.65), channel_id=1, source_target_pairs={{0,1},{1,2},{2,3},{3,0},{4,5},{5,6},{6,7},{7,4},{8,9},{9,10},{10,1... | collective-permute-start | bytes 491528 | tf_op jit(solution)/shard_map/ppermute | solution.py:363
  15.9 10.5 %collective-permute-start.7 = (bf16[640,128]{1,0:T(8,128)(2,1)S(1)}, bf16[640,128]{1,0:T(8,128)(2,1)S(1)}, u32[]{:S(2)}, u32[]{:S(2)}) collective-permute-start(bf16[640,128]{1,0:T(8,128)(2,1)S(1)} %get-tuple-element.66), channel_id=1, source_target_pairs={{0,2},{1,3},{2,0},{3,1},{4,6},{5,7},{6,4},{7,5},{8,10},{9,11},{10,... | collective-permute-start | bytes 491528 | tf_op jit(solution)/shard_map/ppermute | solution.py:363
  26.8 7.0 %collective-permute-start.11 = (bf16[640,128]{1,0:T(8,128)(2,1)S(1)}, bf16[640,128]{1,0:T(8,128)(2,1)S(1)}, u32[]{:S(2)}, u32[]{:S(2)}) collective-permute-start(bf16[640,128]{1,0:T(8,128)(2,1)S(1)} %get-tuple-element.116.refs_5_), channel_id=1, source_target_pairs={{0,12},{4,0},{8,4},{12,8},{1,13},{5,1},{9,5},{13,9},{2,14},{6,2},{... | collective-permute-start | bytes 491528 | tf_op jit(solution)/shard_map/ppermute | solution.py:363
  29.3 12.2 %collective-permute-start.10 = (bf16[640,128]{1,0:T(8,128)(2,1)S(1)}, bf16[640,128]{1,0:T(8,128)(2,1)S(1)}, u32[]{:S(2)}, u32[]{:S(2)}) collective-permute-start(bf16[640,128]{1,0:T(8,128)(2,1)S(1)} %get-tuple-element.116.refs_5_), channel_id=1, source_target_pairs={{0,8},{4,12},{8,0},{12,4},{1,9},{5,13},{9,1},{13,5},{2,10},{6,14},... | collective-permute-start | bytes 491528 | tf_op jit(solution)/shard_map/ppermute | solution.py:363
  29.3 12.2 %collective-permute-start.9 = (bf16[640,128]{1,0:T(8,128)(2,1)S(1)}, bf16[640,128]{1,0:T(8,128)(2,1)S(1)}, u32[]{:S(2)}, u32[]{:S(2)}) collective-permute-start(bf16[640,128]{1,0:T(8,128)(2,1)S(1)} %get-tuple-element.116.refs_5_), channel_id=1, source_target_pairs={{0,4},{4,8},{8,12},{12,0},{1,5},{5,9},{9,13},{13,1},{2,6},{6,10},{... | collective-permute-start | bytes 491528 | tf_op jit(solution)/shard_map/ppermute | solution.py:363
  30.0 11.5 %collective-permute-start.5 = (bf16[640,128]{1,0:T(8,128)(2,1)S(1)}, bf16[640,128]{1,0:T(8,128)(2,1)S(1)}, u32[]{:S(2)}, u32[]{:S(2)}) collective-permute-start(bf16[640,128]{1,0:T(8,128)(2,1)S(1)} %add_convert_fusion.refs_2_.refs_5_), channel_id=1, source_target_pairs={{0,3},{1,0},{2,1},{3,2},{4,7},{5,4},{6,5},{7,6},{8,11},{9,8},{10,9... | collective-permute-start | bytes 491528 | tf_op jit(solution)/shard_map/ppermute | solution.py:363
  33.1 8.4 %collective-permute-start.4 = (bf16[640,128]{1,0:T(8,128)(2,1)S(1)}, bf16[640,128]{1,0:T(8,128)(2,1)S(1)}, u32[]{:S(2)}, u32[]{:S(2)}) collective-permute-start(bf16[640,128]{1,0:T(8,128)(2,1)S(1)} %add_convert_fusion.refs_2_.refs_5_), channel_id=1, source_target_pairs={{0,2},{1,3},{2,0},{3,1},{4,6},{5,7},{6,4},{7,5},{8,10},{9,11},{10,... | collective-permute-start | bytes 491528 | tf_op jit(solution)/shard_map/ppermute | solution.py:363
  33.8 7.8 %collective-permute-start.3 = (bf16[640,128]{1,0:T(8,128)(2,1)S(1)}, bf16[640,128]{1,0:T(8,128)(2,1)S(1)}, u32[]{:S(2)}, u32[]{:S(2)}) collective-permute-start(bf16[640,128]{1,0:T(8,128)(2,1)S(1)} %add_convert_fusion.refs_2_.refs_5_), channel_id=1, source_target_pairs={{0,1},{1,2},{2,3},{3,0},{4,5},{5,6},{6,7},{7,4},{8,9},{9,10},{10,1... | collective-permute-start | bytes 491528 | tf_op jit(solution)/shard_map/ppermute | solution.py:363
  42.9 25.2 %collective-permute-start.18 = (bf16[320,1792]{1,0:T(8,128)(2,1)S(1)}, bf16[320,1792]{1,0:T(8,128)(2,1)S(1)}, u32[]{:S(2)}, u32[]{:S(2)}) collective-permute-start(bf16[320,1792]{1,0:T(8,128)(2,1)S(1)} %get-tuple-element.88), channel_id=1, source_target_pairs={{0,4},{4,8},{8,12},{12,0},{1,5},{5,9},{9,13},{13,1},{2,6},{6,10},{... | collective-permute-start | bytes 3440648 | tf_op jit(solution)/shard_map/ppermute | solution.py:363
  44.9 23.2 %collective-permute-start.19 = (bf16[320,1792]{1,0:T(8,128)(2,1)S(1)}, bf16[320,1792]{1,0:T(8,128)(2,1)S(1)}, u32[]{:S(2)}, u32[]{:S(2)}) collective-permute-start(bf16[320,1792]{1,0:T(8,128)(2,1)S(1)} %get-tuple-element.89), channel_id=1, source_target_pairs={{0,12},{4,0},{8,4},{12,8},{1,13},{5,1},{9,5},{13,9},{2,14},{6,2},{... | collective-permute-start | bytes 3440648 | tf_op jit(solution)/shard_map/ppermute | solution.py:363
  51.5 10.8 %collective-permute-start.12 = (bf16[2224,128]{1,0:T(8,128)(2,1)S(1)}, bf16[2224,128]{1,0:T(8,128)(2,1)S(1)}, u32[]{:S(2)}, u32[]{:S(2)}) collective-permute-start(bf16[2224,128]{1,0:T(8,128)(2,1)S(1)} %get-tuple-element.76), channel_id=1, source_target_pairs={{0,16},{16,0},{32,48},{48,32},{64,80},{80,64},{96,112},{112,96},{1... | collective-permute-start | bytes 1708040 | tf_op jit(solution)/shard_map/ppermute | solution.py:373
  63.8 15.1 %collective-permute-start.15 = (bf16[1664,128]{1,0:T(8,128)(2,1)S(1)}, bf16[1664,128]{1,0:T(8,128)(2,1)S(1)}, u32[]{:S(2)}, u32[]{:S(2)}) collective-permute-start(bf16[1664,128]{1,0:T(8,128)(2,1)S(1)} %get-tuple-element.82), channel_id=1, source_target_pairs={{0,32},{16,48},{32,64},{48,80},{64,96},{80,112},{96,0},{112,16},{1... | collective-permute-start | bytes 1277960 | tf_op jit(solution)/shard_map/ppermute | solution.py:369
  65.1 13.7 %collective-permute-start.16 = (bf16[1664,128]{1,0:T(8,128)(2,1)S(1)}, bf16[1664,128]{1,0:T(8,128)(2,1)S(1)}, u32[]{:S(2)}, u32[]{:S(2)}) collective-permute-start(bf16[1664,128]{1,0:T(8,128)(2,1)S(1)} %get-tuple-element.83), channel_id=1, source_target_pairs={{0,96},{16,112},{32,0},{48,16},{64,32},{80,48},{96,64},{112,80},{1... | collective-permute-start | bytes 1277960 | tf_op jit(solution)/shard_map/ppermute | solution.py:369
  66.6 12.3 %collective-permute-start.17 = (bf16[256,128]{1,0:T(8,128)(2,1)S(1)}, bf16[256,128]{1,0:T(8,128)(2,1)S(1)}, u32[]{:S(2)}, u32[]{:S(2)}) collective-permute-start(bf16[256,128]{1,0:T(8,128)(2,1)S(1)} %get-tuple-element.85), channel_id=1, source_target_pairs={{0,64},{16,80},{32,96},{48,112},{64,0},{80,16},{96,32},{112,48},{1... | collective-permute-start | bytes 196616 | tf_op jit(solution)/shard_map/ppermute | solution.py:369
  69.4 56.8 %collective-permute-start.24 = (bf16[640,1792]{1,0:T(8,128)(2,1)S(1)}, bf16[640,1792]{1,0:T(8,128)(2,1)S(1)}, u32[]{:S(2)}, u32[]{:S(2)}) collective-permute-start(bf16[640,1792]{1,0:T(8,128)(2,1)S(1)} %get-tuple-element.100), channel_id=1, source_target_pairs={{0,4},{4,8},{8,12},{12,0},{1,5},{5,9},{9,13},{13,1},{2,6},{6,10},{... | collective-permute-start | bytes 6881288 | tf_op jit(solution)/shard_map/ppermute | solution.py:363
  69.5 56.7 %collective-permute-start.25 = (bf16[640,1792]{1,0:T(8,128)(2,1)S(1)}, bf16[640,1792]{1,0:T(8,128)(2,1)S(1)}, u32[]{:S(2)}, u32[]{:S(2)}) collective-permute-start(bf16[640,1792]{1,0:T(8,128)(2,1)S(1)} %get-tuple-element.101), channel_id=1, source_target_pairs={{0,12},{4,0},{8,4},{12,8},{1,13},{5,1},{9,5},{13,9},{2,14},{6,2},{... | collective-permute-start | bytes 6881288 | tf_op jit(solution)/shard_map/ppermute | solution.py:363
  80.3 7.2 %collective-permute-start.20 = (bf16[704,128]{1,0:T(8,128)(2,1)S(1)}, bf16[704,128]{1,0:T(8,128)(2,1)S(1)}, u32[]{:S(2)}, u32[]{:S(2)}) collective-permute-start(bf16[704,128]{1,0:T(8,128)(2,1)S(1)} %get-tuple-element.92), channel_id=1, source_target_pairs={{0,32},{16,48},{32,64},{48,80},{64,96},{80,112},{96,0},{112,16},{1... | collective-permute-start | bytes 540680 | tf_op jit(solution)/shard_map/ppermute | solution.py:369
  91.6 13.0 %collective-permute-start.28 = (bf16[2432,128]{1,0:T(8,128)(2,1)S(1)}, bf16[2432,128]{1,0:T(8,128)(2,1)S(1)}, u32[]{:S(2)}, u32[]{:S(2)}) collective-permute-start(bf16[2432,128]{1,0:T(8,128)(2,1)S(1)} %get-tuple-element.102.refs_0_), channel_id=1, source_target_pairs={{0,96},{16,112},{32,0},{48,16},{64,32},{80,48},{96,64},{112,80},{1... | collective-permute-start | bytes 1867784 | tf_op jit(solution)/shard_map/ppermute | solution.py:369
  92.5 13.0 %collective-permute-start.26 = (bf16[2432,128]{1,0:T(8,128)(2,1)S(1)}, bf16[2432,128]{1,0:T(8,128)(2,1)S(1)}, u32[]{:S(2)}, u32[]{:S(2)}) collective-permute-start(bf16[2432,128]{1,0:T(8,128)(2,1)S(1)} %get-tuple-element.102.refs_0_), channel_id=1, source_target_pairs={{0,32},{16,48},{32,64},{48,80},{64,96},{80,112},{96,0},{112,16},{1... | collective-permute-start | bytes 1867784 | tf_op jit(solution)/shard_map/ppermute | solution.py:369
  106.7 19.5 %collective-permute-start.31 = (bf16[5632,128]{1,0:T(8,128)(2,1)S(1)}, bf16[5632,128]{1,0:T(8,128)(2,1)S(1)}, u32[]{:S(2)}, u32[]{:S(2)}) collective-permute-start(bf16[5632,128]{1,0:T(8,128)(2,1)S(1)} %get-tuple-element.104.refs_0_), channel_id=1, source_target_pairs={{0,16},{16,0},{32,48},{48,32},{64,80},{80,64},{96,112},{112,96},{1... | collective-permute-start | bytes 4325384 | tf_op jit(solution)/shard_map/ppermute | solution.py:373
  111.5 9.0 %collective-permute-start.29 = (bf16[1216,128]{1,0:T(8,128)(2,1)S(1)}, bf16[1216,128]{1,0:T(8,128)(2,1)S(1)}, u32[]{:S(2)}, u32[]{:S(2)}) collective-permute-start(bf16[1216,128]{1,0:T(8,128)(2,1)S(1)} %slice.9), channel_id=1, source_target_pairs={{0,96},{16,112},{32,0},{48,16},{64,32},{80,48},{96,64},{112,80},{1... | collective-permute-start | bytes 933896 | tf_op jit(solution)/shard_map/ppermute | solution.py:369
  111.6 10.0 %collective-permute-start.27 = (bf16[1216,128]{1,0:T(8,128)(2,1)S(1)}, bf16[1216,128]{1,0:T(8,128)(2,1)S(1)}, u32[]{:S(2)}, u32[]{:S(2)}) collective-permute-start(bf16[1216,128]{1,0:T(8,128)(2,1)S(1)} %slice.8), channel_id=1, source_target_pairs={{0,32},{16,48},{32,64},{48,80},{64,96},{80,112},{96,0},{112,16},{1... | collective-permute-start | bytes 933896 | tf_op jit(solution)/shard_map/ppermute | solution.py:369
  (24 other events, 259.1 us)

commit v5 on v4

--- a/solution.py
+++ b/solution.py
@@ -57,6 +57,14 @@
 
     def live(self, counts):
         return counts[self.f * self.n_t + self.t]
+
+
+class Part:
+    def __init__(self, ref, start):
+        self.ref, self.start = ref, start
+
+    def __getitem__(self, i):
+        return self.ref[self.start + i]
 
 
 def fetch(*pairs_and_sems):
@@ -136,7 +144,7 @@
     p3[...] = acc[1].astype(BF16)
 
 
-def blocks_kernel(place, counts, rows, cols, tok, cot, _, mine, theirs):
+def blocks_kernel(place, _q, counts, rows, cols, tok, cot, _, mine, theirs):
     live = place.live(counts)
     per = mine.shape[1] // SIDE
 
@@ -387,11 +395,18 @@
     rank_size, quarter = right.shape
     q_blocks = quarter // SIDE
     half = tok_rows // 2
-    lists = (block_counts, block_rows, block_cols)
+    lists = (jnp.concatenate([block_counts, block_rows, block_cols]),)
+    n_owners = block_counts.shape[0]
     vm, dma = pltpu.VMEM, pltpu.SemaphoreType.DMA
 
     def bind(kernel, *args):
         return lambda *refs: kernel(place, *args, *refs)
+
+    def listed(kernel):
+        parts = (0, n_owners, n_owners + maxb)
+        return lambda ints, *refs: kernel(
+            place, q_blocks, *(Part(ints, start) for start in parts), *refs
+        )
 
     def over(n, k_shift):
         return [k_shift(k) for k in range(1, n)]
@@ -399,7 +414,7 @@
     wide, narrow = shape((tok_rows, SIDE), F32), shape((tok_rows, SIDE), BF16)
     part, whole = shape((half, quarter), BF16), shape((tok_rows, quarter), BF16)
     rank, rank_low, back, *back_out, ahead, behind, step = call(
-        bind(front_kernel, q_blocks),
+        listed(front_kernel),
         (wide, narrow, wide, narrow, narrow, narrow, part, part),
         smem=lists,
         hbm=(tokens, left_factor, cotangent, right, block_values),
@@ -422,7 +437,7 @@
 
     for x in rank_in:
         rank = rank + x.astype(F32)
-    rank, back = lax.optimization_barrier((rank.astype(BF16), back))
+    rank = rank.astype(BF16)
     ranks = [rank] + over(n_t, lambda k: shift(rank, "tensor", n_t, k))
     for x in back_in:
         back = back + x.astype(F32)
@@ -431,7 +446,7 @@
 
     n_b = maxb // n_d * SIDE
     blocks_mine, blocks_theirs, step = call(
-        bind(blocks_kernel),
+        listed(blocks_kernel),
         (shape((chips, n_b, SIDE), F32), shape((chips, n_b, SIDE), BF16)),
         smem=lists,
         vmem=(tokens, cotangent, back_low),
@@ -478,7 +493,7 @@
     )
     got = [core_swap(x, n_d) for x in theirs]
     p1, p3, step = call(
-        bind(residual_kernel, q_blocks),
+        listed(residual_kernel),
         (whole, whole),
         smem=lists,
         vmem=(tokens, block_values),
@@ -534,7 +549,7 @@
     m_last_behind = chip_shift(m_behind[: n_msg // 2], n_d, 1)
     m_last_ahead = chip_shift(m_ahead[n_msg // 2 :], n_d, -1)
     low, step = call(
-        bind(low_kernel, q_blocks),
+        listed(low_kernel),
         (shape((tok_rows, quarter), F32),),
         smem=lists,
         vmem=(tokens, block_values, *ranks, right),

time: 131 us -> 126 us (0.962)
  Pallas kernels: 45.3 us -> 41.3 us
  starting transfers between devices: 48.1 us -> 50.8 us
  local copies, waits for them, and re-layouts: 4.11 us -> 1.81 us
  waiting for transfers between devices: 30.9 us -> 28.9 us
    ppermute x9, waiting for transfers between devices: 18.5 us -> 13.5 us  [chip_shift(): return lax.ppermute(x, 'dp', perm)]
    pallas_call x13, Pallas kernels: 40.7 us -> 36.7 us  [call(): pl.pallas_call(body, out_shape=(*outs, shape((1,), jnp.int32)), in_specs=...]
    ppermute x16, waiting for transfers between devices: 6.81 us -> 10.5 us  [shift(): return lax.ppermute(x, axis, [(i, (i + k) % n) for i in range(n)])]
    ppermute x6, starting transfers between devices: 11.7 us -> 9.15 us  [core_swap(): return lax.ppermute(x, 'dp', [(i, i ^ 1) for i in range(n_data)])]
    unnamed x30 -> x18, local copies, waits for them, and re-layouts: 4.07 us -> 1.77 us
    ppermute x16, starting transfers between devices: 23.5 us -> 25.6 us  [shift(): return lax.ppermute(x, axis, [(i, (i + k) % n) for i in range(n)])]
    ppermute x1, starting transfers between devices: 0.09 us -> 1.75 us  [per_device(): left_near = lax.ppermute(left, 'tensor', [(i, i ^ 1) for i in range(n_t)])]
    ppermute x1, starting transfers between devices: 2.64 us -> 4.26 us  [per_device(): lax.ppermute(left_pair, 'tensor', [(i, n_t - 1 - i) for i in range(n_t)])]
  transfers between devices with their start and end apart: 33 -> 33, of which waited for: 12 -> 9; matrix products, arithmetic and copies ran while one was open for 0% -> 0% of each run, Pallas kernels for 26% -> 24%
where the time goes in v5:
time: 126 us; the launch traced here: 125 us
  starting transfers between devices  50.8 us (40%)
  Pallas kernels  41.3 us (33%)
  waiting for transfers between devices  28.9 us (23%)
  local copies, waits for them, and re-layouts  1.81 us (1%)
    pallas_call x13, Pallas kernels, call(): pl.pallas_call(body, out_shape=(*outs, shape((1,), jnp.int32)), in_specs=...  36.7 us
    ppermute x16, starting transfers between devices, shift(): return lax.ppermute(x, axis, [(i, (i + k) % n) for i in range(n)])  25.6 us
    ppermute x9, waiting for transfers between devices, chip_shift(): return lax.ppermute(x, 'dp', perm)  13.5 us
    ppermute x16, waiting for transfers between devices, shift(): return lax.ppermute(x, axis, [(i, (i + k) % n) for i in range(n)])  10.5 us
    ppermute x9, starting transfers between devices, chip_shift(): return lax.ppermute(x, 'dp', perm)  10.1 us
    ppermute x6, starting transfers between devices, core_swap(): return lax.ppermute(x, 'dp', [(i, i ^ 1) for i in range(n_data)])  9.15 us
    ppermute x1, starting transfers between devices, per_device(): lax.ppermute(left_pair, 'tensor', [(i, n_t - 1 - i) for i in range(n_t)])  4.26 us
    pallas_call x1, Pallas kernels, per_device(): pl.pallas_call(bind(last_kernel), out_shape=(whole, *outs), in_specs=[VME...  3.29 us
  transfers between devices with their start and end apart: 33, of which 9 were waited for; matrix products, arithmetic and copies ran while one was open for 0% of the time, Pallas kernels for 24%

profile of v5, /device:TPU:1, one launch (start us, length us, event | category | flops | bytes accessed | tf_op | source)
XLA Modules:
  0.0 124.8 jit_solution(16577125024200254316)
XLA Ops:
  1.4 6.4 %shard_map.111 = (f32[640,128]{1,0:T(8,128)S(1)}, bf16[640,128]{1,0:T(8,128)(2,1)S(1)}, f32[640,128]{1,0:T(8,128)S(1)}, bf16[640,128]{1,0:T(8,128)(2,1)S(1)}, bf...) custom-call(s32[80]{0:T(128)S(1)} %pad_add_fusion.refs_0_, ...), custom_call_target="tpu_custom_call" | custom-call | tf_op jit(solution)/shard_map/pallas_call | solution.py:38
  7.8 2.5 %collective-permute-start.6 = (bf16[640,128]{1,0:T(8,128)(2,1)S(1)}, bf16[640,128]{1,0:T(8,128)(2,1)S(1)}, u32[]{:S(2)}, u32[]{:S(2)}) collective-permute-start(bf16[640,128]{1,0:T(8,128)(2,1)S(1)} %get-tuple-element.61), channel_id=1, source_target_pairs={{0,1},{1,2},{2,3},{3,0},{4,5},{5,6},{6,7},{7,4},{8,9},{9,10},{10,1... | collective-permute-start | bytes 491528 | tf_op jit(solution)/shard_map/ppermute | solution.py:371
  10.4 3.4 %collective-permute-start.7 = (bf16[640,128]{1,0:T(8,128)(2,1)S(1)}, bf16[640,128]{1,0:T(8,128)(2,1)S(1)}, u32[]{:S(2)}, u32[]{:S(2)}) collective-permute-start(bf16[640,128]{1,0:T(8,128)(2,1)S(1)} %get-tuple-element.62), channel_id=1, source_target_pairs={{0,2},{1,3},{2,0},{3,1},{4,6},{5,7},{6,4},{7,5},{8,10},{9,11},{10,... | collective-permute-start | bytes 491528 | tf_op jit(solution)/shard_map/ppermute | solution.py:371
  15.2 2.8 %collective-permute-start.2 = (bf16[640,128]{1,0:T(8,128)(2,1)S(1)}, bf16[640,128]{1,0:T(8,128)(2,1)S(1)}, u32[]{:S(2)}, u32[]{:S(2)}) collective-permute-start(bf16[640,128]{1,0:T(8,128)(2,1)S(1)} %get-tuple-element.59), channel_id=1, source_target_pairs={{0,12},{4,0},{8,4},{12,8},{1,13},{5,1},{9,5},{13,9},{2,14},{6,2},{... | collective-permute-start | bytes 491528 | tf_op jit(solution)/shard_map/ppermute | solution.py:371
  19.1 1.8 %collective-permute-done.7 = bf16[640,128]{1,0:T(8,128)(2,1)S(1)} collective-permute-done((bf16[640,128]{1,0:T(8,128)(2,1)S(1)}, bf16[640,128]{1,0:T(8,128)(2,1)S(1)}, u32[]{:S(2)}, u32[]{:S(2)}) %collective-permute-start.7) | collective-permute-done | bytes 163872 | tf_op jit(solution)/shard_map/ppermute | solution.py:371
  21.0 3.3 %collective-permute-start.11 = (bf16[640,128]{1,0:T(8,128)(2,1)S(1)}, bf16[640,128]{1,0:T(8,128)(2,1)S(1)}, u32[]{:S(2)}, u32[]{:S(2)}) collective-permute-start(bf16[640,128]{1,0:T(8,128)(2,1)S(1)} %get-tuple-element.112.refs_3_), channel_id=1, source_target_pairs={{0,12},{4,0},{8,4},{12,8},{1,13},{5,1},{9,5},{13,9},{2,14},{6,2},{... | collective-permute-start | bytes 491528 | tf_op jit(solution)/shard_map/ppermute | solution.py:371
  25.4 2.7 %collective-permute-done = bf16[640,128]{1,0:T(8,128)(2,1)S(1)} collective-permute-done((bf16[640,128]{1,0:T(8,128)(2,1)S(1)}, bf16[640,128]{1,0:T(8,128)(2,1)S(1)}, u32[]{:S(2)}, u32[]{:S(2)}) %collective-permute-start) | collective-permute-done | bytes 163872 | tf_op jit(solution)/shard_map/ppermute | solution.py:371
  28.6 2.3 %collective-permute-start.4 = (bf16[640,128]{1,0:T(8,128)(2,1)S(1)}, bf16[640,128]{1,0:T(8,128)(2,1)S(1)}, u32[]{:S(2)}, u32[]{:S(2)}) collective-permute-start(bf16[640,128]{1,0:T(8,128)(2,1)S(1)} %add_convert_fusion.refs_2_.refs_3_), channel_id=1, source_target_pairs={{0,2},{1,3},{2,0},{3,1},{4,6},{5,7},{6,4},{7,5},{8,10},{9,11},{10,... | collective-permute-start | bytes 491528 | tf_op jit(solution)/shard_map/ppermute | solution.py:371
  33.5 5.9 %shard_map.112 = (f32[4,512,128]{2,1,0:T(8,128)S(1)}, bf16[4,512,128]{2,1,0:T(8,128)(2,1)S(1)}, s32[1]{0:T(128)}) custom-call(s32[80]{0:T(128)S(1)} %pad_add_fusion.refs_0_, bf16[640,2048]{1,0:T(8,128)(2,1)S(1)} %copy-done, bf16[640,7168]{1,0:T(8,128)(2,1)S(1)} %bitcast.5, bf16[640,128]{1,0:T(8,128)(2,1)S(1)} %get-tuple-element.112.refs_3_, ...), custom_call_target="tpu_custom_call" | custom-call | tf_op jit(solution)/shard_map/pallas_call | solution.py:38
  40.9 3.6 %collective-permute-start.19 = (bf16[320,1792]{1,0:T(8,128)(2,1)S(1)}, bf16[320,1792]{1,0:T(8,128)(2,1)S(1)}, u32[]{:S(2)}, u32[]{:S(2)}) collective-permute-start(bf16[320,1792]{1,0:T(8,128)(2,1)S(1)} %get-tuple-element.85), channel_id=1, source_target_pairs={{0,12},{4,0},{8,4},{12,8},{1,13},{5,1},{9,5},{13,9},{2,14},{6,2},{... | collective-permute-start | bytes 3440648 | tf_op jit(solution)/shard_map/ppermute | solution.py:371
  44.5 4.8 %shard_map.114 = (f32[4,1664,128]{2,1,0:T(8,128)S(1)}, bf16[2224,128]{1,0:T(8,128)(2,1)S(1)}, bf16[2224,128]{1,0:T(8,128)(2,1)S(1)}, bf16[2208,128]{1,0:T(8,128)(2,1)S(1)}, s32[1]{0:T(128)}) custom-call(bf16[640,2048]{1,0:T(8,128)(2,1)S(1)} %copy-done.1, bf16[640,7168]{1,0:T(8,128)(2,1)} %refs_1_.7, bf16[640,128]{1,0:T(8,128)(2,1)S(1)} %add_convert_fusion.refs_2_.refs_3_, ...), custom_call_target="tpu_custom_call" | custom-call | tf_op jit(solution)/shard_map/pallas_call | solution.py:38
  49.3 2.9 %collective-permute-start.12 = (bf16[2224,128]{1,0:T(8,128)(2,1)S(1)}, bf16[2224,128]{1,0:T(8,128)(2,1)S(1)}, u32[]{:S(2)}, u32[]{:S(2)}) collective-permute-start(bf16[2224,128]{1,0:T(8,128)(2,1)S(1)} %get-tuple-element.72), channel_id=1, source_target_pairs={{0,16},{16,0},{32,48},{48,32},{64,80},{80,64},{96,112},{112,96},{1... | collective-permute-start | bytes 1708040 | tf_op jit(solution)/shard_map/ppermute | solution.py:381
  52.7 3.0 %shard_map.115 = (bf16[640,1792]{1,0:T(8,128)(2,1)S(1)}, bf16[640,1792]{1,0:T(8,128)(2,1)S(1)}, s32[1]{0:T(128)}) custom-call(s32[80]{0:T(128)S(1)} %pad_add_fusion.refs_0_, bf16[640,2048]{1,0:T(8,128)(2,1)S(1)} %copy-done.1, bf16[32,128,128]{2,1,0:T(8,128)(2,1)S(1)} %copy-done.2, s32[1]{0:T(128)} %get-tuple-element.75.refs_3_), custom_call_target="tpu_custom_call" | custom-call | tf_op jit(solution)/shard_map/pallas_call | solution.py:38
  61.5 5.9 %collective-permute-done.18.refs_2_ = bf16[320,1792]{1,0:T(8,128)(2,1)S(1)} collective-permute-done((bf16[320,1792]{1,0:T(8,128)(2,1)S(1)}, bf16[320,1792]{1,0:T(8,128)(2,1)S(1)}, u32[]{:S(2)}, u32[]{:S(2)}) %collective-permute-start.18) | collective-permute-done | bytes 1146912 | tf_op jit(solution)/shard_map/ppermute | solution.py:371
  75.7 2.4 %collective-permute-start.21 = (bf16[704,128]{1,0:T(8,128)(2,1)S(1)}, bf16[704,128]{1,0:T(8,128)(2,1)S(1)}, u32[]{:S(2)}, u32[]{:S(2)}) collective-permute-start(bf16[704,128]{1,0:T(8,128)(2,1)S(1)} %get-tuple-element.89), channel_id=1, source_target_pairs={{0,96},{16,112},{32,0},{48,16},{64,32},{80,48},{96,64},{112,80},{1... | collective-permute-start | bytes 540680 | tf_op jit(solution)/shard_map/ppermute | solution.py:377
  79.3 4.3 %collective-permute-start.23 = (bf16[512,128]{1,0:T(8,128)(2,1)S(1)}, bf16[512,128]{1,0:T(8,128)(2,1)S(1)}, u32[]{:S(2)}, u32[]{:S(2)}) collective-permute-start(bf16[512,128]{1,0:T(8,128)(2,1)S(1)} %get-tuple-element.92.refs_5_), channel_id=1, source_target_pairs={{0,3},{1,2},{2,1},{3,0},{4,7},{5,6},{6,5},{7,4},{8,11},{9,10},{10,... | collective-permute-start | bytes 393224 | tf_op jit(solution)/shard_map/ppermute | solution.py:538
  83.6 2.6 %collective-permute-done.23.refs_6_ = bf16[512,128]{1,0:T(8,128)(2,1)S(1)} collective-permute-done((bf16[512,128]{1,0:T(8,128)(2,1)S(1)}, bf16[512,128]{1,0:T(8,128)(2,1)S(1)}, u32[]{:S(2)}, u32[]{:S(2)}) %collective-permute-start.23) | collective-permute-done | bytes 131104 | tf_op jit(solution)/shard_map/ppermute | solution.py:538
  89.0 4.7 %shard_map.121 = (f32[640,1792]{1,0:T(8,128)S(1)}, s32[1]{0:T(128)}) custom-call(s32[80]{0:T(128)S(1)} %pad_add_fusion.refs_0_, bf16[640,2048]{1,0:T(8,128)(2,1)S(1)} %copy-done.1, bf16[32,128,128]{2,1,0:T(8,128)(2,1)S(1)} %copy-done.2, bf16[640,128]{1,0:T(8,128)(2,1)S(1)} %add_convert_fusion.refs_2_.refs_3_, ...), custom_call_target="tpu_custom_call" | custom-call | tf_op jit(solution)/shard_map/pallas_call | solution.py:38
  93.7 7.0 %collective-permute-done.28.refs_2_ = bf16[2432,128]{1,0:T(8,128)(2,1)S(1)} collective-permute-done((bf16[2432,128]{1,0:T(8,128)(2,1)S(1)}, bf16[2432,128]{1,0:T(8,128)(2,1)S(1)}, u32[]{:S(2)}, u32[]{:S(2)}) %collective-permute-start.28) | collective-permute-done | bytes 622624 | tf_op jit(solution)/shard_map/ppermute | solution.py:377
  102.1 4.6 %collective-permute-start.31 = (bf16[5632,128]{1,0:T(8,128)(2,1)S(1)}, bf16[5632,128]{1,0:T(8,128)(2,1)S(1)}, u32[]{:S(2)}, u32[]{:S(2)}) collective-permute-start(bf16[5632,128]{1,0:T(8,128)(2,1)S(1)} %get-tuple-element.100.refs_0_), channel_id=1, source_target_pairs={{0,16},{16,0},{32,48},{48,32},{64,80},{80,64},{96,112},{112,96},{1... | collective-permute-start | bytes 4325384 | tf_op jit(solution)/shard_map/ppermute | solution.py:381
  108.3 2.9 %shard_map.123 = (bf16[2048,512]{1,0:T(8,128)(2,1)}, bf16[512,1792]{1,0:T(8,128)(2,1)}, bf16[4096,128]{1,0:T(8,128)(2,1)}, s32[1]{0:T(128)}) custom-call(bf16[5632,128]{1,0:T(8,128)(2,1)S(1)} %get-tuple-element.100.refs_0_, bf16[1664,128]{1,0:T(8,128)(2,1)S(1)} %get-tuple-element.101.refs_1_, s32[1]{0:T(128)} %get-tuple-element.102.refs_2_), custom_call_target="tpu_custom_call" | custom-call | tf_op jit(solution)/shard_map/pallas_call | solution.py:38
  111.2 4.5 %collective-permute-done.29.refs_1_ = bf16[1216,128]{1,0:T(8,128)(2,1)S(1)} collective-permute-done((bf16[1216,128]{1,0:T(8,128)(2,1)S(1)}, bf16[1216,128]{1,0:T(8,128)(2,1)S(1)}, u32[]{:S(2)}, u32[]{:S(2)}) %collective-permute-start.29) | collective-permute-done | bytes 311328 | tf_op jit(solution)/shard_map/ppermute | solution.py:377
  119.1 2.2 %collective-permute-done.32.refs_6_ = bf16[1664,128]{1,0:T(8,128)(2,1)S(1)} collective-permute-done((bf16[1664,128]{1,0:T(8,128)(2,1)S(1)}, bf16[1664,128]{1,0:T(8,128)(2,1)S(1)}, u32[]{:S(2)}, u32[]{:S(2)}) %collective-permute-start.32) | collective-permute-done | bytes 426016 | tf_op jit(solution)/shard_map/ppermute | solution.py:381
  121.3 3.3 %shard_map.125 = (bf16[640,1792]{1,0:T(8,128)(2,1)}, bf16[2048,512]{1,0:T(8,128)(2,1)}, bf16[512,1792]{1,0:T(8,128)(2,1)}, bf16[4096,128]{1,0:T(8,128)(2,1)}) custom-call(f32[640,1792]{1,0:T(8,128)S(1)} %get-tuple-element.95.refs_0_, ...), custom_call_target="tpu_custom_call", output_to_operand_aliasing={{1}: (7, {}), {2}: (8, {}), {3}: (9, {})} | custom-call | tf_op jit(solution)/shard_map/pallas_call | solution.py:586
  (81 shorter events, 33.7 us)
Async XLA Ops:
  7.8 11.2 %collective-permute-start.6 = (bf16[640,128]{1,0:T(8,128)(2,1)S(1)}, bf16[640,128]{1,0:T(8,128)(2,1)S(1)}, u32[]{:S(2)}, u32[]{:S(2)}) collective-permute-start(bf16[640,128]{1,0:T(8,128)(2,1)S(1)} %get-tuple-element.61), channel_id=1, source_target_pairs={{0,1},{1,2},{2,3},{3,0},{4,5},{5,6},{6,7},{7,4},{8,9},{9,10},{10,1... | collective-permute-start | bytes 491528 | tf_op jit(solution)/shard_map/ppermute | solution.py:371
  10.4 10.5 %collective-permute-start.7 = (bf16[640,128]{1,0:T(8,128)(2,1)S(1)}, bf16[640,128]{1,0:T(8,128)(2,1)S(1)}, u32[]{:S(2)}, u32[]{:S(2)}) collective-permute-start(bf16[640,128]{1,0:T(8,128)(2,1)S(1)} %get-tuple-element.62), channel_id=1, source_target_pairs={{0,2},{1,3},{2,0},{3,1},{4,6},{5,7},{6,4},{7,5},{8,10},{9,11},{10,... | collective-permute-start | bytes 491528 | tf_op jit(solution)/shard_map/ppermute | solution.py:371
  15.2 9.4 %collective-permute-start.2 = (bf16[640,128]{1,0:T(8,128)(2,1)S(1)}, bf16[640,128]{1,0:T(8,128)(2,1)S(1)}, u32[]{:S(2)}, u32[]{:S(2)}) collective-permute-start(bf16[640,128]{1,0:T(8,128)(2,1)S(1)} %get-tuple-element.59), channel_id=1, source_target_pairs={{0,12},{4,0},{8,4},{12,8},{1,13},{5,1},{9,5},{13,9},{2,14},{6,2},{... | collective-permute-start | bytes 491528 | tf_op jit(solution)/shard_map/ppermute | solution.py:371
  19.1 9.1 %collective-permute-start = (bf16[640,128]{1,0:T(8,128)(2,1)S(1)}, bf16[640,128]{1,0:T(8,128)(2,1)S(1)}, u32[]{:S(2)}, u32[]{:S(2)}) collective-permute-start(bf16[640,128]{1,0:T(8,128)(2,1)S(1)} %get-tuple-element.59), channel_id=1, source_target_pairs={{0,4},{4,8},{8,12},{12,0},{1,5},{5,9},{9,13},{13,1},{2,6},{6,10},{... | collective-permute-start | bytes 491528 | tf_op jit(solution)/shard_map/ppermute | solution.py:371
  21.0 9.9 %collective-permute-start.11 = (bf16[640,128]{1,0:T(8,128)(2,1)S(1)}, bf16[640,128]{1,0:T(8,128)(2,1)S(1)}, u32[]{:S(2)}, u32[]{:S(2)}) collective-permute-start(bf16[640,128]{1,0:T(8,128)(2,1)S(1)} %get-tuple-element.112.refs_3_), channel_id=1, source_target_pairs={{0,12},{4,0},{8,4},{12,8},{1,13},{5,1},{9,5},{13,9},{2,14},{6,2},{... | collective-permute-start | bytes 491528 | tf_op jit(solution)/shard_map/ppermute | solution.py:371
  24.3 15.1 %collective-permute-start.10 = (bf16[640,128]{1,0:T(8,128)(2,1)S(1)}, bf16[640,128]{1,0:T(8,128)(2,1)S(1)}, u32[]{:S(2)}, u32[]{:S(2)}) collective-permute-start(bf16[640,128]{1,0:T(8,128)(2,1)S(1)} %get-tuple-element.112.refs_3_), channel_id=1, source_target_pairs={{0,8},{4,12},{8,0},{12,4},{1,9},{5,13},{9,1},{13,5},{2,10},{6,14},... | collective-permute-start | bytes 491528 | tf_op jit(solution)/shard_map/ppermute | solution.py:371
  24.6 14.8 %collective-permute-start.9 = (bf16[640,128]{1,0:T(8,128)(2,1)S(1)}, bf16[640,128]{1,0:T(8,128)(2,1)S(1)}, u32[]{:S(2)}, u32[]{:S(2)}) collective-permute-start(bf16[640,128]{1,0:T(8,128)(2,1)S(1)} %get-tuple-element.112.refs_3_), channel_id=1, source_target_pairs={{0,4},{4,8},{8,12},{12,0},{1,5},{5,9},{9,13},{13,1},{2,6},{6,10},{... | collective-permute-start | bytes 491528 | tf_op jit(solution)/shard_map/ppermute | solution.py:371
  28.2 11.2 %collective-permute-start.5 = (bf16[640,128]{1,0:T(8,128)(2,1)S(1)}, bf16[640,128]{1,0:T(8,128)(2,1)S(1)}, u32[]{:S(2)}, u32[]{:S(2)}) collective-permute-start(bf16[640,128]{1,0:T(8,128)(2,1)S(1)} %add_convert_fusion.refs_2_.refs_3_), channel_id=1, source_target_pairs={{0,3},{1,0},{2,1},{3,2},{4,7},{5,4},{6,5},{7,6},{8,11},{9,8},{10,9... | collective-permute-start | bytes 491528 | tf_op jit(solution)/shard_map/ppermute | solution.py:371
  28.6 10.9 %collective-permute-start.4 = (bf16[640,128]{1,0:T(8,128)(2,1)S(1)}, bf16[640,128]{1,0:T(8,128)(2,1)S(1)}, u32[]{:S(2)}, u32[]{:S(2)}) collective-permute-start(bf16[640,128]{1,0:T(8,128)(2,1)S(1)} %add_convert_fusion.refs_2_.refs_3_), channel_id=1, source_target_pairs={{0,2},{1,3},{2,0},{3,1},{4,6},{5,7},{6,4},{7,5},{8,10},{9,11},{10,... | collective-permute-start | bytes 491528 | tf_op jit(solution)/shard_map/ppermute | solution.py:371
  30.9 8.6 %collective-permute-start.3 = (bf16[640,128]{1,0:T(8,128)(2,1)S(1)}, bf16[640,128]{1,0:T(8,128)(2,1)S(1)}, u32[]{:S(2)}, u32[]{:S(2)}) collective-permute-start(bf16[640,128]{1,0:T(8,128)(2,1)S(1)} %add_convert_fusion.refs_2_.refs_3_), channel_id=1, source_target_pairs={{0,1},{1,2},{2,3},{3,0},{4,5},{5,6},{6,7},{7,4},{8,9},{9,10},{10,1... | collective-permute-start | bytes 491528 | tf_op jit(solution)/shard_map/ppermute | solution.py:371
  40.8 26.6 %collective-permute-start.18 = (bf16[320,1792]{1,0:T(8,128)(2,1)S(1)}, bf16[320,1792]{1,0:T(8,128)(2,1)S(1)}, u32[]{:S(2)}, u32[]{:S(2)}) collective-permute-start(bf16[320,1792]{1,0:T(8,128)(2,1)S(1)} %get-tuple-element.84), channel_id=1, source_target_pairs={{0,4},{4,8},{8,12},{12,0},{1,5},{5,9},{9,13},{13,1},{2,6},{6,10},{... | collective-permute-start | bytes 3440648 | tf_op jit(solution)/shard_map/ppermute | solution.py:371
  40.9 26.5 %collective-permute-start.19 = (bf16[320,1792]{1,0:T(8,128)(2,1)S(1)}, bf16[320,1792]{1,0:T(8,128)(2,1)S(1)}, u32[]{:S(2)}, u32[]{:S(2)}) collective-permute-start(bf16[320,1792]{1,0:T(8,128)(2,1)S(1)} %get-tuple-element.85), channel_id=1, source_target_pairs={{0,12},{4,0},{8,4},{12,8},{1,13},{5,1},{9,5},{13,9},{2,14},{6,2},{... | collective-permute-start | bytes 3440648 | tf_op jit(solution)/shard_map/ppermute | solution.py:371
  57.2 15.1 %collective-permute-start.15 = (bf16[1664,128]{1,0:T(8,128)(2,1)S(1)}, bf16[1664,128]{1,0:T(8,128)(2,1)S(1)}, u32[]{:S(2)}, u32[]{:S(2)}) collective-permute-start(bf16[1664,128]{1,0:T(8,128)(2,1)S(1)} %get-tuple-element.78), channel_id=1, source_target_pairs={{0,32},{16,48},{32,64},{48,80},{64,96},{80,112},{96,0},{112,16},{1... | collective-permute-start | bytes 1277960 | tf_op jit(solution)/shard_map/ppermute | solution.py:377
  58.5 13.8 %collective-permute-start.16 = (bf16[1664,128]{1,0:T(8,128)(2,1)S(1)}, bf16[1664,128]{1,0:T(8,128)(2,1)S(1)}, u32[]{:S(2)}, u32[]{:S(2)}) collective-permute-start(bf16[1664,128]{1,0:T(8,128)(2,1)S(1)} %get-tuple-element.79), channel_id=1, source_target_pairs={{0,96},{16,112},{32,0},{48,16},{64,32},{80,48},{96,64},{112,80},{1... | collective-permute-start | bytes 1277960 | tf_op jit(solution)/shard_map/ppermute | solution.py:377
  60.0 12.3 %collective-permute-start.17 = (bf16[256,128]{1,0:T(8,128)(2,1)S(1)}, bf16[256,128]{1,0:T(8,128)(2,1)S(1)}, u32[]{:S(2)}, u32[]{:S(2)}) collective-permute-start(bf16[256,128]{1,0:T(8,128)(2,1)S(1)} %get-tuple-element.81), channel_id=1, source_target_pairs={{0,64},{16,80},{32,96},{48,112},{64,0},{80,16},{96,32},{112,48},{1... | collective-permute-start | bytes 196616 | tf_op jit(solution)/shard_map/ppermute | solution.py:377
  68.7 52.6 %collective-permute-start.24 = (bf16[640,1792]{1,0:T(8,128)(2,1)S(1)}, bf16[640,1792]{1,0:T(8,128)(2,1)S(1)}, u32[]{:S(2)}, u32[]{:S(2)}) collective-permute-start(bf16[640,1792]{1,0:T(8,128)(2,1)S(1)} %get-tuple-element.96), channel_id=1, source_target_pairs={{0,4},{4,8},{8,12},{12,0},{1,5},{5,9},{9,13},{13,1},{2,6},{6,10},{... | collective-permute-start | bytes 6881288 | tf_op jit(solution)/shard_map/ppermute | solution.py:371
  69.9 51.4 %collective-permute-start.25 = (bf16[640,1792]{1,0:T(8,128)(2,1)S(1)}, bf16[640,1792]{1,0:T(8,128)(2,1)S(1)}, u32[]{:S(2)}, u32[]{:S(2)}) collective-permute-start(bf16[640,1792]{1,0:T(8,128)(2,1)S(1)} %get-tuple-element.97), channel_id=1, source_target_pairs={{0,12},{4,0},{8,4},{12,8},{1,13},{5,1},{9,5},{13,9},{2,14},{6,2},{... | collective-permute-start | bytes 6881288 | tf_op jit(solution)/shard_map/ppermute | solution.py:371
  75.4 8.1 %collective-permute-start.20 = (bf16[704,128]{1,0:T(8,128)(2,1)S(1)}, bf16[704,128]{1,0:T(8,128)(2,1)S(1)}, u32[]{:S(2)}, u32[]{:S(2)}) collective-permute-start(bf16[704,128]{1,0:T(8,128)(2,1)S(1)} %get-tuple-element.88), channel_id=1, source_target_pairs={{0,32},{16,48},{32,64},{48,80},{64,96},{80,112},{96,0},{112,16},{1... | collective-permute-start | bytes 540680 | tf_op jit(solution)/shard_map/ppermute | solution.py:377
  75.7 7.9 %collective-permute-start.21 = (bf16[704,128]{1,0:T(8,128)(2,1)S(1)}, bf16[704,128]{1,0:T(8,128)(2,1)S(1)}, u32[]{:S(2)}, u32[]{:S(2)}) collective-permute-start(bf16[704,128]{1,0:T(8,128)(2,1)S(1)} %get-tuple-element.89), channel_id=1, source_target_pairs={{0,96},{16,112},{32,0},{48,16},{64,32},{80,48},{96,64},{112,80},{1... | collective-permute-start | bytes 540680 | tf_op jit(solution)/shard_map/ppermute | solution.py:377
  87.5 13.3 %collective-permute-start.28 = (bf16[2432,128]{1,0:T(8,128)(2,1)S(1)}, bf16[2432,128]{1,0:T(8,128)(2,1)S(1)}, u32[]{:S(2)}, u32[]{:S(2)}) collective-permute-start(bf16[2432,128]{1,0:T(8,128)(2,1)S(1)} %get-tuple-element.98.refs_0_), channel_id=1, source_target_pairs={{0,96},{16,112},{32,0},{48,16},{64,32},{80,48},{96,64},{112,80},{1... | collective-permute-start | bytes 1867784 | tf_op jit(solution)/shard_map/ppermute | solution.py:377
  87.5 13.2 %collective-permute-start.26 = (bf16[2432,128]{1,0:T(8,128)(2,1)S(1)}, bf16[2432,128]{1,0:T(8,128)(2,1)S(1)}, u32[]{:S(2)}, u32[]{:S(2)}) collective-permute-start(bf16[2432,128]{1,0:T(8,128)(2,1)S(1)} %get-tuple-element.98.refs_0_), channel_id=1, source_target_pairs={{0,32},{16,48},{32,64},{48,80},{64,96},{80,112},{96,0},{112,16},{1... | collective-permute-start | bytes 1867784 | tf_op jit(solution)/shard_map/ppermute | solution.py:377
  102.1 19.3 %collective-permute-start.31 = (bf16[5632,128]{1,0:T(8,128)(2,1)S(1)}, bf16[5632,128]{1,0:T(8,128)(2,1)S(1)}, u32[]{:S(2)}, u32[]{:S(2)}) collective-permute-start(bf16[5632,128]{1,0:T(8,128)(2,1)S(1)} %get-tuple-element.100.refs_0_), channel_id=1, source_target_pairs={{0,16},{16,0},{32,48},{48,32},{64,80},{80,64},{96,112},{112,96},{1... | collective-permute-start | bytes 4325384 | tf_op jit(solution)/shard_map/ppermute | solution.py:381
  106.7 9.0 %collective-permute-start.29 = (bf16[1216,128]{1,0:T(8,128)(2,1)S(1)}, bf16[1216,128]{1,0:T(8,128)(2,1)S(1)}, u32[]{:S(2)}, u32[]{:S(2)}) collective-permute-start(bf16[1216,128]{1,0:T(8,128)(2,1)S(1)} %slice.9), channel_id=1, source_target_pairs={{0,96},{16,112},{32,0},{48,16},{64,32},{80,48},{96,64},{112,80},{1... | collective-permute-start | bytes 933896 | tf_op jit(solution)/shard_map/ppermute | solution.py:377
  106.8 10.0 %collective-permute-start.27 = (bf16[1216,128]{1,0:T(8,128)(2,1)S(1)}, bf16[1216,128]{1,0:T(8,128)(2,1)S(1)}, u32[]{:S(2)}, u32[]{:S(2)}) collective-permute-start(bf16[1216,128]{1,0:T(8,128)(2,1)S(1)} %slice.8), channel_id=1, source_target_pairs={{0,32},{16,48},{32,64},{48,80},{64,96},{80,112},{96,0},{112,16},{1... | collective-permute-start | bytes 933896 | tf_op jit(solution)/shard_map/ppermute | solution.py:377
  (18 other events, 179.5 us)

commit v6 on v5

--- a/solution.py
+++ b/solution.py
@@ -429,7 +429,7 @@
             vm((tok_rows, quarter), BF16),
             dma((7,)),
         ],
-        mib=52,
+        mib=48,
         hbm_outs=2,
     )
     rank_in = over(n_f, lambda k: shift(rank_low, "fsdp", n_f, k))

time: 126 us -> 126 us (level)
  starting transfers between devices: 50.8 us -> 47 us
  waiting for transfers between devices: 28.9 us -> 31.8 us
  Pallas kernels: 41.3 us -> 43.7 us
    ppermute x16, waiting for transfers between devices: 10.5 us -> 13.5 us  [shift(): return lax.ppermute(x, axis, [(i, (i + k) % n) for i in range(n)])]
    pallas_call x13, Pallas kernels: 36.7 us -> 39.2 us  [call(): pl.pallas_call(body, out_shape=(*outs, shape((1,), jnp.int32)), in_specs=...]
    ppermute x16, starting transfers between devices: 25.6 us -> 23.8 us  [shift(): return lax.ppermute(x, axis, [(i, (i + k) % n) for i in range(n)])]
    ppermute x1, starting transfers between devices: 4.26 us -> 2.5 us  [per_device(): lax.ppermute(left_pair, 'tensor', [(i, n_t - 1 - i) for i in range(n_t)])]
    ppermute x1, starting transfers between devices: 1.75 us -> 0.09 us  [per_device(): left_near = lax.ppermute(left, 'tensor', [(i, i ^ 1) for i in range(n_t)])]
  transfers between devices with their start and end apart: 33 -> 33, of which waited for: 9 -> 11; matrix products, arithmetic and copies ran while one was open for 0% -> 0% of each run, Pallas kernels for 24% -> 25%
where the time goes in v6:
time: 126 us
  starting transfers between devices  47 us (37%)
  Pallas kernels  43.7 us (35%)
  waiting for transfers between devices  31.8 us (25%)
  local copies, waits for them, and re-layouts  1.44 us (1%)
    pallas_call x13, Pallas kernels, call(): pl.pallas_call(body, out_shape=(*outs, shape((1,), jnp.int32)), in_specs=...  39.2 us
    ppermute x16, starting transfers between devices, shift(): return lax.ppermute(x, axis, [(i, (i + k) % n) for i in range(n)])  23.8 us
    ppermute x16, waiting for transfers between devices, shift(): return lax.ppermute(x, axis, [(i, (i + k) % n) for i in range(n)])  13.5 us
    ppermute x9, waiting for transfers between devices, chip_shift(): return lax.ppermute(x, 'dp', perm)  12.5 us
    ppermute x9, starting transfers between devices, chip_shift(): return lax.ppermute(x, 'dp', perm)  11.2 us
    ppermute x6, starting transfers between devices, core_swap(): return lax.ppermute(x, 'dp', [(i, i ^ 1) for i in range(n_data)])  9.45 us
    pallas_call x1, Pallas kernels, per_device(): pl.pallas_call(bind(last_kernel), out_shape=(whole, *outs), in_specs=[VME...  3.29 us
    ppermute x1, waiting for transfers between devices, per_device(): lax.ppermute(left_pair, 'tensor', [(i, n_t - 1 - i) for i in range(n_t)])  2.9 us
  transfers between devices with their start and end apart: 33, of which 11 were waited for; matrix products, arithmetic and copies ran while one was open for 0% of the time, Pallas kernels for 25%

profile of v6, /device:TPU:1, one launch (start us, length us, event | category | flops | bytes accessed | tf_op | source)
XLA Modules:
  0.0 125.8 jit_solution(7890876974977302390)
XLA Ops:
  2.8 7.4 %shard_map.111 = (f32[640,128]{1,0:T(8,128)S(1)}, bf16[640,128]{1,0:T(8,128)(2,1)S(1)}, f32[640,128]{1,0:T(8,128)S(1)}, bf16[640,128]{1,0:T(8,128)(2,1)S(1)}, bf...) custom-call(s32[80]{0:T(128)S(1)} %pad_add_fusion.refs_0_, ...), custom_call_target="tpu_custom_call" | custom-call | tf_op jit(solution)/shard_map/pallas_call | solution.py:38
  10.2 2.5 %collective-permute-start.6 = (bf16[640,128]{1,0:T(8,128)(2,1)S(1)}, bf16[640,128]{1,0:T(8,128)(2,1)S(1)}, u32[]{:S(2)}, u32[]{:S(2)}) collective-permute-start(bf16[640,128]{1,0:T(8,128)(2,1)S(1)} %get-tuple-element.61), channel_id=1, source_target_pairs={{0,1},{1,2},{2,3},{3,0},{4,5},{5,6},{6,7},{7,4},{8,9},{9,10},{10,1... | collective-permute-start | bytes 491528 | tf_op jit(solution)/shard_map/ppermute | solution.py:371
  12.6 3.6 %collective-permute-start.7 = (bf16[640,128]{1,0:T(8,128)(2,1)S(1)}, bf16[640,128]{1,0:T(8,128)(2,1)S(1)}, u32[]{:S(2)}, u32[]{:S(2)}) collective-permute-start(bf16[640,128]{1,0:T(8,128)(2,1)S(1)} %get-tuple-element.62), channel_id=1, source_target_pairs={{0,2},{1,3},{2,0},{3,1},{4,6},{5,7},{6,4},{7,5},{8,10},{9,11},{10,... | collective-permute-start | bytes 491528 | tf_op jit(solution)/shard_map/ppermute | solution.py:371
  16.6 2.6 %collective-permute-start.2 = (bf16[640,128]{1,0:T(8,128)(2,1)S(1)}, bf16[640,128]{1,0:T(8,128)(2,1)S(1)}, u32[]{:S(2)}, u32[]{:S(2)}) collective-permute-start(bf16[640,128]{1,0:T(8,128)(2,1)S(1)} %get-tuple-element.59), channel_id=1, source_target_pairs={{0,12},{4,0},{8,4},{12,8},{1,13},{5,1},{9,5},{13,9},{2,14},{6,2},{... | collective-permute-start | bytes 491528 | tf_op jit(solution)/shard_map/ppermute | solution.py:371
  20.8 2.5 %collective-permute-done.7 = bf16[640,128]{1,0:T(8,128)(2,1)S(1)} collective-permute-done((bf16[640,128]{1,0:T(8,128)(2,1)S(1)}, bf16[640,128]{1,0:T(8,128)(2,1)S(1)}, u32[]{:S(2)}, u32[]{:S(2)}) %collective-permute-start.7) | collective-permute-done | bytes 163872 | tf_op jit(solution)/shard_map/ppermute | solution.py:371
  23.4 3.1 %collective-permute-start.11 = (bf16[640,128]{1,0:T(8,128)(2,1)S(1)}, bf16[640,128]{1,0:T(8,128)(2,1)S(1)}, u32[]{:S(2)}, u32[]{:S(2)}) collective-permute-start(bf16[640,128]{1,0:T(8,128)(2,1)S(1)} %get-tuple-element.112.refs_3_), channel_id=1, source_target_pairs={{0,12},{4,0},{8,4},{12,8},{1,13},{5,1},{9,5},{13,9},{2,14},{6,2},{... | collective-permute-start | bytes 491528 | tf_op jit(solution)/shard_map/ppermute | solution.py:371
  30.3 2.7 %collective-permute-start.4 = (bf16[640,128]{1,0:T(8,128)(2,1)S(1)}, bf16[640,128]{1,0:T(8,128)(2,1)S(1)}, u32[]{:S(2)}, u32[]{:S(2)}) collective-permute-start(bf16[640,128]{1,0:T(8,128)(2,1)S(1)} %add_convert_fusion.refs_2_.refs_3_), channel_id=1, source_target_pairs={{0,2},{1,3},{2,0},{3,1},{4,6},{5,7},{6,4},{7,5},{8,10},{9,11},{10,... | collective-permute-start | bytes 491528 | tf_op jit(solution)/shard_map/ppermute | solution.py:371
  33.1 5.8 %shard_map.112 = (f32[4,512,128]{2,1,0:T(8,128)S(1)}, bf16[4,512,128]{2,1,0:T(8,128)(2,1)S(1)}, s32[1]{0:T(128)}) custom-call(s32[80]{0:T(128)S(1)} %pad_add_fusion.refs_0_, bf16[640,2048]{1,0:T(8,128)(2,1)S(1)} %copy-done, bf16[640,7168]{1,0:T(8,128)(2,1)S(1)} %bitcast.5, bf16[640,128]{1,0:T(8,128)(2,1)S(1)} %get-tuple-element.112.refs_3_, ...), custom_call_target="tpu_custom_call" | custom-call | tf_op jit(solution)/shard_map/pallas_call | solution.py:38
  38.9 2.4 %collective-permute-done.3.refs_2_.refs_3_.refs_4_ = bf16[640,128]{1,0:T(8,128)(2,1)S(1)} collective-permute-done((bf16[640,128]{1,0:T(8,128)(2,1)S(1)}, bf16[640,128]{1,0:T(8,128)(2,1)S(1)}, u32[]{:S(2)}, u32[]{:S(2)}) %collective-permute-start.3) | collective-permute-done | bytes 163872 | tf_op jit(solution)/shard_map/ppermute | solution.py:371
  45.2 4.7 %shard_map.114 = (f32[4,1664,128]{2,1,0:T(8,128)S(1)}, bf16[2224,128]{1,0:T(8,128)(2,1)S(1)}, bf16[2224,128]{1,0:T(8,128)(2,1)S(1)}, bf16[2208,128]{1,0:T(8,128)(2,1)S(1)}, s32[1]{0:T(128)}) custom-call(bf16[640,2048]{1,0:T(8,128)(2,1)S(1)} %copy-done, bf16[640,7168]{1,0:T(8,128)(2,1)} %refs_1_.7, bf16[640,128]{1,0:T(8,128)(2,1)S(1)} %add_convert_fusion.refs_2_.refs_3_, ...), custom_call_target="tpu_custom_call" | custom-call | tf_op jit(solution)/shard_map/pallas_call | solution.py:38
  52.4 4.4 %shard_map.115 = (bf16[640,1792]{1,0:T(8,128)(2,1)S(1)}, bf16[640,1792]{1,0:T(8,128)(2,1)S(1)}, s32[1]{0:T(128)}) custom-call(s32[80]{0:T(128)S(1)} %pad_add_fusion.refs_0_, bf16[640,2048]{1,0:T(8,128)(2,1)S(1)} %copy-done, bf16[32,128,128]{2,1,0:T(8,128)(2,1)S(1)} %copy-done.1, s32[1]{0:T(128)} %get-tuple-element.75.refs_3_), custom_call_target="tpu_custom_call" | custom-call | tf_op jit(solution)/shard_map/pallas_call | solution.py:38
  62.6 6.7 %collective-permute-done.18.refs_2_ = bf16[320,1792]{1,0:T(8,128)(2,1)S(1)} collective-permute-done((bf16[320,1792]{1,0:T(8,128)(2,1)S(1)}, bf16[320,1792]{1,0:T(8,128)(2,1)S(1)}, u32[]{:S(2)}, u32[]{:S(2)}) %collective-permute-start.18) | collective-permute-done | bytes 1146912 | tf_op jit(solution)/shard_map/ppermute | solution.py:371
  71.0 2.3 %collective-permute-start.25 = (bf16[640,1792]{1,0:T(8,128)(2,1)S(1)}, bf16[640,1792]{1,0:T(8,128)(2,1)S(1)}, u32[]{:S(2)}, u32[]{:S(2)}) collective-permute-start(bf16[640,1792]{1,0:T(8,128)(2,1)S(1)} %get-tuple-element.97), channel_id=1, source_target_pairs={{0,12},{4,0},{8,4},{12,8},{1,13},{5,1},{9,5},{13,9},{2,14},{6,2},{... | collective-permute-start | bytes 6881288 | tf_op jit(solution)/shard_map/ppermute | solution.py:371
  79.4 2.5 %collective-permute-start.23 = (bf16[512,128]{1,0:T(8,128)(2,1)S(1)}, bf16[512,128]{1,0:T(8,128)(2,1)S(1)}, u32[]{:S(2)}, u32[]{:S(2)}) collective-permute-start(bf16[512,128]{1,0:T(8,128)(2,1)S(1)} %get-tuple-element.92.refs_5_), channel_id=1, source_target_pairs={{0,3},{1,2},{2,1},{3,0},{4,7},{5,6},{6,5},{7,4},{8,11},{9,10},{10,... | collective-permute-start | bytes 393224 | tf_op jit(solution)/shard_map/ppermute | solution.py:538
  81.9 2.9 %collective-permute-done.23.refs_6_ = bf16[512,128]{1,0:T(8,128)(2,1)S(1)} collective-permute-done((bf16[512,128]{1,0:T(8,128)(2,1)S(1)}, bf16[512,128]{1,0:T(8,128)(2,1)S(1)}, u32[]{:S(2)}, u32[]{:S(2)}) %collective-permute-start.23) | collective-permute-done | bytes 131104 | tf_op jit(solution)/shard_map/ppermute | solution.py:538
  86.1 2.5 %collective-permute-start.28 = (bf16[2432,128]{1,0:T(8,128)(2,1)S(1)}, bf16[2432,128]{1,0:T(8,128)(2,1)S(1)}, u32[]{:S(2)}, u32[]{:S(2)}) collective-permute-start(bf16[2432,128]{1,0:T(8,128)(2,1)S(1)} %get-tuple-element.98.refs_0_), channel_id=1, source_target_pairs={{0,96},{16,112},{32,0},{48,16},{64,32},{80,48},{96,64},{112,80},{1... | collective-permute-start | bytes 1867784 | tf_op jit(solution)/shard_map/ppermute | solution.py:377
  88.6 5.1 %shard_map.121 = (f32[640,1792]{1,0:T(8,128)S(1)}, s32[1]{0:T(128)}) custom-call(s32[80]{0:T(128)S(1)} %pad_add_fusion.refs_0_, bf16[640,2048]{1,0:T(8,128)(2,1)S(1)} %copy-done, bf16[32,128,128]{2,1,0:T(8,128)(2,1)S(1)} %copy-done.1, bf16[640,128]{1,0:T(8,128)(2,1)S(1)} %add_convert_fusion.refs_2_.refs_3_, ...), custom_call_target="tpu_custom_call" | custom-call | tf_op jit(solution)/shard_map/pallas_call | solution.py:38
  93.7 3.8 %collective-permute-done.28.refs_2_ = bf16[2432,128]{1,0:T(8,128)(2,1)S(1)} collective-permute-done((bf16[2432,128]{1,0:T(8,128)(2,1)S(1)}, bf16[2432,128]{1,0:T(8,128)(2,1)S(1)}, u32[]{:S(2)}, u32[]{:S(2)}) %collective-permute-start.28) | collective-permute-done | bytes 622624 | tf_op jit(solution)/shard_map/ppermute | solution.py:377
  97.5 3.1 %collective-permute-done.26.refs_1_ = bf16[2432,128]{1,0:T(8,128)(2,1)S(1)} collective-permute-done((bf16[2432,128]{1,0:T(8,128)(2,1)S(1)}, bf16[2432,128]{1,0:T(8,128)(2,1)S(1)}, u32[]{:S(2)}, u32[]{:S(2)}) %collective-permute-start.26) | collective-permute-done | bytes 622624 | tf_op jit(solution)/shard_map/ppermute | solution.py:377
  101.9 5.7 %collective-permute-start.31 = (bf16[5632,128]{1,0:T(8,128)(2,1)S(1)}, bf16[5632,128]{1,0:T(8,128)(2,1)S(1)}, u32[]{:S(2)}, u32[]{:S(2)}) collective-permute-start(bf16[5632,128]{1,0:T(8,128)(2,1)S(1)} %get-tuple-element.100.refs_0_), channel_id=1, source_target_pairs={{0,16},{16,0},{32,48},{48,32},{64,80},{80,64},{96,112},{112,96},{1... | collective-permute-start | bytes 4325384 | tf_op jit(solution)/shard_map/ppermute | solution.py:381
  109.3 2.9 %shard_map.123 = (bf16[2048,512]{1,0:T(8,128)(2,1)}, bf16[512,1792]{1,0:T(8,128)(2,1)}, bf16[4096,128]{1,0:T(8,128)(2,1)}, s32[1]{0:T(128)}) custom-call(bf16[5632,128]{1,0:T(8,128)(2,1)S(1)} %get-tuple-element.100.refs_0_, bf16[1664,128]{1,0:T(8,128)(2,1)S(1)} %get-tuple-element.101.refs_1_, s32[1]{0:T(128)} %get-tuple-element.102.refs_2_), custom_call_target="tpu_custom_call" | custom-call | tf_op jit(solution)/shard_map/pallas_call | solution.py:38
  112.2 4.5 %collective-permute-done.29.refs_1_ = bf16[1216,128]{1,0:T(8,128)(2,1)S(1)} collective-permute-done((bf16[1216,128]{1,0:T(8,128)(2,1)S(1)}, bf16[1216,128]{1,0:T(8,128)(2,1)S(1)}, u32[]{:S(2)}, u32[]{:S(2)}) %collective-permute-start.29) | collective-permute-done | bytes 311328 | tf_op jit(solution)/shard_map/ppermute | solution.py:377
  120.2 2.2 %collective-permute-done.32.refs_6_ = bf16[1664,128]{1,0:T(8,128)(2,1)S(1)} collective-permute-done((bf16[1664,128]{1,0:T(8,128)(2,1)S(1)}, bf16[1664,128]{1,0:T(8,128)(2,1)S(1)}, u32[]{:S(2)}, u32[]{:S(2)}) %collective-permute-start.32) | collective-permute-done | bytes 426016 | tf_op jit(solution)/shard_map/ppermute | solution.py:381
  122.4 3.3 %shard_map.125 = (bf16[640,1792]{1,0:T(8,128)(2,1)}, bf16[2048,512]{1,0:T(8,128)(2,1)}, bf16[512,1792]{1,0:T(8,128)(2,1)}, bf16[4096,128]{1,0:T(8,128)(2,1)}) custom-call(f32[640,1792]{1,0:T(8,128)S(1)} %get-tuple-element.95.refs_0_, ...), custom_call_target="tpu_custom_call", output_to_operand_aliasing={{1}: (7, {}), {2}: (8, {}), {3}: (9, {})} | custom-call | tf_op jit(solution)/shard_map/pallas_call | solution.py:586
  (75 shorter events, 35.7 us)
Async XLA Ops:
  10.2 10.6 %collective-permute-start.6 = (bf16[640,128]{1,0:T(8,128)(2,1)S(1)}, bf16[640,128]{1,0:T(8,128)(2,1)S(1)}, u32[]{:S(2)}, u32[]{:S(2)}) collective-permute-start(bf16[640,128]{1,0:T(8,128)(2,1)S(1)} %get-tuple-element.61), channel_id=1, source_target_pairs={{0,1},{1,2},{2,3},{3,0},{4,5},{5,6},{6,7},{7,4},{8,9},{9,10},{10,1... | collective-permute-start | bytes 491528 | tf_op jit(solution)/shard_map/ppermute | solution.py:371
  12.6 10.7 %collective-permute-start.7 = (bf16[640,128]{1,0:T(8,128)(2,1)S(1)}, bf16[640,128]{1,0:T(8,128)(2,1)S(1)}, u32[]{:S(2)}, u32[]{:S(2)}) collective-permute-start(bf16[640,128]{1,0:T(8,128)(2,1)S(1)} %get-tuple-element.62), channel_id=1, source_target_pairs={{0,2},{1,3},{2,0},{3,1},{4,6},{5,7},{6,4},{7,5},{8,10},{9,11},{10,... | collective-permute-start | bytes 491528 | tf_op jit(solution)/shard_map/ppermute | solution.py:371
  16.2 7.1 %collective-permute-start.8 = (bf16[640,128]{1,0:T(8,128)(2,1)S(1)}, bf16[640,128]{1,0:T(8,128)(2,1)S(1)}, u32[]{:S(2)}, u32[]{:S(2)}) collective-permute-start(bf16[640,128]{1,0:T(8,128)(2,1)S(1)} %get-tuple-element.63), channel_id=1, source_target_pairs={{0,3},{1,0},{2,1},{3,2},{4,7},{5,4},{6,5},{7,6},{8,11},{9,8},{10,9... | collective-permute-start | bytes 491528 | tf_op jit(solution)/shard_map/ppermute | solution.py:371
  16.6 9.9 %collective-permute-start.2 = (bf16[640,128]{1,0:T(8,128)(2,1)S(1)}, bf16[640,128]{1,0:T(8,128)(2,1)S(1)}, u32[]{:S(2)}, u32[]{:S(2)}) collective-permute-start(bf16[640,128]{1,0:T(8,128)(2,1)S(1)} %get-tuple-element.59), channel_id=1, source_target_pairs={{0,12},{4,0},{8,4},{12,8},{1,13},{5,1},{9,5},{13,9},{2,14},{6,2},{... | collective-permute-start | bytes 491528 | tf_op jit(solution)/shard_map/ppermute | solution.py:371
  19.2 8.1 %collective-permute-start.1 = (bf16[640,128]{1,0:T(8,128)(2,1)S(1)}, bf16[640,128]{1,0:T(8,128)(2,1)S(1)}, u32[]{:S(2)}, u32[]{:S(2)}) collective-permute-start(bf16[640,128]{1,0:T(8,128)(2,1)S(1)} %get-tuple-element.59), channel_id=1, source_target_pairs={{0,8},{4,12},{8,0},{12,4},{1,9},{5,13},{9,1},{13,5},{2,10},{6,14},... | collective-permute-start | bytes 491528 | tf_op jit(solution)/shard_map/ppermute | solution.py:371
  20.8 8.3 %collective-permute-start = (bf16[640,128]{1,0:T(8,128)(2,1)S(1)}, bf16[640,128]{1,0:T(8,128)(2,1)S(1)}, u32[]{:S(2)}, u32[]{:S(2)}) collective-permute-start(bf16[640,128]{1,0:T(8,128)(2,1)S(1)} %get-tuple-element.59), channel_id=1, source_target_pairs={{0,4},{4,8},{8,12},{12,0},{1,5},{5,9},{9,13},{13,1},{2,6},{6,10},{... | collective-permute-start | bytes 491528 | tf_op jit(solution)/shard_map/ppermute | solution.py:371
  23.4 9.6 %collective-permute-start.11 = (bf16[640,128]{1,0:T(8,128)(2,1)S(1)}, bf16[640,128]{1,0:T(8,128)(2,1)S(1)}, u32[]{:S(2)}, u32[]{:S(2)}) collective-permute-start(bf16[640,128]{1,0:T(8,128)(2,1)S(1)} %get-tuple-element.112.refs_3_), channel_id=1, source_target_pairs={{0,12},{4,0},{8,4},{12,8},{1,13},{5,1},{9,5},{13,9},{2,14},{6,2},{... | collective-permute-start | bytes 491528 | tf_op jit(solution)/shard_map/ppermute | solution.py:371
  26.5 12.4 %collective-permute-start.10 = (bf16[640,128]{1,0:T(8,128)(2,1)S(1)}, bf16[640,128]{1,0:T(8,128)(2,1)S(1)}, u32[]{:S(2)}, u32[]{:S(2)}) collective-permute-start(bf16[640,128]{1,0:T(8,128)(2,1)S(1)} %get-tuple-element.112.refs_3_), channel_id=1, source_target_pairs={{0,8},{4,12},{8,0},{12,4},{1,9},{5,13},{9,1},{13,5},{2,10},{6,14},... | collective-permute-start | bytes 491528 | tf_op jit(solution)/shard_map/ppermute | solution.py:371
  26.5 12.4 %collective-permute-start.9 = (bf16[640,128]{1,0:T(8,128)(2,1)S(1)}, bf16[640,128]{1,0:T(8,128)(2,1)S(1)}, u32[]{:S(2)}, u32[]{:S(2)}) collective-permute-start(bf16[640,128]{1,0:T(8,128)(2,1)S(1)} %get-tuple-element.112.refs_3_), channel_id=1, source_target_pairs={{0,4},{4,8},{8,12},{12,0},{1,5},{5,9},{9,13},{13,1},{2,6},{6,10},{... | collective-permute-start | bytes 491528 | tf_op jit(solution)/shard_map/ppermute | solution.py:371
  29.2 9.6 %collective-permute-start.5 = (bf16[640,128]{1,0:T(8,128)(2,1)S(1)}, bf16[640,128]{1,0:T(8,128)(2,1)S(1)}, u32[]{:S(2)}, u32[]{:S(2)}) collective-permute-start(bf16[640,128]{1,0:T(8,128)(2,1)S(1)} %add_convert_fusion.refs_2_.refs_3_), channel_id=1, source_target_pairs={{0,3},{1,0},{2,1},{3,2},{4,7},{5,4},{6,5},{7,6},{8,11},{9,8},{10,9... | collective-permute-start | bytes 491528 | tf_op jit(solution)/shard_map/ppermute | solution.py:371
  30.3 8.6 %collective-permute-start.4 = (bf16[640,128]{1,0:T(8,128)(2,1)S(1)}, bf16[640,128]{1,0:T(8,128)(2,1)S(1)}, u32[]{:S(2)}, u32[]{:S(2)}) collective-permute-start(bf16[640,128]{1,0:T(8,128)(2,1)S(1)} %add_convert_fusion.refs_2_.refs_3_), channel_id=1, source_target_pairs={{0,2},{1,3},{2,0},{3,1},{4,6},{5,7},{6,4},{7,5},{8,10},{9,11},{10,... | collective-permute-start | bytes 491528 | tf_op jit(solution)/shard_map/ppermute | solution.py:371
  33.0 8.3 %collective-permute-start.3 = (bf16[640,128]{1,0:T(8,128)(2,1)S(1)}, bf16[640,128]{1,0:T(8,128)(2,1)S(1)}, u32[]{:S(2)}, u32[]{:S(2)}) collective-permute-start(bf16[640,128]{1,0:T(8,128)(2,1)S(1)} %add_convert_fusion.refs_2_.refs_3_), channel_id=1, source_target_pairs={{0,1},{1,2},{2,3},{3,0},{4,5},{5,6},{6,7},{7,4},{8,9},{9,10},{10,1... | collective-permute-start | bytes 491528 | tf_op jit(solution)/shard_map/ppermute | solution.py:371
  42.5 26.8 %collective-permute-start.18 = (bf16[320,1792]{1,0:T(8,128)(2,1)S(1)}, bf16[320,1792]{1,0:T(8,128)(2,1)S(1)}, u32[]{:S(2)}, u32[]{:S(2)}) collective-permute-start(bf16[320,1792]{1,0:T(8,128)(2,1)S(1)} %get-tuple-element.84), channel_id=1, source_target_pairs={{0,4},{4,8},{8,12},{12,0},{1,5},{5,9},{9,13},{13,1},{2,6},{6,10},{... | collective-permute-start | bytes 3440648 | tf_op jit(solution)/shard_map/ppermute | solution.py:371
  43.3 26.0 %collective-permute-start.19 = (bf16[320,1792]{1,0:T(8,128)(2,1)S(1)}, bf16[320,1792]{1,0:T(8,128)(2,1)S(1)}, u32[]{:S(2)}, u32[]{:S(2)}) collective-permute-start(bf16[320,1792]{1,0:T(8,128)(2,1)S(1)} %get-tuple-element.85), channel_id=1, source_target_pairs={{0,12},{4,0},{8,4},{12,8},{1,13},{5,1},{9,5},{13,9},{2,14},{6,2},{... | collective-permute-start | bytes 3440648 | tf_op jit(solution)/shard_map/ppermute | solution.py:371
  58.3 15.0 %collective-permute-start.15 = (bf16[1664,128]{1,0:T(8,128)(2,1)S(1)}, bf16[1664,128]{1,0:T(8,128)(2,1)S(1)}, u32[]{:S(2)}, u32[]{:S(2)}) collective-permute-start(bf16[1664,128]{1,0:T(8,128)(2,1)S(1)} %get-tuple-element.78), channel_id=1, source_target_pairs={{0,32},{16,48},{32,64},{48,80},{64,96},{80,112},{96,0},{112,16},{1... | collective-permute-start | bytes 1277960 | tf_op jit(solution)/shard_map/ppermute | solution.py:377
  59.6 13.7 %collective-permute-start.16 = (bf16[1664,128]{1,0:T(8,128)(2,1)S(1)}, bf16[1664,128]{1,0:T(8,128)(2,1)S(1)}, u32[]{:S(2)}, u32[]{:S(2)}) collective-permute-start(bf16[1664,128]{1,0:T(8,128)(2,1)S(1)} %get-tuple-element.79), channel_id=1, source_target_pairs={{0,96},{16,112},{32,0},{48,16},{64,32},{80,48},{96,64},{112,80},{1... | collective-permute-start | bytes 1277960 | tf_op jit(solution)/shard_map/ppermute | solution.py:377
  61.0 12.3 %collective-permute-start.17 = (bf16[256,128]{1,0:T(8,128)(2,1)S(1)}, bf16[256,128]{1,0:T(8,128)(2,1)S(1)}, u32[]{:S(2)}, u32[]{:S(2)}) collective-permute-start(bf16[256,128]{1,0:T(8,128)(2,1)S(1)} %get-tuple-element.81), channel_id=1, source_target_pairs={{0,64},{16,80},{32,96},{48,112},{64,0},{80,16},{96,32},{112,48},{1... | collective-permute-start | bytes 196616 | tf_op jit(solution)/shard_map/ppermute | solution.py:377
  70.5 51.8 %collective-permute-start.24 = (bf16[640,1792]{1,0:T(8,128)(2,1)S(1)}, bf16[640,1792]{1,0:T(8,128)(2,1)S(1)}, u32[]{:S(2)}, u32[]{:S(2)}) collective-permute-start(bf16[640,1792]{1,0:T(8,128)(2,1)S(1)} %get-tuple-element.96), channel_id=1, source_target_pairs={{0,4},{4,8},{8,12},{12,0},{1,5},{5,9},{9,13},{13,1},{2,6},{6,10},{... | collective-permute-start | bytes 6881288 | tf_op jit(solution)/shard_map/ppermute | solution.py:371
  71.0 51.4 %collective-permute-start.25 = (bf16[640,1792]{1,0:T(8,128)(2,1)S(1)}, bf16[640,1792]{1,0:T(8,128)(2,1)S(1)}, u32[]{:S(2)}, u32[]{:S(2)}) collective-permute-start(bf16[640,1792]{1,0:T(8,128)(2,1)S(1)} %get-tuple-element.97), channel_id=1, source_target_pairs={{0,12},{4,0},{8,4},{12,8},{1,13},{5,1},{9,5},{13,9},{2,14},{6,2},{... | collective-permute-start | bytes 6881288 | tf_op jit(solution)/shard_map/ppermute | solution.py:371
  86.1 11.4 %collective-permute-start.28 = (bf16[2432,128]{1,0:T(8,128)(2,1)S(1)}, bf16[2432,128]{1,0:T(8,128)(2,1)S(1)}, u32[]{:S(2)}, u32[]{:S(2)}) collective-permute-start(bf16[2432,128]{1,0:T(8,128)(2,1)S(1)} %get-tuple-element.98.refs_0_), channel_id=1, source_target_pairs={{0,96},{16,112},{32,0},{48,16},{64,32},{80,48},{96,64},{112,80},{1... | collective-permute-start | bytes 1867784 | tf_op jit(solution)/shard_map/ppermute | solution.py:377
  88.6 12.0 %collective-permute-start.26 = (bf16[2432,128]{1,0:T(8,128)(2,1)S(1)}, bf16[2432,128]{1,0:T(8,128)(2,1)S(1)}, u32[]{:S(2)}, u32[]{:S(2)}) collective-permute-start(bf16[2432,128]{1,0:T(8,128)(2,1)S(1)} %get-tuple-element.98.refs_0_), channel_id=1, source_target_pairs={{0,32},{16,48},{32,64},{48,80},{64,96},{80,112},{96,0},{112,16},{1... | collective-permute-start | bytes 1867784 | tf_op jit(solution)/shard_map/ppermute | solution.py:377
  101.9 20.5 %collective-permute-start.31 = (bf16[5632,128]{1,0:T(8,128)(2,1)S(1)}, bf16[5632,128]{1,0:T(8,128)(2,1)S(1)}, u32[]{:S(2)}, u32[]{:S(2)}) collective-permute-start(bf16[5632,128]{1,0:T(8,128)(2,1)S(1)} %get-tuple-element.100.refs_0_), channel_id=1, source_target_pairs={{0,16},{16,0},{32,48},{48,32},{64,80},{80,64},{96,112},{112,96},{1... | collective-permute-start | bytes 4325384 | tf_op jit(solution)/shard_map/ppermute | solution.py:381
  107.6 9.0 %collective-permute-start.29 = (bf16[1216,128]{1,0:T(8,128)(2,1)S(1)}, bf16[1216,128]{1,0:T(8,128)(2,1)S(1)}, u32[]{:S(2)}, u32[]{:S(2)}) collective-permute-start(bf16[1216,128]{1,0:T(8,128)(2,1)S(1)} %slice.9), channel_id=1, source_target_pairs={{0,96},{16,112},{32,0},{48,16},{64,32},{80,48},{96,64},{112,80},{1... | collective-permute-start | bytes 933896 | tf_op jit(solution)/shard_map/ppermute | solution.py:377
  107.8 10.0 %collective-permute-start.27 = (bf16[1216,128]{1,0:T(8,128)(2,1)S(1)}, bf16[1216,128]{1,0:T(8,128)(2,1)S(1)}, u32[]{:S(2)}, u32[]{:S(2)}) collective-permute-start(bf16[1216,128]{1,0:T(8,128)(2,1)S(1)} %slice.8), channel_id=1, source_target_pairs={{0,32},{16,48},{32,64},{48,80},{64,96},{80,112},{96,0},{112,16},{1... | collective-permute-start | bytes 933896 | tf_op jit(solution)/shard_map/ppermute | solution.py:377
  (15 other events, 183.2 us)
